TPU v7x, 256 devices: a whole 4x4x8 slice. The times are simulated.
256 devices in a mesh: row: 32 (over x, z), col: 8 (over y, core).
Axes of the slice: x: 4, y: 4, z: 8, core: 2. Of those that a mesh axis runs over, the one named last changes fastest.
Arguments:
- right_sides: bfloat16 [4, 256, 256, 256], P(None, ('row', 'col')), may hold values from -6 to 6
- lower_blocks: bfloat16 [32, 8, 3, 6, 256, 256], P('row', 'col'), may hold values from -0.1875 to 0.1875
- lower_source: int32 [32, 8, 3, 6], P('row', 'col'), may hold values from 0 to 31
- lower_target: int32 [32, 8, 3, 6], P('row', 'col'), may hold values from 8 to 32, as said below
- diag_lower_inv: bfloat16 [4, 256, 256, 256], P(None, ('row', 'col')), may hold values from -1 to 2, as said below
- upper_blocks: bfloat16 [32, 8, 3, 6, 256, 256], P('row', 'col'), may hold values from -0.1875 to 0.1875
- upper_source: int32 [32, 8, 3, 6], P('row', 'col'), may hold values from 0 to 31
- upper_target: int32 [32, 8, 3, 6], P('row', 'col'), may hold values from 0 to 32, as said below
- diag_upper_inv: bfloat16 [4, 256, 256, 256], P(None, ('row', 'col')), may hold values from -1 to 2, as said below
Outputs:
- solution: float32 [4, 256, 256, 256], P(None, ('row', 'col'))
Inputs may be any that keep to these rules, and one draw needn't show every extreme that they name: lower_target[r, c, a, k] is 32 for an empty slot, else b * 8 + q with a < b < 4 and 0 <= q < 8. upper_target[r, c, a, k] is 32 for an empty slot, else b * 8 + q with 0 <= b <= a and 0 <= q < 8. `diag_lower_inv`: each block is lower triangular with a positive diagonal. `diag_upper_inv`: each block is upper triangular with a positive diagonal.
All inputs are finite; a program needn't handle non-finite values.
Results may differ from a plain program's by a relative error of at most 0.029.
Values may be sent and summed in bfloat16 or wider, within the bound.
No kernel may reach another device: no remote copies, remote signals or barrier semaphores. Data moves between devices by JAX's collectives and lax.ppermute only.
A program may use at most 128 MiB of HBM per device.

v0:
```python
import functools

import jax
import jax.numpy as jnp
from jax import lax
from jax.experimental import pallas as pl
from jax.experimental.pallas import tpu as pltpu
from jax.sharding import PartitionSpec as P

X, Z, Y, C = 4, 8, 4, 2
LOCAL = Y * C
GROUP = 4
VMEM = pl.BlockSpec(memory_space=pltpu.VMEM)
SMEM = pl.BlockSpec(memory_space=pltpu.SMEM)
ANY = pl.BlockSpec(memory_space=pl.ANY)
PARAMS = pltpu.CompilerParams(vmem_limit_bytes=20 * 1024 * 1024)
NT = (((1,), (1,)), ((), ()))


def dot_nt(a, b):
    return lax.dot_general(a, b, NT, preferred_element_type=jnp.float32)


def along_x(value, d):
    return lax.ppermute(value, "row", [(x * Z + z, (x + d) % X * Z + z) for x in range(X) for z in range(Z)])


def along_z(value, d):
    return lax.ppermute(value, "row", [(x * Z + z, x * Z + (z + d) % Z) for x in range(X) for z in range(Z)])


def along_y(value, d):
    return lax.ppermute(value, "col", [(y * C + k, (y + d) % Y * C + k) for y in range(Y) for k in range(C)])


def other_core(value):
    return lax.ppermute(value, "col", [(y * C + k, y * C + 1 - k) for y in range(Y) for k in range(C)])


def gather_x(value):
    groups = [[x * Z + z for x in range(X)] for z in range(Z)]
    gathered = lax.all_gather(value, "row", axis=0, tiled=True, axis_index_groups=groups)
    return pltpu.with_memory_space_constraint(gathered, pltpu.HBM)


def ring_pieces(panel):
    up, down = [panel], [panel]
    for _ in range(Z // 2 - 1):
        up.append(along_z(up[-1], 1))
        down.append(along_z(down[-1], -1))
    up.append(along_z(up[-1], 1))
    return up + down[:0:-1]


def update_body(level, columns, slots, per_rows, keep, *refs):
    count = len(columns)
    place, table = refs[:2]
    pieces = refs[2 : 2 + Z]
    kept = refs[2 + Z : 1 + Z + count]
    blocks = refs[1 + Z + count : 1 + Z + 2 * count]
    rest = refs[1 + Z + 2 * count :]
    mine, other, rest = rest[0], rest[1], rest[2:]
    if keep:
        held, rest = rest[0], rest[1:]
    block_buf, piece_buf, acc, slot_at, slot_from, block_sem, piece_sem, keep_sem = rest
    x, y, core = place[0], place[2], place[3]
    spare = piece_buf.shape[0] - 1

    def scan(n, found):
        for d in range(X):
            first_block = ((x - d) & (X - 1)) * per_rows[n]

            def visit(k, at, d=d, first_block=first_block):
                entry = table[d, columns[n] + k]
                live = (entry >> 8) == level

                @pl.when(live)
                def _():
                    block = blocks[n].at[first_block + k]
                    pltpu.make_async_copy(block, block_buf.at[at], block_sem.at[at]).start()
                    slot_at[at] = ((entry >> 5) & (LOCAL - 1)) * X + d
                    piece = entry & (X * Z - 1)
                    if n < count - 1:
                        copy = pltpu.make_async_copy(
                            kept[n].at[piece], piece_buf.at[X * Z + at], piece_sem.at[at]
                        )
                        copy.start()
                        slot_from[at] = X * Z + at
                    else:
                        slot_from[at] = piece

                return at + live.astype(jnp.int32)

            for k in range(slots):
                found = visit(k, found)
        return found

    earlier = jnp.int32(0)
    for n in range(count - 1):
        earlier = scan(n, earlier)
    live = scan(count - 1, earlier)
    for d in range(Z):
        piece_buf[d * X : (d + 1) * X] = pieces[d][...]
    if keep:
        keep_copy = pltpu.make_async_copy(piece_buf.at[pl.ds(0, X * Z)], held, keep_sem)
        keep_copy.start()
    acc[...] = jnp.zeros_like(acc)
    piece_buf[spare] = jnp.zeros_like(piece_buf[spare])
    for i in range(GROUP - 1):
        slot_from[live + i] = spare
        slot_at[live + i] = 0

    def add_products(group, carry):
        products = []
        for i in range(GROUP):
            at = group * GROUP + i

            @pl.when(at < live)
            def _():
                pltpu.make_async_copy(blocks[0].at[0], block_buf.at[at], block_sem.at[at]).wait()

            if count > 1:

                @pl.when(at < earlier)
                def _():
                    pltpu.make_async_copy(kept[0].at[0], piece_buf.at[X * Z + at], piece_sem.at[at]).wait()

        for i in range(GROUP):
            at = group * GROUP + i
            block = block_buf[jnp.minimum(at, live - 1)]
            products.append((slot_at[at], dot_nt(piece_buf[slot_from[at]], block)))
        for to, product in products:
            acc[to] += product
        return carry

    lax.fori_loop(0, (live + (GROUP - 1)) // GROUP, add_products, 0)
    for d in range(Y):
        column = ((y + d) & (Y - 1)) * C
        mine[d] = acc[pl.ds((column + core) * X, X)].astype(mine.dtype)
        other[d] = acc[pl.ds((column + 1 - core) * X, X)].astype(other.dtype)
    if keep:
        keep_copy.wait()


def block_updates(place, table, level, columns, slots, pieces, kept, blocks, keep):
    panel = pieces[0].shape
    count = len(columns)
    half = jax.ShapeDtypeStruct((Y,) + panel, jnp.bfloat16)
    held = jax.ShapeDtypeStruct((X * Z,) + panel[1:], jnp.bfloat16)
    total = count * X * slots
    return pl.pallas_call(
        functools.partial(update_body, level, columns, slots, [b.shape[0] // X for b in blocks], keep),
        out_shape=(half, half) + (held,) * keep,
        in_specs=[SMEM] * 2 + [VMEM] * Z + [ANY] * (2 * count - 1),
        out_specs=(VMEM, VMEM) + (ANY,) * keep,
        scratch_shapes=[
            pltpu.VMEM((total,) + blocks[0].shape[1:], jnp.bfloat16),
            pltpu.VMEM((X * Z + total + 1,) + panel[1:], jnp.bfloat16),
            pltpu.VMEM((LOCAL * X,) + panel[1:], jnp.float32),
            pltpu.SMEM((total + GROUP,), jnp.int32),
            pltpu.SMEM((total + GROUP,), jnp.int32),
            pltpu.SemaphoreType.DMA((total,)),
            pltpu.SemaphoreType.DMA((total,)),
            pltpu.SemaphoreType.DMA,
        ],
        compiler_params=PARAMS,
        cost_estimate=pl.CostEstimate(flops=400_000_000, bytes_accessed=9_000_000, transcendentals=0),
    )(place, table, *pieces, *kept, *blocks)


def add_body(mine, theirs, *outs):
    for d in range(Y):
        outs[d][...] = (mine[d].astype(jnp.float32) + theirs[d].astype(jnp.float32)).astype(jnp.bfloat16)


def add_halves(mine, theirs):
    part = jax.ShapeDtypeStruct(mine.shape[1:], mine.dtype)
    return pl.pallas_call(
        add_body,
        out_shape=[part] * Y,
        in_specs=[VMEM] * 2,
        out_specs=[VMEM] * Y,
        compiler_params=PARAMS,
        cost_estimate=pl.CostEstimate(flops=300_000, bytes_accessed=1_500_000, transcendentals=0),
    )(mine, theirs)


def col_total(mine, other):
    sums = add_halves(mine, other_core(other))
    return [sums[0]] + [along_y(sums[d], d) for d in range(1, Y)]


def solve_body(per_row, slots, inverses, start, keep_result, *refs):
    place = refs[0]
    terms = refs[1 : 1 + Y]
    rights = refs[1 + Y : 1 + Y + X]
    blocks, first_out, panel_out, buffer, sem = refs[1 + Y + X :]
    x = place[0]

    def copy(i, d):
        at = ((x - d) & (X - 1)) * per_row + slots + i
        return pltpu.make_async_copy(blocks.at[at], buffer.at[i * X + d], sem.at[i * X + d])

    for i in range(inverses):
        for d in range(X):
            copy(i, d).start()
    for d in range(X):
        total = sum(term[d].astype(jnp.float32) for term in terms)
        right = rights[d][start : start + total.shape[0]].astype(jnp.float32)
        vector = (right - total).astype(jnp.bfloat16)
        copy(0, d).wait()
        result = dot_nt(vector, buffer[d])
        if inverses == 2:
            vector = result.astype(jnp.bfloat16)
            copy(1, d).wait()
            result = dot_nt(vector, buffer[X + d])
        first_out[d] = result if keep_result else vector
        panel_out[d] = result.astype(jnp.bfloat16)


def diag_solve(place, terms, rights, start, blocks, slots, inverses, keep_result):
    panel = terms[0].shape
    return pl.pallas_call(
        functools.partial(solve_body, blocks.shape[0] // X, slots, inverses, start, keep_result),
        out_shape=(
            jax.ShapeDtypeStruct(panel, jnp.float32 if keep_result else jnp.bfloat16),
            jax.ShapeDtypeStruct(panel, jnp.bfloat16),
        ),
        in_specs=[SMEM] + [VMEM] * (Y + X) + [ANY],
        out_specs=(VMEM, VMEM),
        scratch_shapes=[
            pltpu.VMEM((inverses * X,) + blocks.shape[1:], jnp.bfloat16),
            pltpu.SemaphoreType.DMA((inverses * X,)),
        ],
        compiler_params=PARAMS,
        cost_estimate=pl.CostEstimate(flops=33_000_000, bytes_accessed=1_800_000, transcendentals=0),
    )(place, *terms, *rights, blocks)


def begin_body(place, right, inverse, table, first, *rest):
    parts, whole = rest[:X], rest[X]
    levels = right.shape[0]
    rows = whole.shape[1] // X
    result = jnp.dot(inverse[...], right[0], preferred_element_type=jnp.float32).T
    first[...] = result
    whole[0] = result.astype(jnp.bfloat16)
    for level in range(1, levels):
        whole[level] = right[level].astype(jnp.float32).T.astype(jnp.bfloat16)
    for d in range(X):
        at = pl.ds(pl.multiple_of(((place[0] + d) & (X - 1)) * rows, rows), rows)
        for level in range(levels):
            parts[d][level * rows : (level + 1) * rows] = whole[level, at]
        parts[d][levels * rows :] = table[...]


def begin(place, right, inverse, table):
    levels, width, rhs_cols = right.shape
    part = jax.ShapeDtypeStruct((levels * rhs_cols // X + table.shape[0], width), jnp.bfloat16)
    return pl.pallas_call(
        begin_body,
        out_shape=[jax.ShapeDtypeStruct((rhs_cols, width), jnp.float32)] + [part] * X,
        in_specs=[SMEM] + [VMEM] * 3,
        out_specs=[VMEM] * (1 + X),
        scratch_shapes=[pltpu.VMEM((levels, rhs_cols, width), jnp.bfloat16)],
        compiler_params=PARAMS,
        cost_estimate=pl.CostEstimate(flops=33_000_000, bytes_accessed=1_800_000, transcendentals=0),
    )(place, right, inverse, table)


def return_body(*refs):
    terms, vectors, parts = refs[:Y], refs[Y:-X], refs[-X:]
    for d in range(X):
        parts[d][0] = sum(term[d].astype(jnp.float32) for term in terms).astype(jnp.bfloat16)
        for level, vector in enumerate(vectors):
            parts[d][level + 1] = vector[d]


def return_parts(terms, vectors):
    part = jax.ShapeDtypeStruct((1 + len(vectors),) + terms[0].shape[1:], jnp.bfloat16)
    return pl.pallas_call(
        return_body,
        out_shape=[part] * X,
        in_specs=[VMEM] * (Y + len(vectors)),
        out_specs=[VMEM] * X,
        compiler_params=PARAMS,
        cost_estimate=pl.CostEstimate(flops=300_000, bytes_accessed=1_500_000, transcendentals=0),
    )(*terms, *vectors)


def finish_body(place, *refs):
    parts = refs[:X]
    forward, inverse, out, right, result, sem = refs[X:]
    levels, rows = parts[0].shape[:2]
    for level in range(levels):
        for d in range(X):
            at = pl.ds(pl.multiple_of(((place[0] + d) & (X - 1)) * rows, rows), rows)
            vector = parts[d][level]
            if level == 0:
                vector = (forward[at, :] - vector.astype(jnp.float32)).astype(jnp.bfloat16)
            right[level, at, :] = vector
        result[level] = dot_nt(inverse[level], right[level])
        pltpu.make_async_copy(result.at[level], out.at[level], sem.at[level]).start()
    for level in range(levels):
        pltpu.make_async_copy(result.at[level], out.at[level], sem.at[level]).wait()


def finish(place, parts, forward, inverse):
    levels, rows, width = parts[0].shape
    return pl.pallas_call(
        finish_body,
        out_shape=jax.ShapeDtypeStruct((levels, width, rows * X), jnp.float32),
        in_specs=[SMEM] + [VMEM] * (X + 2),
        out_specs=ANY,
        scratch_shapes=[
            pltpu.VMEM((levels, rows * X, width), jnp.bfloat16),
            pltpu.VMEM((levels, width, rows * X), jnp.float32),
            pltpu.SemaphoreType.DMA((levels,)),
        ],
        compiler_params=PARAMS,
        cost_estimate=pl.CostEstimate(flops=130_000_000, bytes_accessed=2_000_000, transcendentals=0),
    )(place, *parts, forward, inverse)


def after(values, token):
    return lax.optimization_barrier((values, token))[0]


def shards(
    right_sides,
    lower_blocks,
    lower_source,
    lower_target,
    diag_lower_inv,
    upper_blocks,
    upper_source,
    upper_target,
    diag_upper_inv,
):
    levels = right_sides.shape[0]
    slots = lower_blocks.shape[3]
    rows, width = right_sides.shape[3] // X, right_sides.shape[2]
    top = levels - 1
    row, col = lax.axis_index("row"), lax.axis_index("col")
    place = jnp.stack([row // Z, row % Z, col // C, col % C]).astype(jnp.int32)

    def lower_group(level, token):
        held = [lower_blocks[0, 0, level], diag_lower_inv[level + 1]]
        if level + 1 == top:
            held.append(diag_upper_inv[top])
        if token is not None:
            held = after(held, token)
        return gather_x(jnp.concatenate(held))

    def upper_group(level, token):
        held = [upper_blocks[0, 0, level]]
        if level > 0:
            held.append(diag_upper_inv[level])
        return gather_x(jnp.concatenate(after(held, token)))

    lower = [lower_group(0, None)]
    upper = [None] * top

    table = jnp.stack([lower_source, lower_target, upper_source, upper_target]).reshape(1, -1)
    entries = table.shape[1]
    table = jnp.pad(table.astype(jnp.bfloat16), ((0, 15), (0, width - entries)))
    first, *parts = begin(place, right_sides[:, 0], diag_lower_inv[0, 0], table)
    parts = [parts[0]] + [along_x(parts[d], d) for d in range(1, X)]
    table = jnp.stack([part[levels * rows, :entries] for part in parts]).astype(jnp.int32)
    table = table.reshape(X, 2, 2, top * slots)
    source, target = table[:, :, 0], table[:, :, 1]
    table = target * (X * Z) + ((place[1] - source) & (Z - 1)) * X + ((place[0] - source // Z) & (X - 1))
    table = table.reshape(X, 2 * top * slots)
    panel = jnp.stack([part[:rows] for part in parts])
    lower.append(lower_group(1, parts[1]))

    def later_groups(step, token):
        if step + 2 < top:
            lower.append(lower_group(step + 2, token))
        elif step + 2 < 2 * top:
            level = 2 * top - step - 3
            upper[level] = upper_group(level, token)

    forward = [None] * levels
    kept = []
    for level in range(top):
        pieces = ring_pieces(panel)
        later_groups(level, pieces[1])
        columns = [n * slots for n in range(level + 1)]
        mine, other, *held = block_updates(
            place, table, level + 1, columns, slots, pieces, kept, lower[: level + 1], level + 1 < top
        )
        kept += held
        terms = col_total(mine, other)
        is_top = level + 1 == top
        forward[level + 1], panel = diag_solve(
            place, terms, parts, (level + 1) * rows, lower[level], slots, 2 if is_top else 1, not is_top
        )

    vectors = [None] * levels
    vectors[top] = forward[top]
    kept = []
    for level in range(top - 1, -1, -1):
        pieces = ring_pieces(panel)
        later_groups(2 * top - 1 - level, pieces[1])
        columns = [(top + n) * slots for n in range(top - 1, level - 1, -1)]
        held_blocks = [upper[n] for n in range(top - 1, level - 1, -1)]
        mine, other, *held = block_updates(
            place, table, level, columns, slots, pieces, kept, held_blocks, level > 0
        )
        kept += held
        terms = col_total(mine, other)
        if level > 0:
            rights = [forward[level][d] for d in range(X)]
            vectors[level], panel = diag_solve(place, terms, rights, 0, upper[level], slots, 1, False)

    back = return_parts(terms, vectors[1:])
    back = [back[0]] + [along_x(back[d], -d) for d in range(1, X)]
    return finish(place, back, first, diag_upper_inv[:, 0])[:, None]


def solution(mesh):
    by_block = P("row", "col", None, None, None, None)
    by_slot = P("row", "col", None, None)
    by_supernode = P(None, ("row", "col"), None, None)
    in_specs = (
        by_supernode,
        by_block,
        by_slot,
        by_slot,
        by_supernode,
        by_block,
        by_slot,
        by_slot,
        by_supernode,
    )
    return jax.shard_map(shards, mesh=mesh, in_specs=in_specs, out_specs=by_supernode, check_vma=False)
```

profile of v0, /device:TPU:8, one launch (start us, length us, event | category | flops | bytes accessed | tf_op | source)
XLA Modules:
  0.0 358.7 jit_solution(932568253504327237)
XLA Ops:
  14.2 5.1 %collective-permute-done.refs_6_ = bf16[272,256]{1,0:T(8,128)(2,1)S(1)} collective-permute-done((bf16[272,256]{1,0:T(8,128)(2,1)S(1)}, bf16[272,256]{1,0:T(8,128)(2,1)S(1)}, u32[]{:S(2)}, u32[]{:S(2)}) %collective-permute-start) | collective-permute-done | bytes 139296 | tf_op jit(solution)/shard_map/ppermute | solution.py:25
  24.4 3.6 %collective-permute-done.1.refs_7_ = bf16[272,256]{1,0:T(8,128)(2,1)S(1)} collective-permute-done((bf16[272,256]{1,0:T(8,128)(2,1)S(1)}, bf16[272,256]{1,0:T(8,128)(2,1)S(1)}, u32[]{:S(2)}, u32[]{:S(2)}) %collective-permute-start.1) | collective-permute-done | bytes 139296 | tf_op jit(solution)/shard_map/ppermute | solution.py:25
  32.1 9.5 %collective-permute-done.3.refs_3_ = bf16[4,64,256]{2,1,0:T(8,128)(2,1)S(1)} collective-permute-done((bf16[4,64,256]{2,1,0:T(8,128)(2,1)S(1)}, bf16[4,64,256]{2,1,0:T(8,128)(2,1)S(1)}, u32[]{:S(2)}, u32[]{:S(2)}) %collective-permute-start.3) | collective-permute-done | bytes 131104 | tf_op jit(solution)/shard_map/ppermute | solution.py:29
  43.8 2.4 collective-permute-start.7
  48.8 3.7 %collective-permute-start.8 = (bf16[4,64,256]{2,1,0:T(8,128)(2,1)S(1)}, bf16[4,64,256]{2,1,0:T(8,128)(2,1)S(1)}, u32[]{:S(2)}, u32[]{:S(2)}) collective-permute-start(bf16[4,64,256]{2,1,0:T(8,128)(2,1)S(1)} %collective-permute-done.7.refs_9_), channel_id=1, source_target_pairs={{0,56},{8,0},{16,8},{24,16},{32,24},{40,32},{48,40},{56,48},{64,12... | collective-permute-start | bytes 393224 | tf_op jit(solution)/shard_map/ppermute | solution.py:29
  52.7 2.2 collective-permute-done.8.refs_8_
  54.9 3.7 %collective-permute-start.9 = (bf16[4,64,256]{2,1,0:T(8,128)(2,1)S(1)}, bf16[4,64,256]{2,1,0:T(8,128)(2,1)S(1)}, u32[]{:S(2)}, u32[]{:S(2)}) collective-permute-start(bf16[4,64,256]{2,1,0:T(8,128)(2,1)S(1)} %collective-permute-done.8.refs_8_), channel_id=1, source_target_pairs={{0,56},{8,0},{16,8},{24,16},{32,24},{40,32},{48,40},{56,48},{64,12... | collective-permute-start | bytes 393224 | tf_op jit(solution)/shard_map/ppermute | solution.py:29
  58.7 2.4 collective-permute-done.9.refs_7_
  61.1 3.7 %collective-permute-done.6.refs_6_ = bf16[4,64,256]{2,1,0:T(8,128)(2,1)S(1)} collective-permute-done((bf16[4,64,256]{2,1,0:T(8,128)(2,1)S(1)}, bf16[4,64,256]{2,1,0:T(8,128)(2,1)S(1)}, u32[]{:S(2)}, u32[]{:S(2)}) %collective-permute-start.6) | collective-permute-done | bytes 131104 | tf_op jit(solution)/shard_map/ppermute | solution.py:29
  64.9 2.8 shard_map.92
  72.7 2.8 collective-permute-start.13
  75.5 4.2 %collective-permute-done.12.refs_3_ = bf16[4,64,256]{2,1,0:T(8,128)(2,1)S(1)} collective-permute-done((bf16[4,64,256]{2,1,0:T(8,128)(2,1)S(1)}, bf16[4,64,256]{2,1,0:T(8,128)(2,1)S(1)}, u32[]{:S(2)}, u32[]{:S(2)}) %collective-permute-start.12) | collective-permute-done | bytes 131104 | tf_op jit(solution)/shard_map/ppermute | solution.py:33
  81.1 2.3 shard_map.94
  85.4 5.0 %collective-permute-done.14.refs_3_ = bf16[4,64,256]{2,1,0:T(8,128)(2,1)S(1)} collective-permute-done((bf16[4,64,256]{2,1,0:T(8,128)(2,1)S(1)}, bf16[4,64,256]{2,1,0:T(8,128)(2,1)S(1)}, u32[]{:S(2)}, u32[]{:S(2)}) %collective-permute-start.14) | collective-permute-done | bytes 131104 | tf_op jit(solution)/shard_map/ppermute | solution.py:29
  93.7 2.9 collective-permute-done.18.refs_9_
  101.6 2.4 collective-permute-start.20
  105.3 4.7 %all-gather.9.cloned.1.call-done.refs_12_.refs_9_.refs_13_ = bf16[28,256,256]{2,1,0:T(8,128)(2,1)} async-done(((bf16[7,256,256]{2,1,0:T(8,128)(2,1)}), bf16[28,256,256]{2,1,0:T(8,128)(2,1)}) %all-gather.9.cloned.1.call-update) | async-done | bytes 3670032 | tf_op jit(solution)/shard_map/all_gather | solution.py:42
  118.7 3.8 %shard_map.95 = (bf16[4,4,64,256]{3,2,1,0:T(8,128)(2,1)S(1)}, bf16[4,4,64,256]{3,2,1,0:T(8,128)(2,1)S(1)}, bf16[32,64,256]{2,1,0:T(8,128)(2,1)S(1)}) custom-call(s32[4]{0:T(128)S(1)} %pad_add_fusion.place.refs_0_, s32[4,36]{1,0:T(4,128)S(1)} %fusion.4.refs_1_, bf16[4,64,256]{2,1,0:T(8,128)(2,1)S(1)} %copy-done.7, bf16[4,64,256]{2,1,0:T(8,128)(2,1)S(1)} %copy-done.11, ...), custom_call_target="tpu_custom_call" | custom-call | flops 400000000 | bytes 9000000 | tf_op jit(solution)/shard_map/pallas_call | solution.py:151
  127.3 2.5 collective-permute-start.24
  130.2 3.9 %collective-permute-done.23.refs_3_ = bf16[4,64,256]{2,1,0:T(8,128)(2,1)S(1)} collective-permute-done((bf16[4,64,256]{2,1,0:T(8,128)(2,1)S(1)}, bf16[4,64,256]{2,1,0:T(8,128)(2,1)S(1)}, u32[]{:S(2)}, u32[]{:S(2)}) %collective-permute-start.23) | collective-permute-done | bytes 131104 | tf_op jit(solution)/shard_map/ppermute | solution.py:33
  135.3 2.3 shard_map.97
  140.3 5.0 %collective-permute-done.25.refs_3_ = bf16[4,64,256]{2,1,0:T(8,128)(2,1)S(1)} collective-permute-done((bf16[4,64,256]{2,1,0:T(8,128)(2,1)S(1)}, bf16[4,64,256]{2,1,0:T(8,128)(2,1)S(1)}, u32[]{:S(2)}, u32[]{:S(2)}) %collective-permute-start.25) | collective-permute-done | bytes 131104 | tf_op jit(solution)/shard_map/ppermute | solution.py:29
  147.0 10.2 %collective-permute-start.29 = (bf16[4,64,256]{2,1,0:T(8,128)(2,1)}, bf16[4,64,256]{2,1,0:T(8,128)(2,1)S(1)}, u32[]{:S(2)}, u32[]{:S(2)}) collective-permute-start(bf16[4,64,256]{2,1,0:T(8,128)(2,1)} %copy-done.8), channel_id=1, source_target_pairs={{0,56},{8,0},{16,8},{24,16},{32,24},{40,32},{48,40},{56,48},{64,12... | collective-permute-start | bytes 393224 | tf_op jit(solution)/shard_map/ppermute | solution.py:29
  157.9 3.2 collective-permute-done.29.refs_9_
  161.1 2.5 collective-permute-start.30
  166.2 3.7 %collective-permute-start.31 = (bf16[4,64,256]{2,1,0:T(8,128)(2,1)}, bf16[4,64,256]{2,1,0:T(8,128)(2,1)}, u32[]{:S(2)}, u32[]{:S(2)}) collective-permute-start(bf16[4,64,256]{2,1,0:T(8,128)(2,1)} %collective-permute-done.30.refs_8_), channel_id=1, source_target_pairs={{0,56},{8,0},{16,8},{24,16},{32,24},{40,32},{48,40},{56,48},{64,12... | collective-permute-start | bytes 393224 | tf_op jit(solution)/shard_map/ppermute | solution.py:29
  170.6 2.2 collective-permute-done.31.refs_7_
  172.7 4.3 %collective-permute-done.28.refs_6_ = bf16[4,64,256]{2,1,0:T(8,128)(2,1)} collective-permute-done((bf16[4,64,256]{2,1,0:T(8,128)(2,1)}, bf16[4,64,256]{2,1,0:T(8,128)(2,1)}, u32[]{:S(2)}, u32[]{:S(2)}) %collective-permute-start.28) | collective-permute-done | bytes 131104 | tf_op jit(solution)/shard_map/ppermute | solution.py:29
  180.7 5.6 %shard_map.98 = (bf16[4,4,64,256]{3,2,1,0:T(8,128)(2,1)S(1)}, bf16[4,4,64,256]{3,2,1,0:T(8,128)(2,1)S(1)}) custom-call(s32[4]{0:T(128)S(1)} %pad_add_fusion.place.refs_0_, s32[4,36]{1,0:T(4,128)S(1)} %fusion.4.refs_1_, bf16[4,64,256]{2,1,0:T(8,128)(2,1)S(1)} %copy-done.9, bf16[4,64,256]{2,1,0:T(8,128)(2,1)S(1)} %copy-done.13, ...), custom_call_target="tpu_custom_call" | custom-call | flops 400000000 | bytes 9000000 | tf_op jit(solution)/shard_map/pallas_call | solution.py:151
  188.5 2.5 collective-permute-start.33
  193.6 3.2 collective-permute-done.33.refs_2_
  200.1 3.2 shard_map.100
  203.9 6.2 %collective-permute-done.36.refs_3_ = bf16[4,64,256]{2,1,0:T(8,128)(2,1)S(1)} collective-permute-done((bf16[4,64,256]{2,1,0:T(8,128)(2,1)S(1)}, bf16[4,64,256]{2,1,0:T(8,128)(2,1)S(1)}, u32[]{:S(2)}, u32[]{:S(2)}) %collective-permute-start.36) | collective-permute-done | bytes 131104 | tf_op jit(solution)/shard_map/ppermute | solution.py:29
  212.2 2.9 collective-permute-done.40.refs_9_
  217.6 3.5 collective-permute-done.41.refs_8_
  223.1 2.9 collective-permute-done.42.refs_7_
  226.1 3.2 collective-permute-done.39.refs_6_
  229.2 2.8 shard_map.101
  238.3 2.3 collective-permute-done.44.refs_2_
  240.6 2.6 collective-permute-done.45.refs_3_
  244.1 2.3 shard_map.103
  247.1 3.2 collective-permute-start.51
  250.3 2.9 collective-permute-done.47.refs_3_
  253.3 3.2 collective-permute-start.52
  256.5 2.9 collective-permute-done.48.refs_4_
  259.5 3.2 collective-permute-start.53
  262.7 2.9 collective-permute-done.49.refs_5_
  266.9 4.9 %collective-permute-done.50.refs_6_ = bf16[4,64,256]{2,1,0:T(8,128)(2,1)S(1)} collective-permute-done((bf16[4,64,256]{2,1,0:T(8,128)(2,1)S(1)}, bf16[4,64,256]{2,1,0:T(8,128)(2,1)S(1)}, u32[]{:S(2)}, u32[]{:S(2)}) %collective-permute-start.50) | collective-permute-done | bytes 131104 | tf_op jit(solution)/shard_map/ppermute | solution.py:29
  275.2 4.0 %shard_map.104 = (bf16[4,4,64,256]{3,2,1,0:T(8,128)(2,1)S(1)}, bf16[4,4,64,256]{3,2,1,0:T(8,128)(2,1)S(1)}, bf16[32,64,256]{2,1,0:T(8,128)(2,1)S(1)}) custom-call(s32[4]{0:T(128)S(1)} %pad_add_fusion.place.refs_0_, s32[4,36]{1,0:T(4,128)S(1)} %fusion.4.refs_1_, bf16[4,64,256]{2,1,0:T(8,128)(2,1)S(1)} %get-tuple-element.115.refs_2_, ...), custom_call_target="tpu_custom_call" | custom-call | flops 400000000 | bytes 9000000 | tf_op jit(solution)/shard_map/pallas_call | solution.py:151
  283.9 2.5 collective-permute-start.57
  287.3 3.6 %collective-permute-done.56.refs_3_ = bf16[4,64,256]{2,1,0:T(8,128)(2,1)S(1)} collective-permute-done((bf16[4,64,256]{2,1,0:T(8,128)(2,1)S(1)}, bf16[4,64,256]{2,1,0:T(8,128)(2,1)S(1)}, u32[]{:S(2)}, u32[]{:S(2)}) %collective-permute-start.56) | collective-permute-done | bytes 131104 | tf_op jit(solution)/shard_map/ppermute | solution.py:33
  292.0 2.3 shard_map.106
  295.0 3.2 collective-permute-start.62
  298.2 2.9 collective-permute-done.58.refs_3_
  301.1 3.2 collective-permute-start.63
  304.4 2.9 collective-permute-done.59.refs_4_
  307.3 3.2 collective-permute-start.64
  310.5 3.0 collective-permute-done.60.refs_5_
  313.6 6.5 %collective-permute-done.61.refs_6_ = bf16[4,64,256]{2,1,0:T(8,128)(2,1)} collective-permute-done((bf16[4,64,256]{2,1,0:T(8,128)(2,1)}, bf16[4,64,256]{2,1,0:T(8,128)(2,1)}, u32[]{:S(2)}, u32[]{:S(2)}) %collective-permute-start.61) | collective-permute-done | bytes 131104 | tf_op jit(solution)/shard_map/ppermute | solution.py:29
  320.1 5.6 %shard_map.107 = (bf16[4,4,64,256]{3,2,1,0:T(8,128)(2,1)S(1)}, bf16[4,4,64,256]{3,2,1,0:T(8,128)(2,1)S(1)}) custom-call(s32[4]{0:T(128)S(1)} %pad_add_fusion.place.refs_0_, s32[4,36]{1,0:T(4,128)S(1)} %fusion.4.refs_1_, bf16[4,64,256]{2,1,0:T(8,128)(2,1)S(1)} %get-tuple-element.126.refs_2_, bf16[4,64,256]{2,1,0:T(8,128)(2,1)S(1)} %collective-permute-done.58.refs_3_, ...), custom_call_target="tpu_custom_call" | custom-call | flops 400000000 | bytes 9000000 | tf_op jit(solution)/shard_map/pallas_call | solution.py:151
  329.2 2.2 collective-permute-start.67
  334.3 2.8 collective-permute-done.67.refs_2_
  340.0 3.0 collective-permute-start.70
  345.3 2.6 collective-permute-done.70.refs_2_
  (257 shorter events, 116.9 us)
Async XLA Ops:
  6.5 58.3 %all-gather.7.cloned.1.call-start = ((), (), s32[]{:S(2)}) async-start(), calls=%async_computation | async-start | bytes 4587520 | tf_op jit(solution)/shard_map/all_gather | solution.py:42
  11.3 98.8 %all-gather.9.cloned.1.call-start = ((), (), s32[]{:S(2)}) async-start(), calls=%async_computation.1 | async-start | bytes 4587520 | tf_op jit(solution)/shard_map/all_gather | solution.py:42
  12.6 6.7 %collective-permute-start = (bf16[272,256]{1,0:T(8,128)(2,1)S(1)}, bf16[272,256]{1,0:T(8,128)(2,1)S(1)}, u32[]{:S(2)}, u32[]{:S(2)}) collective-permute-start(bf16[272,256]{1,0:T(8,128)(2,1)S(1)} %get-tuple-element.75), channel_id=1, source_target_pairs={{0,64},{8,72},{16,80},{24,88},{32,96},{40,104},{48,112},{56,120},{... | collective-permute-start | bytes 417800 | tf_op jit(solution)/shard_map/ppermute | solution.py:25
  21.3 149.2 %all-gather.11.cloned.1.call-start = ((), (), s32[]{:S(2)}) async-start(), calls=%async_computation.2 | async-start | bytes 5242880 | tf_op jit(solution)/shard_map/all_gather | solution.py:42
  21.4 6.6 %collective-permute-start.1 = (bf16[272,256]{1,0:T(8,128)(2,1)S(1)}, bf16[272,256]{1,0:T(8,128)(2,1)S(1)}, u32[]{:S(2)}, u32[]{:S(2)}) collective-permute-start(bf16[272,256]{1,0:T(8,128)(2,1)S(1)} %get-tuple-element.76), channel_id=1, source_target_pairs={{0,128},{8,136},{16,144},{24,152},{32,160},{40,168},{48,176},{56,1... | collective-permute-start | bytes 417800 | tf_op jit(solution)/shard_map/ppermute | solution.py:25
  23.3 6.1 %collective-permute-start.2 = (bf16[272,256]{1,0:T(8,128)(2,1)S(1)}, bf16[272,256]{1,0:T(8,128)(2,1)S(1)}, u32[]{:S(2)}, u32[]{:S(2)}) collective-permute-start(bf16[272,256]{1,0:T(8,128)(2,1)S(1)} %get-tuple-element.77), channel_id=1, source_target_pairs={{0,192},{8,200},{16,208},{24,216},{32,224},{40,232},{48,240},{56,2... | collective-permute-start | bytes 417800 | tf_op jit(solution)/shard_map/ppermute | solution.py:25
  29.4 12.2 %collective-permute-start.3 = (bf16[4,64,256]{2,1,0:T(8,128)(2,1)S(1)}, bf16[4,64,256]{2,1,0:T(8,128)(2,1)S(1)}, u32[]{:S(2)}, u32[]{:S(2)}) collective-permute-start(bf16[4,64,256]{2,1,0:T(8,128)(2,1)S(1)} %pad_maximum_fusion.5.refs_2_), channel_id=1, source_target_pairs={{0,8},{8,16},{16,24},{24,32},{32,40},{40,48},{48,56},{56,0},{64,72... | collective-permute-start | bytes 393224 | tf_op jit(solution)/shard_map/ppermute | solution.py:29
  43.6 185.6 %all-gather.13.cloned.1.call-start = ((), (), s32[]{:S(2)}) async-start(), calls=%async_computation.3 | async-start | bytes 4587520 | tf_op jit(solution)/shard_map/all_gather | solution.py:42
  46.3 6.2 %collective-permute-start.4 = (bf16[4,64,256]{2,1,0:T(8,128)(2,1)S(1)}, bf16[4,64,256]{2,1,0:T(8,128)(2,1)S(1)}, u32[]{:S(2)}, u32[]{:S(2)}) collective-permute-start(bf16[4,64,256]{2,1,0:T(8,128)(2,1)S(1)} %collective-permute-done.3.refs_3_), channel_id=1, source_target_pairs={{0,8},{8,16},{16,24},{24,32},{32,40},{40,48},{48,56},{56,0},{64,72... | collective-permute-start | bytes 393224 | tf_op jit(solution)/shard_map/ppermute | solution.py:29
  48.8 6.2 %collective-permute-start.8 = (bf16[4,64,256]{2,1,0:T(8,128)(2,1)S(1)}, bf16[4,64,256]{2,1,0:T(8,128)(2,1)S(1)}, u32[]{:S(2)}, u32[]{:S(2)}) collective-permute-start(bf16[4,64,256]{2,1,0:T(8,128)(2,1)S(1)} %collective-permute-done.7.refs_9_), channel_id=1, source_target_pairs={{0,56},{8,0},{16,8},{24,16},{32,24},{40,32},{48,40},{56,48},{64,12... | collective-permute-start | bytes 393224 | tf_op jit(solution)/shard_map/ppermute | solution.py:29
  52.5 6.2 %collective-permute-start.5 = (bf16[4,64,256]{2,1,0:T(8,128)(2,1)S(1)}, bf16[4,64,256]{2,1,0:T(8,128)(2,1)S(1)}, u32[]{:S(2)}, u32[]{:S(2)}) collective-permute-start(bf16[4,64,256]{2,1,0:T(8,128)(2,1)S(1)} %collective-permute-done.4.refs_4_), channel_id=1, source_target_pairs={{0,8},{8,16},{16,24},{24,32},{32,40},{40,48},{48,56},{56,0},{64,72... | collective-permute-start | bytes 393224 | tf_op jit(solution)/shard_map/ppermute | solution.py:29
  54.9 6.2 %collective-permute-start.9 = (bf16[4,64,256]{2,1,0:T(8,128)(2,1)S(1)}, bf16[4,64,256]{2,1,0:T(8,128)(2,1)S(1)}, u32[]{:S(2)}, u32[]{:S(2)}) collective-permute-start(bf16[4,64,256]{2,1,0:T(8,128)(2,1)S(1)} %collective-permute-done.8.refs_8_), channel_id=1, source_target_pairs={{0,56},{8,0},{16,8},{24,16},{32,24},{40,32},{48,40},{56,48},{64,12... | collective-permute-start | bytes 393224 | tf_op jit(solution)/shard_map/ppermute | solution.py:29
  58.7 6.2 %collective-permute-start.6 = (bf16[4,64,256]{2,1,0:T(8,128)(2,1)S(1)}, bf16[4,64,256]{2,1,0:T(8,128)(2,1)S(1)}, u32[]{:S(2)}, u32[]{:S(2)}) collective-permute-start(bf16[4,64,256]{2,1,0:T(8,128)(2,1)S(1)} %collective-permute-done.5.refs_5_), channel_id=1, source_target_pairs={{0,8},{8,16},{16,24},{24,32},{32,40},{40,48},{48,56},{56,0},{64,72... | collective-permute-start | bytes 393224 | tf_op jit(solution)/shard_map/ppermute | solution.py:29
  71.8 7.9 %collective-permute-start.12 = (bf16[4,64,256]{2,1,0:T(8,128)(2,1)S(1)}, bf16[4,64,256]{2,1,0:T(8,128)(2,1)S(1)}, u32[]{:S(2)}, u32[]{:S(2)}) collective-permute-start(bf16[4,64,256]{2,1,0:T(8,128)(2,1)S(1)} %get-tuple-element.82), channel_id=1, source_target_pairs={{0,4},{1,5},{2,6},{3,7},{4,0},{5,1},{6,2},{7,3},{8,12},{9,13},{10,... | collective-permute-start | bytes 393224 | tf_op jit(solution)/shard_map/ppermute | solution.py:33
  72.7 8.3 %collective-permute-start.13 = (bf16[4,64,256]{2,1,0:T(8,128)(2,1)S(1)}, bf16[4,64,256]{2,1,0:T(8,128)(2,1)S(1)}, u32[]{:S(2)}, u32[]{:S(2)}) collective-permute-start(bf16[4,64,256]{2,1,0:T(8,128)(2,1)S(1)} %get-tuple-element.83), channel_id=1, source_target_pairs={{0,6},{1,7},{2,0},{3,1},{4,2},{5,3},{6,4},{7,5},{8,14},{9,15},{10,... | collective-permute-start | bytes 393224 | tf_op jit(solution)/shard_map/ppermute | solution.py:33
  84.1 6.4 %collective-permute-start.14 = (bf16[4,64,256]{2,1,0:T(8,128)(2,1)S(1)}, bf16[4,64,256]{2,1,0:T(8,128)(2,1)S(1)}, u32[]{:S(2)}, u32[]{:S(2)}) collective-permute-start(bf16[4,64,256]{2,1,0:T(8,128)(2,1)S(1)} %get-tuple-element.84.refs_2_), channel_id=1, source_target_pairs={{0,8},{8,16},{16,24},{24,32},{32,40},{40,48},{48,56},{56,0},{64,72... | collective-permute-start | bytes 393224 | tf_op jit(solution)/shard_map/ppermute | solution.py:29
  91.5 175.4 %all-gather.15.cloned.1.call-start = ((), (), s32[]{:S(2)}) async-start(), calls=%async_computation.4 | async-start | bytes 4587520 | tf_op jit(solution)/shard_map/all_gather | solution.py:42
  91.6 6.8 %collective-permute-start.15 = (bf16[4,64,256]{2,1,0:T(8,128)(2,1)S(1)}, bf16[4,64,256]{2,1,0:T(8,128)(2,1)S(1)}, u32[]{:S(2)}, u32[]{:S(2)}) collective-permute-start(bf16[4,64,256]{2,1,0:T(8,128)(2,1)S(1)} %collective-permute-done.14.refs_3_), channel_id=1, source_target_pairs={{0,8},{8,16},{16,24},{24,32},{32,40},{40,48},{48,56},{56,0},{64,72... | collective-permute-start | bytes 393224 | tf_op jit(solution)/shard_map/ppermute | solution.py:29
  98.5 6.2 %collective-permute-start.16 = (bf16[4,64,256]{2,1,0:T(8,128)(2,1)S(1)}, bf16[4,64,256]{2,1,0:T(8,128)(2,1)S(1)}, u32[]{:S(2)}, u32[]{:S(2)}) collective-permute-start(bf16[4,64,256]{2,1,0:T(8,128)(2,1)S(1)} %collective-permute-done.15.refs_4_), channel_id=1, source_target_pairs={{0,8},{8,16},{16,24},{24,32},{32,40},{40,48},{48,56},{56,0},{64,72... | collective-permute-start | bytes 393224 | tf_op jit(solution)/shard_map/ppermute | solution.py:29
  101.6 8.5 %collective-permute-start.20 = (bf16[4,64,256]{2,1,0:T(8,128)(2,1)S(1)}, bf16[4,64,256]{2,1,0:T(8,128)(2,1)S(1)}, u32[]{:S(2)}, u32[]{:S(2)}) collective-permute-start(bf16[4,64,256]{2,1,0:T(8,128)(2,1)S(1)} %collective-permute-done.19.refs_8_), channel_id=1, source_target_pairs={{0,56},{8,0},{16,8},{24,16},{32,24},{40,32},{48,40},{56,48},{64,12... | collective-permute-start | bytes 393224 | tf_op jit(solution)/shard_map/ppermute | solution.py:29
  104.6 6.2 %collective-permute-start.17 = (bf16[4,64,256]{2,1,0:T(8,128)(2,1)S(1)}, bf16[4,64,256]{2,1,0:T(8,128)(2,1)S(1)}, u32[]{:S(2)}, u32[]{:S(2)}) collective-permute-start(bf16[4,64,256]{2,1,0:T(8,128)(2,1)S(1)} %collective-permute-done.16.refs_5_), channel_id=1, source_target_pairs={{0,8},{8,16},{16,24},{24,32},{32,40},{40,48},{48,56},{56,0},{64,72... | collective-permute-start | bytes 393224 | tf_op jit(solution)/shard_map/ppermute | solution.py:29
  126.3 7.9 %collective-permute-start.23 = (bf16[4,64,256]{2,1,0:T(8,128)(2,1)S(1)}, bf16[4,64,256]{2,1,0:T(8,128)(2,1)S(1)}, u32[]{:S(2)}, u32[]{:S(2)}) collective-permute-start(bf16[4,64,256]{2,1,0:T(8,128)(2,1)S(1)} %get-tuple-element.92), channel_id=1, source_target_pairs={{0,4},{1,5},{2,6},{3,7},{4,0},{5,1},{6,2},{7,3},{8,12},{9,13},{10,... | collective-permute-start | bytes 393224 | tf_op jit(solution)/shard_map/ppermute | solution.py:33
  127.3 8.1 %collective-permute-start.24 = (bf16[4,64,256]{2,1,0:T(8,128)(2,1)S(1)}, bf16[4,64,256]{2,1,0:T(8,128)(2,1)S(1)}, u32[]{:S(2)}, u32[]{:S(2)}) collective-permute-start(bf16[4,64,256]{2,1,0:T(8,128)(2,1)S(1)} %get-tuple-element.93), channel_id=1, source_target_pairs={{0,6},{1,7},{2,0},{3,1},{4,2},{5,3},{6,4},{7,5},{8,14},{9,15},{10,... | collective-permute-start | bytes 393224 | tf_op jit(solution)/shard_map/ppermute | solution.py:33
  139.0 6.2 %collective-permute-start.25 = (bf16[4,64,256]{2,1,0:T(8,128)(2,1)S(1)}, bf16[4,64,256]{2,1,0:T(8,128)(2,1)S(1)}, u32[]{:S(2)}, u32[]{:S(2)}) collective-permute-start(bf16[4,64,256]{2,1,0:T(8,128)(2,1)S(1)} %get-tuple-element.94.refs_2_), channel_id=1, source_target_pairs={{0,8},{8,16},{16,24},{24,32},{32,40},{40,48},{48,56},{56,0},{64,72... | collective-permute-start | bytes 393224 | tf_op jit(solution)/shard_map/ppermute | solution.py:29
  146.9 166.6 %all-gather.17.cloned.1.call-start = ((), (), s32[]{:S(2)}) async-start(), calls=%async_computation.5 | async-start | bytes 3932160 | tf_op jit(solution)/shard_map/all_gather | solution.py:42
  147.0 14.1 %collective-permute-start.29 = (bf16[4,64,256]{2,1,0:T(8,128)(2,1)}, bf16[4,64,256]{2,1,0:T(8,128)(2,1)S(1)}, u32[]{:S(2)}, u32[]{:S(2)}) collective-permute-start(bf16[4,64,256]{2,1,0:T(8,128)(2,1)} %copy-done.8), channel_id=1, source_target_pairs={{0,56},{8,0},{16,8},{24,16},{32,24},{40,32},{48,40},{56,48},{64,12... | collective-permute-start | bytes 393224 | tf_op jit(solution)/shard_map/ppermute | solution.py:29
  157.2 7.0 %collective-permute-start.26 = (bf16[4,64,256]{2,1,0:T(8,128)(2,1)}, bf16[4,64,256]{2,1,0:T(8,128)(2,1)S(1)}, u32[]{:S(2)}, u32[]{:S(2)}) collective-permute-start(bf16[4,64,256]{2,1,0:T(8,128)(2,1)} %copy-done.12), channel_id=1, source_target_pairs={{0,8},{8,16},{16,24},{24,32},{32,40},{40,48},{48,56},{56,0},{64,72... | collective-permute-start | bytes 393224 | tf_op jit(solution)/shard_map/ppermute | solution.py:29
  164.3 6.3 %collective-permute-start.27 = (bf16[4,64,256]{2,1,0:T(8,128)(2,1)S(1)}, bf16[4,64,256]{2,1,0:T(8,128)(2,1)}, u32[]{:S(2)}, u32[]{:S(2)}) collective-permute-start(bf16[4,64,256]{2,1,0:T(8,128)(2,1)S(1)} %collective-permute-done.26.refs_4_), channel_id=1, source_target_pairs={{0,8},{8,16},{16,24},{24,32},{32,40},{40,48},{48,56},{56,0},{64,72... | collective-permute-start | bytes 393224 | tf_op jit(solution)/shard_map/ppermute | solution.py:29
  166.2 6.6 %collective-permute-start.31 = (bf16[4,64,256]{2,1,0:T(8,128)(2,1)}, bf16[4,64,256]{2,1,0:T(8,128)(2,1)}, u32[]{:S(2)}, u32[]{:S(2)}) collective-permute-start(bf16[4,64,256]{2,1,0:T(8,128)(2,1)} %collective-permute-done.30.refs_8_), channel_id=1, source_target_pairs={{0,56},{8,0},{16,8},{24,16},{32,24},{40,32},{48,40},{56,48},{64,12... | collective-permute-start | bytes 393224 | tf_op jit(solution)/shard_map/ppermute | solution.py:29
  170.6 6.5 %collective-permute-start.28 = (bf16[4,64,256]{2,1,0:T(8,128)(2,1)}, bf16[4,64,256]{2,1,0:T(8,128)(2,1)}, u32[]{:S(2)}, u32[]{:S(2)}) collective-permute-start(bf16[4,64,256]{2,1,0:T(8,128)(2,1)} %collective-permute-done.27.refs_5_), channel_id=1, source_target_pairs={{0,8},{8,16},{16,24},{24,32},{32,40},{40,48},{48,56},{56,0},{64,72... | collective-permute-start | bytes 393224 | tf_op jit(solution)/shard_map/ppermute | solution.py:29
  188.5 8.3 %collective-permute-start.33 = (bf16[4,64,256]{2,1,0:T(8,128)(2,1)S(1)}, bf16[4,64,256]{2,1,0:T(8,128)(2,1)S(1)}, u32[]{:S(2)}, u32[]{:S(2)}) collective-permute-start(bf16[4,64,256]{2,1,0:T(8,128)(2,1)S(1)} %get-tuple-element.102), channel_id=1, source_target_pairs={{0,2},{1,3},{2,4},{3,5},{4,6},{5,7},{6,0},{7,1},{8,10},{9,11},{10,... | collective-permute-start | bytes 393224 | tf_op jit(solution)/shard_map/ppermute | solution.py:33
  191.0 7.9 %collective-permute-start.34 = (bf16[4,64,256]{2,1,0:T(8,128)(2,1)S(1)}, bf16[4,64,256]{2,1,0:T(8,128)(2,1)S(1)}, u32[]{:S(2)}, u32[]{:S(2)}) collective-permute-start(bf16[4,64,256]{2,1,0:T(8,128)(2,1)S(1)} %get-tuple-element.103), channel_id=1, source_target_pairs={{0,4},{1,5},{2,6},{3,7},{4,0},{5,1},{6,2},{7,3},{8,12},{9,13},{10,... | collective-permute-start | bytes 393224 | tf_op jit(solution)/shard_map/ppermute | solution.py:33
  192.3 7.8 %collective-permute-start.35 = (bf16[4,64,256]{2,1,0:T(8,128)(2,1)S(1)}, bf16[4,64,256]{2,1,0:T(8,128)(2,1)S(1)}, u32[]{:S(2)}, u32[]{:S(2)}) collective-permute-start(bf16[4,64,256]{2,1,0:T(8,128)(2,1)S(1)} %get-tuple-element.104), channel_id=1, source_target_pairs={{0,6},{1,7},{2,0},{3,1},{4,2},{5,3},{6,4},{7,5},{8,14},{9,15},{10,... | collective-permute-start | bytes 393224 | tf_op jit(solution)/shard_map/ppermute | solution.py:33
  203.9 6.2 %collective-permute-start.36 = (bf16[4,64,256]{2,1,0:T(8,128)(2,1)S(1)}, bf16[4,64,256]{2,1,0:T(8,128)(2,1)S(1)}, u32[]{:S(2)}, u32[]{:S(2)}) collective-permute-start(bf16[4,64,256]{2,1,0:T(8,128)(2,1)S(1)} %get-tuple-element.105.refs_2_), channel_id=1, source_target_pairs={{0,8},{8,16},{16,24},{24,32},{32,40},{40,48},{48,56},{56,0},{64,72... | collective-permute-start | bytes 393224 | tf_op jit(solution)/shard_map/ppermute | solution.py:29
  210.2 6.3 %collective-permute-start.37 = (bf16[4,64,256]{2,1,0:T(8,128)(2,1)S(1)}, bf16[4,64,256]{2,1,0:T(8,128)(2,1)S(1)}, u32[]{:S(2)}, u32[]{:S(2)}) collective-permute-start(bf16[4,64,256]{2,1,0:T(8,128)(2,1)S(1)} %collective-permute-done.36.refs_3_), channel_id=1, source_target_pairs={{0,8},{8,16},{16,24},{24,32},{32,40},{40,48},{48,56},{56,0},{64,72... | collective-permute-start | bytes 393224 | tf_op jit(solution)/shard_map/ppermute | solution.py:29
  215.2 5.9 %collective-permute-start.41 = (bf16[4,64,256]{2,1,0:T(8,128)(2,1)S(1)}, bf16[4,64,256]{2,1,0:T(8,128)(2,1)S(1)}, u32[]{:S(2)}, u32[]{:S(2)}) collective-permute-start(bf16[4,64,256]{2,1,0:T(8,128)(2,1)S(1)} %collective-permute-done.40.refs_9_), channel_id=1, source_target_pairs={{0,56},{8,0},{16,8},{24,16},{32,24},{40,32},{48,40},{56,48},{64,12... | collective-permute-start | bytes 393224 | tf_op jit(solution)/shard_map/ppermute | solution.py:29
  216.5 6.6 %collective-permute-start.38 = (bf16[4,64,256]{2,1,0:T(8,128)(2,1)S(1)}, bf16[4,64,256]{2,1,0:T(8,128)(2,1)S(1)}, u32[]{:S(2)}, u32[]{:S(2)}) collective-permute-start(bf16[4,64,256]{2,1,0:T(8,128)(2,1)S(1)} %collective-permute-done.37.refs_4_), channel_id=1, source_target_pairs={{0,8},{8,16},{16,24},{24,32},{32,40},{40,48},{48,56},{56,0},{64,72... | collective-permute-start | bytes 393224 | tf_op jit(solution)/shard_map/ppermute | solution.py:29
  223.0 6.2 %collective-permute-start.39 = (bf16[4,64,256]{2,1,0:T(8,128)(2,1)S(1)}, bf16[4,64,256]{2,1,0:T(8,128)(2,1)S(1)}, u32[]{:S(2)}, u32[]{:S(2)}) collective-permute-start(bf16[4,64,256]{2,1,0:T(8,128)(2,1)S(1)} %collective-permute-done.38.refs_5_), channel_id=1, source_target_pairs={{0,8},{8,16},{16,24},{24,32},{32,40},{40,48},{48,56},{56,0},{64,72... | collective-permute-start | bytes 393224 | tf_op jit(solution)/shard_map/ppermute | solution.py:29
  234.2 6.4 %collective-permute-start.44 = (bf16[4,64,256]{2,1,0:T(8,128)(2,1)S(1)}, bf16[4,64,256]{2,1,0:T(8,128)(2,1)S(1)}, u32[]{:S(2)}, u32[]{:S(2)}) collective-permute-start(bf16[4,64,256]{2,1,0:T(8,128)(2,1)S(1)} %get-tuple-element.111), channel_id=1, source_target_pairs={{0,2},{1,3},{2,4},{3,5},{4,6},{5,7},{6,0},{7,1},{8,10},{9,11},{10,... | collective-permute-start | bytes 393224 | tf_op jit(solution)/shard_map/ppermute | solution.py:33
  235.3 7.9 %collective-permute-start.45 = (bf16[4,64,256]{2,1,0:T(8,128)(2,1)S(1)}, bf16[4,64,256]{2,1,0:T(8,128)(2,1)S(1)}, u32[]{:S(2)}, u32[]{:S(2)}) collective-permute-start(bf16[4,64,256]{2,1,0:T(8,128)(2,1)S(1)} %get-tuple-element.112), channel_id=1, source_target_pairs={{0,4},{1,5},{2,6},{3,7},{4,0},{5,1},{6,2},{7,3},{8,12},{9,13},{10,... | collective-permute-start | bytes 393224 | tf_op jit(solution)/shard_map/ppermute | solution.py:33
  236.3 7.8 %collective-permute-start.46 = (bf16[4,64,256]{2,1,0:T(8,128)(2,1)S(1)}, bf16[4,64,256]{2,1,0:T(8,128)(2,1)S(1)}, u32[]{:S(2)}, u32[]{:S(2)}) collective-permute-start(bf16[4,64,256]{2,1,0:T(8,128)(2,1)S(1)} %get-tuple-element.113), channel_id=1, source_target_pairs={{0,6},{1,7},{2,0},{3,1},{4,2},{5,3},{6,4},{7,5},{8,14},{9,15},{10,... | collective-permute-start | bytes 393224 | tf_op jit(solution)/shard_map/ppermute | solution.py:33
  247.1 6.2 %collective-permute-start.47 = (bf16[4,64,256]{2,1,0:T(8,128)(2,1)S(1)}, bf16[4,64,256]{2,1,0:T(8,128)(2,1)S(1)}, u32[]{:S(2)}, u32[]{:S(2)}) collective-permute-start(bf16[4,64,256]{2,1,0:T(8,128)(2,1)S(1)} %get-tuple-element.115.refs_2_), channel_id=1, source_target_pairs={{0,8},{8,16},{16,24},{24,32},{32,40},{40,48},{48,56},{56,0},{64,72... | collective-permute-start | bytes 393224 | tf_op jit(solution)/shard_map/ppermute | solution.py:29
  247.1 6.2 %collective-permute-start.51 = (bf16[4,64,256]{2,1,0:T(8,128)(2,1)S(1)}, bf16[4,64,256]{2,1,0:T(8,128)(2,1)S(1)}, u32[]{:S(2)}, u32[]{:S(2)}) collective-permute-start(bf16[4,64,256]{2,1,0:T(8,128)(2,1)S(1)} %get-tuple-element.115.refs_2_), channel_id=1, source_target_pairs={{0,56},{8,0},{16,8},{24,16},{32,24},{40,32},{48,40},{56,48},{64,12... | collective-permute-start | bytes 393224 | tf_op jit(solution)/shard_map/ppermute | solution.py:29
  253.3 6.2 %collective-permute-start.48 = (bf16[4,64,256]{2,1,0:T(8,128)(2,1)S(1)}, bf16[4,64,256]{2,1,0:T(8,128)(2,1)S(1)}, u32[]{:S(2)}, u32[]{:S(2)}) collective-permute-start(bf16[4,64,256]{2,1,0:T(8,128)(2,1)S(1)} %collective-permute-done.47.refs_3_), channel_id=1, source_target_pairs={{0,8},{8,16},{16,24},{24,32},{32,40},{40,48},{48,56},{56,0},{64,72... | collective-permute-start | bytes 393224 | tf_op jit(solution)/shard_map/ppermute | solution.py:29
  253.3 6.2 %collective-permute-start.52 = (bf16[4,64,256]{2,1,0:T(8,128)(2,1)S(1)}, bf16[4,64,256]{2,1,0:T(8,128)(2,1)S(1)}, u32[]{:S(2)}, u32[]{:S(2)}) collective-permute-start(bf16[4,64,256]{2,1,0:T(8,128)(2,1)S(1)} %collective-permute-done.51.refs_9_), channel_id=1, source_target_pairs={{0,56},{8,0},{16,8},{24,16},{32,24},{40,32},{48,40},{56,48},{64,12... | collective-permute-start | bytes 393224 | tf_op jit(solution)/shard_map/ppermute | solution.py:29
  259.4 6.2 %collective-permute-start.49 = (bf16[4,64,256]{2,1,0:T(8,128)(2,1)S(1)}, bf16[4,64,256]{2,1,0:T(8,128)(2,1)S(1)}, u32[]{:S(2)}, u32[]{:S(2)}) collective-permute-start(bf16[4,64,256]{2,1,0:T(8,128)(2,1)S(1)} %collective-permute-done.48.refs_4_), channel_id=1, source_target_pairs={{0,8},{8,16},{16,24},{24,32},{32,40},{40,48},{48,56},{56,0},{64,72... | collective-permute-start | bytes 393224 | tf_op jit(solution)/shard_map/ppermute | solution.py:29
  259.5 6.8 %collective-permute-start.53 = (bf16[4,64,256]{2,1,0:T(8,128)(2,1)S(1)}, bf16[4,64,256]{2,1,0:T(8,128)(2,1)S(1)}, u32[]{:S(2)}, u32[]{:S(2)}) collective-permute-start(bf16[4,64,256]{2,1,0:T(8,128)(2,1)S(1)} %collective-permute-done.52.refs_8_), channel_id=1, source_target_pairs={{0,56},{8,0},{16,8},{24,16},{32,24},{40,32},{48,40},{56,48},{64,12... | collective-permute-start | bytes 393224 | tf_op jit(solution)/shard_map/ppermute | solution.py:29
  265.6 6.2 %collective-permute-start.50 = (bf16[4,64,256]{2,1,0:T(8,128)(2,1)S(1)}, bf16[4,64,256]{2,1,0:T(8,128)(2,1)S(1)}, u32[]{:S(2)}, u32[]{:S(2)}) collective-permute-start(bf16[4,64,256]{2,1,0:T(8,128)(2,1)S(1)} %collective-permute-done.49.refs_5_), channel_id=1, source_target_pairs={{0,8},{8,16},{16,24},{24,32},{32,40},{40,48},{48,56},{56,0},{64,72... | collective-permute-start | bytes 393224 | tf_op jit(solution)/shard_map/ppermute | solution.py:29
  281.5 5.8 %collective-permute-start.55 = (bf16[4,64,256]{2,1,0:T(8,128)(2,1)S(1)}, bf16[4,64,256]{2,1,0:T(8,128)(2,1)S(1)}, u32[]{:S(2)}, u32[]{:S(2)}) collective-permute-start(bf16[4,64,256]{2,1,0:T(8,128)(2,1)S(1)} %get-tuple-element.122), channel_id=1, source_target_pairs={{0,2},{1,3},{2,4},{3,5},{4,6},{5,7},{6,0},{7,1},{8,10},{9,11},{10,... | collective-permute-start | bytes 393224 | tf_op jit(solution)/shard_map/ppermute | solution.py:33
  283.0 7.9 %collective-permute-start.56 = (bf16[4,64,256]{2,1,0:T(8,128)(2,1)S(1)}, bf16[4,64,256]{2,1,0:T(8,128)(2,1)S(1)}, u32[]{:S(2)}, u32[]{:S(2)}) collective-permute-start(bf16[4,64,256]{2,1,0:T(8,128)(2,1)S(1)} %get-tuple-element.123), channel_id=1, source_target_pairs={{0,4},{1,5},{2,6},{3,7},{4,0},{5,1},{6,2},{7,3},{8,12},{9,13},{10,... | collective-permute-start | bytes 393224 | tf_op jit(solution)/shard_map/ppermute | solution.py:33
  283.9 8.1 %collective-permute-start.57 = (bf16[4,64,256]{2,1,0:T(8,128)(2,1)S(1)}, bf16[4,64,256]{2,1,0:T(8,128)(2,1)S(1)}, u32[]{:S(2)}, u32[]{:S(2)}) collective-permute-start(bf16[4,64,256]{2,1,0:T(8,128)(2,1)S(1)} %get-tuple-element.124), channel_id=1, source_target_pairs={{0,6},{1,7},{2,0},{3,1},{4,2},{5,3},{6,4},{7,5},{8,14},{9,15},{10,... | collective-permute-start | bytes 393224 | tf_op jit(solution)/shard_map/ppermute | solution.py:33
  294.9 6.2 %collective-permute-start.58 = (bf16[4,64,256]{2,1,0:T(8,128)(2,1)S(1)}, bf16[4,64,256]{2,1,0:T(8,128)(2,1)S(1)}, u32[]{:S(2)}, u32[]{:S(2)}) collective-permute-start(bf16[4,64,256]{2,1,0:T(8,128)(2,1)S(1)} %get-tuple-element.126.refs_2_), channel_id=1, source_target_pairs={{0,8},{8,16},{16,24},{24,32},{32,40},{40,48},{48,56},{56,0},{64,72... | collective-permute-start | bytes 393224 | tf_op jit(solution)/shard_map/ppermute | solution.py:29
  295.0 6.2 %collective-permute-start.62 = (bf16[4,64,256]{2,1,0:T(8,128)(2,1)S(1)}, bf16[4,64,256]{2,1,0:T(8,128)(2,1)S(1)}, u32[]{:S(2)}, u32[]{:S(2)}) collective-permute-start(bf16[4,64,256]{2,1,0:T(8,128)(2,1)S(1)} %get-tuple-element.126.refs_2_), channel_id=1, source_target_pairs={{0,56},{8,0},{16,8},{24,16},{32,24},{40,32},{48,40},{56,48},{64,12... | collective-permute-start | bytes 393224 | tf_op jit(solution)/shard_map/ppermute | solution.py:29
  301.1 6.2 %collective-permute-start.59 = (bf16[4,64,256]{2,1,0:T(8,128)(2,1)S(1)}, bf16[4,64,256]{2,1,0:T(8,128)(2,1)S(1)}, u32[]{:S(2)}, u32[]{:S(2)}) collective-permute-start(bf16[4,64,256]{2,1,0:T(8,128)(2,1)S(1)} %collective-permute-done.58.refs_3_), channel_id=1, source_target_pairs={{0,8},{8,16},{16,24},{24,32},{32,40},{40,48},{48,56},{56,0},{64,72... | collective-permute-start | bytes 393224 | tf_op jit(solution)/shard_map/ppermute | solution.py:29
  301.1 6.2 %collective-permute-start.63 = (bf16[4,64,256]{2,1,0:T(8,128)(2,1)S(1)}, bf16[4,64,256]{2,1,0:T(8,128)(2,1)S(1)}, u32[]{:S(2)}, u32[]{:S(2)}) collective-permute-start(bf16[4,64,256]{2,1,0:T(8,128)(2,1)S(1)} %collective-permute-done.62.refs_9_), channel_id=1, source_target_pairs={{0,56},{8,0},{16,8},{24,16},{32,24},{40,32},{48,40},{56,48},{64,12... | collective-permute-start | bytes 393224 | tf_op jit(solution)/shard_map/ppermute | solution.py:29
  307.3 6.3 %collective-permute-start.60 = (bf16[4,64,256]{2,1,0:T(8,128)(2,1)S(1)}, bf16[4,64,256]{2,1,0:T(8,128)(2,1)}, u32[]{:S(2)}, u32[]{:S(2)}) collective-permute-start(bf16[4,64,256]{2,1,0:T(8,128)(2,1)S(1)} %collective-permute-done.59.refs_4_), channel_id=1, source_target_pairs={{0,8},{8,16},{16,24},{24,32},{32,40},{40,48},{48,56},{56,0},{64,72... | collective-permute-start | bytes 393224 | tf_op jit(solution)/shard_map/ppermute | solution.py:29
  307.3 6.3 %collective-permute-start.64 = (bf16[4,64,256]{2,1,0:T(8,128)(2,1)S(1)}, bf16[4,64,256]{2,1,0:T(8,128)(2,1)}, u32[]{:S(2)}, u32[]{:S(2)}) collective-permute-start(bf16[4,64,256]{2,1,0:T(8,128)(2,1)S(1)} %collective-permute-done.63.refs_8_), channel_id=1, source_target_pairs={{0,56},{8,0},{16,8},{24,16},{32,24},{40,32},{48,40},{56,48},{64,12... | collective-permute-start | bytes 393224 | tf_op jit(solution)/shard_map/ppermute | solution.py:29
  313.6 6.5 %collective-permute-start.61 = (bf16[4,64,256]{2,1,0:T(8,128)(2,1)}, bf16[4,64,256]{2,1,0:T(8,128)(2,1)}, u32[]{:S(2)}, u32[]{:S(2)}) collective-permute-start(bf16[4,64,256]{2,1,0:T(8,128)(2,1)} %collective-permute-done.60.refs_5_), channel_id=1, source_target_pairs={{0,8},{8,16},{16,24},{24,32},{32,40},{40,48},{48,56},{56,0},{64,72... | collective-permute-start | bytes 393224 | tf_op jit(solution)/shard_map/ppermute | solution.py:29
  327.9 6.4 %collective-permute-start.66 = (bf16[4,64,256]{2,1,0:T(8,128)(2,1)S(1)}, bf16[4,64,256]{2,1,0:T(8,128)(2,1)S(1)}, u32[]{:S(2)}, u32[]{:S(2)}) collective-permute-start(bf16[4,64,256]{2,1,0:T(8,128)(2,1)S(1)} %get-tuple-element.132), channel_id=1, source_target_pairs={{0,2},{1,3},{2,4},{3,5},{4,6},{5,7},{6,0},{7,1},{8,10},{9,11},{10,... | collective-permute-start | bytes 393224 | tf_op jit(solution)/shard_map/ppermute | solution.py:33
  329.2 7.9 %collective-permute-start.67 = (bf16[4,64,256]{2,1,0:T(8,128)(2,1)S(1)}, bf16[4,64,256]{2,1,0:T(8,128)(2,1)S(1)}, u32[]{:S(2)}, u32[]{:S(2)}) collective-permute-start(bf16[4,64,256]{2,1,0:T(8,128)(2,1)S(1)} %get-tuple-element.133), channel_id=1, source_target_pairs={{0,4},{1,5},{2,6},{3,7},{4,0},{5,1},{6,2},{7,3},{8,12},{9,13},{10,... | collective-permute-start | bytes 393224 | tf_op jit(solution)/shard_map/ppermute | solution.py:33
  331.4 7.3 %collective-permute-start.68 = (bf16[4,64,256]{2,1,0:T(8,128)(2,1)S(1)}, bf16[4,64,256]{2,1,0:T(8,128)(2,1)S(1)}, u32[]{:S(2)}, u32[]{:S(2)}) collective-permute-start(bf16[4,64,256]{2,1,0:T(8,128)(2,1)S(1)} %get-tuple-element.134), channel_id=1, source_target_pairs={{0,6},{1,7},{2,0},{3,1},{4,2},{5,3},{6,4},{7,5},{8,14},{9,15},{10,... | collective-permute-start | bytes 393224 | tf_op jit(solution)/shard_map/ppermute | solution.py:33
  338.9 6.4 %collective-permute-start.69 = (bf16[4,64,256]{2,1,0:T(8,128)(2,1)S(1)}, bf16[4,64,256]{2,1,0:T(8,128)(2,1)S(1)}, u32[]{:S(2)}, u32[]{:S(2)}) collective-permute-start(bf16[4,64,256]{2,1,0:T(8,128)(2,1)S(1)} %get-tuple-element.139), channel_id=1, source_target_pairs={{0,192},{8,200},{16,208},{24,216},{32,224},{40,232},{48,240},{56,2... | collective-permute-start | bytes 393224 | tf_op jit(solution)/shard_map/ppermute | solution.py:25
  340.0 7.8 %collective-permute-start.70 = (bf16[4,64,256]{2,1,0:T(8,128)(2,1)S(1)}, bf16[4,64,256]{2,1,0:T(8,128)(2,1)S(1)}, u32[]{:S(2)}, u32[]{:S(2)}) collective-permute-start(bf16[4,64,256]{2,1,0:T(8,128)(2,1)S(1)} %get-tuple-element.140), channel_id=1, source_target_pairs={{0,128},{8,136},{16,144},{24,152},{32,160},{40,168},{48,176},{56,1... | collective-permute-start | bytes 393224 | tf_op jit(solution)/shard_map/ppermute | solution.py:25
  343.0 6.9 %collective-permute-start.71 = (bf16[4,64,256]{2,1,0:T(8,128)(2,1)S(1)}, bf16[4,64,256]{2,1,0:T(8,128)(2,1)S(1)}, u32[]{:S(2)}, u32[]{:S(2)}) collective-permute-start(bf16[4,64,256]{2,1,0:T(8,128)(2,1)S(1)} %get-tuple-element.141), channel_id=1, source_target_pairs={{0,64},{8,72},{16,80},{24,88},{32,96},{40,104},{48,112},{56,120},{... | collective-permute-start | bytes 393224 | tf_op jit(solution)/shard_map/ppermute | solution.py:25
  (64 other events, 317.7 us)
Sparse Core Ops, SparseCore 0:
  11.4 49.3 all-gather.6
  62.6 47.4 all-gather.8
  111.9 51.0 all-gather.10
  164.6 46.8 all-gather.12
  213.2 46.7 all-gather.14
  261.6 42.3 all-gather.16
where the time goes:
time: 363 us; the launch traced here: 359 us
  waiting for transfers between devices  163 us (45%)
  starting transfers between devices  102 us (28%)
  Pallas kernels  40.6 us (11%)
  local copies, waits for them, and re-layouts  32 us (9%)
  between operations  14.3 us (4%)
  other arithmetic  7.23 us (2%)
    ppermute x42, waiting for transfers between devices, along_z(): lax.ppermute(value, 'row', [(x * Z + z, x * Z + (z + d) % Z) for x in ran...  94.8 us
    ppermute x42, starting transfers between devices, along_z(): lax.ppermute(value, 'row', [(x * Z + z, x * Z + (z + d) % Z) for x in ran...  62.3 us
    ppermute x18, waiting for transfers between devices, along_y(): lax.ppermute(value, 'col', [(y * C + k, (y + d) % Y * C + k) for y in ran...  35.5 us
    ppermute x18, starting transfers between devices, along_y(): lax.ppermute(value, 'col', [(y * C + k, (y + d) % Y * C + k) for y in ran...  29.3 us
    unnamed x102, local copies, waits for them, and re-layouts  25.5 us
    pallas_call x6, Pallas kernels, block_updates(): pl.pallas_call(functools.partial(update_body, level, columns, slots, [b.s...  24.6 us
    ppermute x6, waiting for transfers between devices, along_x(): lax.ppermute(value, 'row', [(x * Z + z, (x + d) % X * Z + z) for x in ran...  16.4 us
    pallas_call x5, Pallas kernels, diag_solve(): pl.pallas_call(functools.partial(solve_body, blocks.shape[0] // X, slots,...  12.4 us
  transfers between devices with their start and end apart: 78, of which 62 were waited for; matrix products, arithmetic and copies ran while one was open for 3% of the time, Pallas kernels for 9%

commit v1 on v0

--- a/solution.py
+++ b/solution.py
@@ -13,8 +13,11 @@
 VMEM = pl.BlockSpec(memory_space=pltpu.VMEM)
 SMEM = pl.BlockSpec(memory_space=pltpu.SMEM)
 ANY = pl.BlockSpec(memory_space=pl.ANY)
-PARAMS = pltpu.CompilerParams(vmem_limit_bytes=20 * 1024 * 1024)
 NT = (((1,), (1,)), ((), ()))
+
+
+def params(mebibytes):
+    return pltpu.CompilerParams(vmem_limit_bytes=mebibytes * 1024 * 1024)
 
 
 def dot_nt(a, b):
@@ -35,12 +38,37 @@
 
 def other_core(value):
     return lax.ppermute(value, "col", [(y * C + k, y * C + 1 - k) for y in range(Y) for k in range(C)])
+
+
+def exchange_x(value):
+    cut = (value.shape[0] + 1) // 2
+    last, following = along_x(value, 1), along_x(value, -1)
+    far = along_x(last[:cut], 1), along_x(following[cut:], -1)
+    return [hbm(held) for held in (value, last, *far, following)], (last, following)
+
+
+def block_at(blocks, x, d, k):
+    if len(blocks) == 1:
+        return blocks[0].at[((x - d) & (X - 1)) * (blocks[0].shape[0] // X) + k]
+    value, last, far_low, far_high, following = blocks
+    cut = far_low.shape[0]
+    if d == 2:
+        return far_low.at[k] if k < cut else far_high.at[k - cut]
+    return (value, last, None, following)[d].at[k]
+
+
+def hbm(value):
+    return pltpu.with_memory_space_constraint(value, pltpu.HBM)
 
 
 def gather_x(value):
     groups = [[x * Z + z for x in range(X)] for z in range(Z)]
     gathered = lax.all_gather(value, "row", axis=0, tiled=True, axis_index_groups=groups)
-    return pltpu.with_memory_space_constraint(gathered, pltpu.HBM)
+    return [hbm(gathered)]
+
+
+def after(values, token):
+    return lax.optimization_barrier((values, token))[0]
 
 
 def ring_pieces(panel):
@@ -52,31 +80,33 @@
     return up + down[:0:-1]
 
 
-def update_body(level, columns, slots, per_rows, keep, *refs):
+def update_body(level, columns, slots, sizes, keep, *refs):
     count = len(columns)
     place, table = refs[:2]
     pieces = refs[2 : 2 + Z]
     kept = refs[2 + Z : 1 + Z + count]
-    blocks = refs[1 + Z + count : 1 + Z + 2 * count]
-    rest = refs[1 + Z + 2 * count :]
+    rest = refs[1 + Z + count :]
+    blocks = []
+    for size in sizes:
+        blocks.append(rest[:size])
+        rest = rest[size:]
     mine, other, rest = rest[0], rest[1], rest[2:]
     if keep:
         held, rest = rest[0], rest[1:]
-    block_buf, piece_buf, acc, slot_at, slot_from, block_sem, piece_sem, keep_sem = rest
+    block_buf, piece_buf, acc, slot_at, slot_from, block_sem, piece_sem, panel_sem, keep_sem = rest
     x, y, core = place[0], place[2], place[3]
     spare = piece_buf.shape[0] - 1
 
     def scan(n, found):
         for d in range(X):
-            first_block = ((x - d) & (X - 1)) * per_rows[n]
-
-            def visit(k, at, d=d, first_block=first_block):
+
+            def visit(k, at, d=d):
                 entry = table[d, columns[n] + k]
                 live = (entry >> 8) == level
 
                 @pl.when(live)
                 def _():
-                    block = blocks[n].at[first_block + k]
+                    block = block_at(blocks[n], x, d, k)
                     pltpu.make_async_copy(block, block_buf.at[at], block_sem.at[at]).start()
                     slot_at[at] = ((entry >> 5) & (LOCAL - 1)) * X + d
                     piece = entry & (X * Z - 1)
@@ -95,17 +125,22 @@
                 found = visit(k, found)
         return found
 
+    def panel_copy(d):
+        return pltpu.make_async_copy(pieces[d], piece_buf.at[pl.ds(d * X, X)], panel_sem.at[d])
+
+    for d in range(Z):
+        panel_copy(d).start()
     earlier = jnp.int32(0)
     for n in range(count - 1):
         earlier = scan(n, earlier)
     live = scan(count - 1, earlier)
+    acc[...] = jnp.zeros_like(acc)
+    piece_buf[spare] = jnp.zeros_like(piece_buf[spare])
     for d in range(Z):
-        piece_buf[d * X : (d + 1) * X] = pieces[d][...]
+        panel_copy(d).wait()
     if keep:
         keep_copy = pltpu.make_async_copy(piece_buf.at[pl.ds(0, X * Z)], held, keep_sem)
         keep_copy.start()
-    acc[...] = jnp.zeros_like(acc)
-    piece_buf[spare] = jnp.zeros_like(piece_buf[spare])
     for i in range(GROUP - 1):
         slot_from[live + i] = spare
         slot_at[live + i] = 0
@@ -117,7 +152,7 @@
 
             @pl.when(at < live)
             def _():
-                pltpu.make_async_copy(blocks[0].at[0], block_buf.at[at], block_sem.at[at]).wait()
+                pltpu.make_async_copy(blocks[0][0].at[0], block_buf.at[at], block_sem.at[at]).wait()
 
             if count > 1:
 
@@ -149,23 +184,55 @@
     held = jax.ShapeDtypeStruct((X * Z,) + panel[1:], jnp.bfloat16)
     total = count * X * slots
     return pl.pallas_call(
-        functools.partial(update_body, level, columns, slots, [b.shape[0] // X for b in blocks], keep),
+        functools.partial(update_body, level, columns, slots, [len(b) for b in blocks], keep),
         out_shape=(half, half) + (held,) * keep,
-        in_specs=[SMEM] * 2 + [VMEM] * Z + [ANY] * (2 * count - 1),
+        in_specs=[SMEM] * 2 + [ANY] * (Z + count - 1 + sum(len(b) for b in blocks)),
         out_specs=(VMEM, VMEM) + (ANY,) * keep,
         scratch_shapes=[
-            pltpu.VMEM((total,) + blocks[0].shape[1:], jnp.bfloat16),
+            pltpu.VMEM((total,) + blocks[0][0].shape[1:], jnp.bfloat16),
             pltpu.VMEM((X * Z + total + 1,) + panel[1:], jnp.bfloat16),
             pltpu.VMEM((LOCAL * X,) + panel[1:], jnp.float32),
             pltpu.SMEM((total + GROUP,), jnp.int32),
             pltpu.SMEM((total + GROUP,), jnp.int32),
             pltpu.SemaphoreType.DMA((total,)),
             pltpu.SemaphoreType.DMA((total,)),
+            pltpu.SemaphoreType.DMA((Z,)),
             pltpu.SemaphoreType.DMA,
         ],
-        compiler_params=PARAMS,
+        compiler_params=params(6 + 5 * count),
         cost_estimate=pl.CostEstimate(flops=400_000_000, bytes_accessed=9_000_000, transcendentals=0),
-    )(place, table, *pieces, *kept, *blocks)
+    )(place, table, *map(hbm, pieces), *map(hbm, kept), *sum(blocks, []))
+
+
+def pack_body(plan, *refs):
+    lower, upper, diag_lower, diag_upper = refs[:4]
+    groups, sem = refs[4:-1], refs[-1]
+    copies = []
+    for group, parts in zip(groups, plan):
+        at = 0
+        for kind, level in parts:
+            source = (lower.at[0, 0, level], upper.at[0, 0, level], diag_lower.at[level], diag_upper.at[level])[kind]
+            size = source.shape[0]
+            copies.append(pltpu.make_async_copy(source, group.at[pl.ds(at, size)], sem.at[len(copies)]))
+            at += size
+    for copy in copies:
+        copy.start()
+    for copy in copies:
+        copy.wait()
+
+
+def pack(plan, lower, upper, diag_lower, diag_upper):
+    sizes = [sum(lower.shape[3] if kind < 2 else 1 for kind, _ in parts) for parts in plan]
+    groups = pl.pallas_call(
+        functools.partial(pack_body, plan),
+        out_shape=[jax.ShapeDtypeStruct((size,) + lower.shape[4:], lower.dtype) for size in sizes],
+        in_specs=[ANY] * 4,
+        out_specs=[ANY] * len(plan),
+        scratch_shapes=[pltpu.SemaphoreType.DMA((sum(map(len, plan)),))],
+        compiler_params=params(4),
+        cost_estimate=pl.CostEstimate(flops=0, bytes_accessed=sum(sizes) * 262_144, transcendentals=0),
+    )(hbm(lower), hbm(upper), hbm(diag_lower), hbm(diag_upper))
+    return list(groups)
 
 
 def add_body(mine, theirs, *outs):
@@ -180,7 +247,7 @@
         out_shape=[part] * Y,
         in_specs=[VMEM] * 2,
         out_specs=[VMEM] * Y,
-        compiler_params=PARAMS,
+        compiler_params=params(8),
         cost_estimate=pl.CostEstimate(flops=300_000, bytes_accessed=1_500_000, transcendentals=0),
     )(mine, theirs)
 
@@ -190,16 +257,16 @@
     return [sums[0]] + [along_y(sums[d], d) for d in range(1, Y)]
 
 
-def solve_body(per_row, slots, inverses, start, keep_result, *refs):
+def solve_body(at, inverses, start, keep_result, *refs):
     place = refs[0]
     terms = refs[1 : 1 + Y]
     rights = refs[1 + Y : 1 + Y + X]
-    blocks, first_out, panel_out, buffer, sem = refs[1 + Y + X :]
+    blocks = refs[1 + Y + X : -4]
+    first_out, panel_out, buffer, sem = refs[-4:]
     x = place[0]
 
     def copy(i, d):
-        at = ((x - d) & (X - 1)) * per_row + slots + i
-        return pltpu.make_async_copy(blocks.at[at], buffer.at[i * X + d], sem.at[i * X + d])
+        return pltpu.make_async_copy(block_at(blocks, x, d, at + i), buffer.at[i * X + d], sem.at[i * X + d])
 
     for i in range(inverses):
         for d in range(X):
@@ -218,23 +285,23 @@
         panel_out[d] = result.astype(jnp.bfloat16)
 
 
-def diag_solve(place, terms, rights, start, blocks, slots, inverses, keep_result):
+def diag_solve(place, terms, rights, start, blocks, at, inverses, keep_result):
     panel = terms[0].shape
     return pl.pallas_call(
-        functools.partial(solve_body, blocks.shape[0] // X, slots, inverses, start, keep_result),
+        functools.partial(solve_body, at, inverses, start, keep_result),
         out_shape=(
             jax.ShapeDtypeStruct(panel, jnp.float32 if keep_result else jnp.bfloat16),
             jax.ShapeDtypeStruct(panel, jnp.bfloat16),
         ),
-        in_specs=[SMEM] + [VMEM] * (Y + X) + [ANY],
+        in_specs=[SMEM] + [VMEM] * (Y + X) + [ANY] * len(blocks),
         out_specs=(VMEM, VMEM),
         scratch_shapes=[
-            pltpu.VMEM((inverses * X,) + blocks.shape[1:], jnp.bfloat16),
+            pltpu.VMEM((inverses * X,) + blocks[0].shape[1:], jnp.bfloat16),
             pltpu.SemaphoreType.DMA((inverses * X,)),
         ],
-        compiler_params=PARAMS,
+        compiler_params=params(8),
         cost_estimate=pl.CostEstimate(flops=33_000_000, bytes_accessed=1_800_000, transcendentals=0),
-    )(place, *terms, *rights, blocks)
+    )(place, *terms, *rights, *blocks)
 
 
 def begin_body(place, right, inverse, table, first, *rest):
@@ -262,7 +329,7 @@
         in_specs=[SMEM] + [VMEM] * 3,
         out_specs=[VMEM] * (1 + X),
         scratch_shapes=[pltpu.VMEM((levels, rhs_cols, width), jnp.bfloat16)],
-        compiler_params=PARAMS,
+        compiler_params=params(8),
         cost_estimate=pl.CostEstimate(flops=33_000_000, bytes_accessed=1_800_000, transcendentals=0),
     )(place, right, inverse, table)
 
@@ -282,7 +349,7 @@
         out_shape=[part] * X,
         in_specs=[VMEM] * (Y + len(vectors)),
         out_specs=[VMEM] * X,
-        compiler_params=PARAMS,
+        compiler_params=params(8),
         cost_estimate=pl.CostEstimate(flops=300_000, bytes_accessed=1_500_000, transcendentals=0),
     )(*terms, *vectors)
 
@@ -316,13 +383,9 @@
             pltpu.VMEM((levels, width, rows * X), jnp.float32),
             pltpu.SemaphoreType.DMA((levels,)),
         ],
-        compiler_params=PARAMS,
+        compiler_params=params(8),
         cost_estimate=pl.CostEstimate(flops=130_000_000, bytes_accessed=2_000_000, transcendentals=0),
     )(place, *parts, forward, inverse)
-
-
-def after(values, token):
-    return lax.optimization_barrier((values, token))[0]
 
 
 def shards(
@@ -343,22 +406,17 @@
     row, col = lax.axis_index("row"), lax.axis_index("col")
     place = jnp.stack([row // Z, row % Z, col // C, col % C]).astype(jnp.int32)
 
-    def lower_group(level, token):
-        held = [lower_blocks[0, 0, level], diag_lower_inv[level + 1]]
-        if level + 1 == top:
-            held.append(diag_upper_inv[top])
-        if token is not None:
-            held = after(held, token)
-        return gather_x(jnp.concatenate(held))
-
-    def upper_group(level, token):
-        held = [upper_blocks[0, 0, level]]
-        if level > 0:
-            held.append(diag_upper_inv[level])
-        return gather_x(jnp.concatenate(after(held, token)))
-
-    lower = [lower_group(0, None)]
-    upper = [None] * top
+    factors = (lower_blocks, upper_blocks, diag_lower_inv, diag_upper_inv)
+    plan = [[(0, level), (2, level + 1)] for level in range(top)]
+    plan[-1].append((3, top))
+    plan += [[(1, level), (3, level)] if level else [(1, level)] for level in range(top - 1, -1, -1)]
+    first_group, near = exchange_x(pack(plan[:1], *factors)[0])
+    held = [
+        [factors[kind][0, 0, level] if kind < 2 else factors[kind][level] for kind, level in parts]
+        for parts in plan[1:]
+    ]
+    packed = [jnp.concatenate(parts) for parts in held]
+    groups = [first_group]
 
     table = jnp.stack([lower_source, lower_target, upper_source, upper_target]).reshape(1, -1)
     entries = table.shape[1]
@@ -370,30 +428,28 @@
     source, target = table[:, :, 0], table[:, :, 1]
     table = target * (X * Z) + ((place[1] - source) & (Z - 1)) * X + ((place[0] - source // Z) & (X - 1))
     table = table.reshape(X, 2 * top * slots)
-    panel = jnp.stack([part[:rows] for part in parts])
-    lower.append(lower_group(1, parts[1]))
-
-    def later_groups(step, token):
-        if step + 2 < top:
-            lower.append(lower_group(step + 2, token))
-        elif step + 2 < 2 * top:
-            level = 2 * top - step - 3
-            upper[level] = upper_group(level, token)
-
+    panel = after(jnp.stack([part[:rows] for part in parts]), (near, packed))
+
+    def next_group(token):
+        if packed:
+            groups.append(gather_x(after(packed.pop(0), token)))
+
+    next_group(panel)
     forward = [None] * levels
     kept = []
     for level in range(top):
         pieces = ring_pieces(panel)
-        later_groups(level, pieces[1])
+        if level > 0:
+            next_group(pieces[1])
         columns = [n * slots for n in range(level + 1)]
         mine, other, *held = block_updates(
-            place, table, level + 1, columns, slots, pieces, kept, lower[: level + 1], level + 1 < top
+            place, table, level + 1, columns, slots, pieces, kept, groups[: level + 1], level + 1 < top
         )
         kept += held
         terms = col_total(mine, other)
         is_top = level + 1 == top
         forward[level + 1], panel = diag_solve(
-            place, terms, parts, (level + 1) * rows, lower[level], slots, 2 if is_top else 1, not is_top
+            place, terms, parts, (level + 1) * rows, groups[level], slots, 2 if is_top else 1, not is_top
         )
 
     vectors = [None] * levels
@@ -401,9 +457,9 @@
     kept = []
     for level in range(top - 1, -1, -1):
         pieces = ring_pieces(panel)
-        later_groups(2 * top - 1 - level, pieces[1])
+        next_group(pieces[1])
         columns = [(top + n) * slots for n in range(top - 1, level - 1, -1)]
-        held_blocks = [upper[n] for n in range(top - 1, level - 1, -1)]
+        held_blocks = groups[top : 2 * top - level]
         mine, other, *held = block_updates(
             place, table, level, columns, slots, pieces, kept, held_blocks, level > 0
         )
@@ -411,7 +467,7 @@
         terms = col_total(mine, other)
         if level > 0:
             rights = [forward[level][d] for d in range(X)]
-            vectors[level], panel = diag_solve(place, terms, rights, 0, upper[level], slots, 1, False)
+            vectors[level], panel = diag_solve(place, terms, rights, 0, groups[2 * top - 1 - level], slots, 1, False)
 
     back = return_parts(terms, vectors[1:])
     back = [back[0]] + [along_x(back[d], -d) for d in range(1, X)]

time: 363 us -> 353 us (0.972)
  local copies, waits for them, and re-layouts: 32 us -> 15.4 us
  starting transfers between devices: 102 us -> 107 us
    unnamed x102 -> x122, local copies, waits for them, and re-layouts: 25.5 us -> 8.47 us
    ppermute x42, starting transfers between devices: 62.3 us -> 48.3 us  [along_z(): lax.ppermute(value, 'row', [(x * Z + z, x * Z + (z + d) % Z) for x in ran...]
    ppermute x18, starting transfers between devices: 29.3 us -> 42.5 us  [along_y(): lax.ppermute(value, 'col', [(y * C + k, (y + d) % Y * C + k) for y in ran...]
    ppermute x18, waiting for transfers between devices: 35.5 us -> 26.1 us  [along_y(): lax.ppermute(value, 'col', [(y * C + k, (y + d) % Y * C + k) for y in ran...]
    ppermute x42, waiting for transfers between devices: 94.8 us -> 102 us  [along_z(): lax.ppermute(value, 'row', [(x * Z + z, x * Z + (z + d) % Z) for x in ran...]
    ppermute x6 -> x10, starting transfers between devices: 9.25 us -> 16 us  [along_x(): lax.ppermute(value, 'row', [(x * Z + z, (x + d) % X * Z + z) for x in ran...]
    all_gather x6 -> x5, waiting for transfers between devices: 4.74 us -> 0.01 us  [gather_x(): lax.all_gather(value, 'row', axis=0, tiled=True, axis_index_groups=groups)]
    ppermute x6 -> x10, waiting for transfers between devices: 16.4 us -> 21.1 us  [along_x(): lax.ppermute(value, 'row', [(x * Z + z, (x + d) % X * Z + z) for x in ran...]
  transfers between devices with their start and end apart: 78 -> 81, of which waited for: 62 -> 60; matrix products, arithmetic and copies ran while one was open for 3% -> 3% of each run, Pallas kernels for 9% -> 10%
where the time goes in v1:
time: 353 us; the launch traced here: 347 us
  waiting for transfers between devices  161 us (46%)
  starting transfers between devices  107 us (30%)
  Pallas kernels  44.1 us (12%)
  local copies, waits for them, and re-layouts  15.4 us (4%)
  between operations  14.3 us (4%)
  other arithmetic  4.88 us (1%)
    ppermute x42, waiting for transfers between devices, along_z(): lax.ppermute(value, 'row', [(x * Z + z, x * Z + (z + d) % Z) for x in ran...  102 us
    ppermute x42, starting transfers between devices, along_z(): lax.ppermute(value, 'row', [(x * Z + z, x * Z + (z + d) % Z) for x in ran...  48.3 us
    ppermute x18, starting transfers between devices, along_y(): lax.ppermute(value, 'col', [(y * C + k, (y + d) % Y * C + k) for y in ran...  42.5 us
    pallas_call x6, Pallas kernels, block_updates(): pl.pallas_call(functools.partial(update_body, level, columns, slots, [len...  26.8 us
    ppermute x18, waiting for transfers between devices, along_y(): lax.ppermute(value, 'col', [(y * C + k, (y + d) % Y * C + k) for y in ran...  26.1 us
    ppermute x10, waiting for transfers between devices, along_x(): lax.ppermute(value, 'row', [(x * Z + z, (x + d) % X * Z + z) for x in ran...  21.1 us
    ppermute x10, starting transfers between devices, along_x(): lax.ppermute(value, 'row', [(x * Z + z, (x + d) % X * Z + z) for x in ran...  16 us
    pallas_call x5, Pallas kernels, diag_solve(): pl.pallas_call(functools.partial(solve_body, at, inverses, start, keep_re...  12.4 us
  transfers between devices with their start and end apart: 81, of which 60 were waited for; matrix products, arithmetic and copies ran while one was open for 3% of the time, Pallas kernels for 10%

profile of v1, /device:TPU:8, one launch (start us, length us, event | category | flops | bytes accessed | tf_op | source)
XLA Modules:
  0.0 347.1 jit_solution(15947739748995200174)
XLA Ops:
  16.5 2.4 slice_bitcast_fusion.3
  24.6 11.9 %collective-permute-done.2.refs_8_ = bf16[272,256]{1,0:T(8,128)(2,1)S(1)} collective-permute-done((bf16[272,256]{1,0:T(8,128)(2,1)S(1)}, bf16[272,256]{1,0:T(8,128)(2,1)S(1)}, u32[]{:S(2)}, u32[]{:S(2)}) %collective-permute-start.2) | collective-permute-done | bytes 139296 | tf_op jit(solution)/shard_map/ppermute | solution.py:28
  39.5 4.0 %collective-permute-start.9 = (bf16[4,64,256]{2,1,0:T(8,128)(2,1)S(1)}, bf16[4,64,256]{2,1,0:T(8,128)(2,1)}, u32[]{:S(2)}, u32[]{:S(2)}) collective-permute-start(bf16[4,64,256]{2,1,0:T(8,128)(2,1)S(1)} %pad_maximum_fusion.4.refs_2_), channel_id=1, source_target_pairs={{0,56},{8,0},{16,8},{24,16},{32,24},{40,32},{48,40},{56,48},{64,12... | collective-permute-start | bytes 393224 | tf_op jit(solution)/shard_map/ppermute | solution.py:32
  43.5 2.7 collective-permute-done.5.refs_3_
  52.0 3.2 collective-permute-start.10
  55.5 2.6 collective-permute-done.10.refs_8_
  58.1 3.7 %collective-permute-start.11 = (bf16[4,64,256]{2,1,0:T(8,128)(2,1)}, bf16[4,64,256]{2,1,0:T(8,128)(2,1)S(1)}, u32[]{:S(2)}, u32[]{:S(2)}) collective-permute-start(bf16[4,64,256]{2,1,0:T(8,128)(2,1)} %collective-permute-done.10.refs_8_), channel_id=1, source_target_pairs={{0,56},{8,0},{16,8},{24,16},{32,24},{40,32},{48,40},{56,48},{64,12... | collective-permute-start | bytes 393224 | tf_op jit(solution)/shard_map/ppermute | solution.py:32
  62.0 2.6 collective-permute-done.11.refs_7_
  65.9 2.5 collective-permute-done.8.refs_6_
  69.8 3.4 shard_map.93
  78.7 2.5 collective-permute-start.17
  82.0 3.4 collective-permute-done.16.refs_3_
  86.8 2.3 shard_map.95
  89.2 6.4 %collective-permute-done.18.refs_3_ = bf16[4,64,256]{2,1,0:T(8,128)(2,1)S(1)} collective-permute-done((bf16[4,64,256]{2,1,0:T(8,128)(2,1)S(1)}, bf16[4,64,256]{2,1,0:T(8,128)(2,1)S(1)}, u32[]{:S(2)}, u32[]{:S(2)}) %collective-permute-start.18) | collective-permute-done | bytes 131104 | tf_op jit(solution)/shard_map/ppermute | solution.py:32
  97.8 2.9 collective-permute-done.22.refs_9_
  102.8 3.7 %collective-permute-done.23.refs_8_ = bf16[4,64,256]{2,1,0:T(8,128)(2,1)S(1)} collective-permute-done((bf16[4,64,256]{2,1,0:T(8,128)(2,1)S(1)}, bf16[4,64,256]{2,1,0:T(8,128)(2,1)S(1)}, u32[]{:S(2)}, u32[]{:S(2)}) %collective-permute-start.23) | collective-permute-done | bytes 131104 | tf_op jit(solution)/shard_map/ppermute | solution.py:32
  108.6 2.9 collective-permute-done.24.refs_7_
  111.5 2.9 collective-permute-done.21.refs_6_
  115.1 4.6 %shard_map.96 = (bf16[4,4,64,256]{3,2,1,0:T(8,128)(2,1)S(1)}, bf16[4,4,64,256]{3,2,1,0:T(8,128)(2,1)S(1)}, bf16[32,64,256]{2,1,0:T(8,128)(2,1)S(1)}) custom-call(s32[4]{0:T(128)S(1)} %pad_add_fusion.place.refs_0_, s32[4,36]{1,0:T(4,128)S(1)} %fusion.4.refs_1_, bf16[4,64,256]{2,1,0:T(8,128)(2,1)} %copy-done.10, bf16[4,64,256]{2,1,0:T(8,128)(2,1)} %copy-done.19, ...), custom_call_target="tpu_custom_call" | custom-call | flops 400000000 | bytes 9000000 | tf_op jit(solution)/shard_map/pallas_call | solution.py:186
  125.6 9.8 %collective-permute-start.28 = (bf16[4,64,256]{2,1,0:T(8,128)(2,1)S(1)}, bf16[4,64,256]{2,1,0:T(8,128)(2,1)S(1)}, u32[]{:S(2)}, u32[]{:S(2)}) collective-permute-start(bf16[4,64,256]{2,1,0:T(8,128)(2,1)S(1)} %get-tuple-element.89), channel_id=1, source_target_pairs={{0,6},{1,7},{2,0},{3,1},{4,2},{5,3},{6,4},{7,5},{8,14},{9,15},{10,... | collective-permute-start | bytes 393224 | tf_op jit(solution)/shard_map/ppermute | solution.py:36
  135.4 3.9 %collective-permute-done.28.refs_4_ = bf16[4,64,256]{2,1,0:T(8,128)(2,1)S(1)} collective-permute-done((bf16[4,64,256]{2,1,0:T(8,128)(2,1)S(1)}, bf16[4,64,256]{2,1,0:T(8,128)(2,1)S(1)}, u32[]{:S(2)}, u32[]{:S(2)}) %collective-permute-start.28) | collective-permute-done | bytes 131104 | tf_op jit(solution)/shard_map/ppermute | solution.py:36
  139.2 2.3 shard_map.98
  141.6 6.2 %collective-permute-done.29.refs_3_ = bf16[4,64,256]{2,1,0:T(8,128)(2,1)S(1)} collective-permute-done((bf16[4,64,256]{2,1,0:T(8,128)(2,1)S(1)}, bf16[4,64,256]{2,1,0:T(8,128)(2,1)S(1)}, u32[]{:S(2)}, u32[]{:S(2)}) %collective-permute-start.29) | collective-permute-done | bytes 131104 | tf_op jit(solution)/shard_map/ppermute | solution.py:32
  150.0 3.9 %collective-permute-done.33.refs_9_ = bf16[4,64,256]{2,1,0:T(8,128)(2,1)S(1)} collective-permute-done((bf16[4,64,256]{2,1,0:T(8,128)(2,1)S(1)}, bf16[4,64,256]{2,1,0:T(8,128)(2,1)S(1)}, u32[]{:S(2)}, u32[]{:S(2)}) %collective-permute-start.33) | collective-permute-done | bytes 131104 | tf_op jit(solution)/shard_map/ppermute | solution.py:32
  155.9 3.9 %collective-permute-done.34.refs_8_ = bf16[4,64,256]{2,1,0:T(8,128)(2,1)S(1)} collective-permute-done((bf16[4,64,256]{2,1,0:T(8,128)(2,1)S(1)}, bf16[4,64,256]{2,1,0:T(8,128)(2,1)S(1)}, u32[]{:S(2)}, u32[]{:S(2)}) %collective-permute-start.34) | collective-permute-done | bytes 131104 | tf_op jit(solution)/shard_map/ppermute | solution.py:32
  161.8 2.9 collective-permute-done.35.refs_7_
  164.7 2.7 collective-permute-done.32.refs_6_
  168.1 5.2 %shard_map.99 = (bf16[4,4,64,256]{3,2,1,0:T(8,128)(2,1)S(1)}, bf16[4,4,64,256]{3,2,1,0:T(8,128)(2,1)S(1)}) custom-call(s32[4]{0:T(128)S(1)} %pad_add_fusion.place.refs_0_, s32[4,36]{1,0:T(4,128)S(1)} %fusion.4.refs_1_, bf16[4,64,256]{2,1,0:T(8,128)(2,1)} %copy-done.7, bf16[4,64,256]{2,1,0:T(8,128)(2,1)} %copy-done.18, bf16[4,64,256]{2,1,0:T(8,128)(2,1)} %copy-done.24, ...), custom_call_target="tpu_custom_call" | custom-call | flops 400000000 | bytes 9000000 | tf_op jit(solution)/shard_map/pallas_call | solution.py:186
  176.5 3.2 collective-permute-start.38
  179.7 2.5 collective-permute-start.39
  186.3 3.2 shard_map.101
  189.6 6.5 %collective-permute-done.40.refs_3_ = bf16[4,64,256]{2,1,0:T(8,128)(2,1)S(1)} collective-permute-done((bf16[4,64,256]{2,1,0:T(8,128)(2,1)S(1)}, bf16[4,64,256]{2,1,0:T(8,128)(2,1)S(1)}, u32[]{:S(2)}, u32[]{:S(2)}) %collective-permute-start.40) | collective-permute-done | bytes 131104 | tf_op jit(solution)/shard_map/ppermute | solution.py:32
  198.7 2.6 collective-permute-done.44.refs_9_
  203.7 2.8 collective-permute-done.45.refs_8_
  206.5 2.6 collective-permute-start.46
  211.6 4.0 %collective-permute-done.43.refs_6_ = bf16[4,64,256]{2,1,0:T(8,128)(2,1)S(1)} collective-permute-done((bf16[4,64,256]{2,1,0:T(8,128)(2,1)S(1)}, bf16[4,64,256]{2,1,0:T(8,128)(2,1)S(1)}, u32[]{:S(2)}, u32[]{:S(2)}) %collective-permute-start.43) | collective-permute-done | bytes 131104 | tf_op jit(solution)/shard_map/ppermute | solution.py:32
  216.3 3.4 shard_map.102
  222.8 3.3 collective-permute-start.49
  226.1 2.5 collective-permute-start.50
  232.8 2.3 shard_map.104
  235.2 6.6 %collective-permute-done.51.refs_3_ = bf16[4,64,256]{2,1,0:T(8,128)(2,1)S(1)} collective-permute-done((bf16[4,64,256]{2,1,0:T(8,128)(2,1)S(1)}, bf16[4,64,256]{2,1,0:T(8,128)(2,1)S(1)}, u32[]{:S(2)}, u32[]{:S(2)}) %collective-permute-start.51) | collective-permute-done | bytes 131104 | tf_op jit(solution)/shard_map/ppermute | solution.py:32
  243.9 2.9 collective-permute-done.55.refs_9_
  248.8 3.3 collective-permute-done.56.refs_8_
  254.5 2.6 collective-permute-done.57.refs_7_
  257.1 3.5 %collective-permute-done.54.refs_6_ = bf16[4,64,256]{2,1,0:T(8,128)(2,1)S(1)} collective-permute-done((bf16[4,64,256]{2,1,0:T(8,128)(2,1)S(1)}, bf16[4,64,256]{2,1,0:T(8,128)(2,1)S(1)}, u32[]{:S(2)}, u32[]{:S(2)}) %collective-permute-start.54) | collective-permute-done | bytes 131104 | tf_op jit(solution)/shard_map/ppermute | solution.py:32
  261.3 4.1 %shard_map.105 = (bf16[4,4,64,256]{3,2,1,0:T(8,128)(2,1)S(1)}, bf16[4,4,64,256]{3,2,1,0:T(8,128)(2,1)S(1)}, bf16[32,64,256]{2,1,0:T(8,128)(2,1)S(1)}) custom-call(s32[4]{0:T(128)S(1)} %pad_add_fusion.place.refs_0_, s32[4,36]{1,0:T(4,128)S(1)} %fusion.4.refs_1_, bf16[4,64,256]{2,1,0:T(8,128)(2,1)} %copy-done.8, bf16[4,64,256]{2,1,0:T(8,128)(2,1)} %copy-done.20, ...), custom_call_target="tpu_custom_call" | custom-call | flops 400000000 | bytes 9000000 | tf_op jit(solution)/shard_map/pallas_call | solution.py:186
  269.1 3.3 collective-permute-start.60
  274.5 2.6 collective-permute-done.60.refs_3_
  278.7 2.3 shard_map.107
  281.2 3.2 collective-permute-start.66
  284.4 3.0 collective-permute-done.62.refs_3_
  287.4 3.2 collective-permute-start.67
  290.6 2.9 collective-permute-done.63.refs_4_
  293.6 3.2 collective-permute-start.68
  296.8 2.9 collective-permute-done.64.refs_5_
  299.7 6.2 %collective-permute-done.65.refs_6_ = bf16[4,64,256]{2,1,0:T(8,128)(2,1)S(1)} collective-permute-done((bf16[4,64,256]{2,1,0:T(8,128)(2,1)S(1)}, bf16[4,64,256]{2,1,0:T(8,128)(2,1)S(1)}, u32[]{:S(2)}, u32[]{:S(2)}) %collective-permute-start.65) | collective-permute-done | bytes 131104 | tf_op jit(solution)/shard_map/ppermute | solution.py:32
  306.6 6.2 %shard_map.108 = (bf16[4,4,64,256]{3,2,1,0:T(8,128)(2,1)S(1)}, bf16[4,4,64,256]{3,2,1,0:T(8,128)(2,1)S(1)}) custom-call(s32[4]{0:T(128)S(1)} %pad_add_fusion.place.refs_0_, s32[4,36]{1,0:T(4,128)S(1)} %fusion.4.refs_1_, bf16[4,64,256]{2,1,0:T(8,128)(2,1)} %copy-done.9, bf16[4,64,256]{2,1,0:T(8,128)(2,1)} %copy-done.21, bf16[4,64,256]{2,1,0:T(8,128)(2,1)} %copy-done.25, ...), custom_call_target="tpu_custom_call" | custom-call | flops 400000000 | bytes 9000000 | tf_op jit(solution)/shard_map/pallas_call | solution.py:186
  315.4 3.0 collective-permute-start.71
  318.4 2.5 collective-permute-start.72
  320.9 2.6 collective-permute-done.71.refs_2_
  325.2 3.7 %collective-permute-start.73 = (bf16[4,64,256]{2,1,0:T(8,128)(2,1)S(1)}, bf16[4,64,256]{2,1,0:T(8,128)(2,1)S(1)}, u32[]{:S(2)}, u32[]{:S(2)}) collective-permute-start(bf16[4,64,256]{2,1,0:T(8,128)(2,1)S(1)} %get-tuple-element.131), channel_id=1, source_target_pairs={{0,192},{8,200},{16,208},{24,216},{32,224},{40,232},{48,240},{56,2... | collective-permute-start | bytes 393224 | tf_op jit(solution)/shard_map/ppermute | solution.py:28
  328.9 2.3 collective-permute-start.74
  331.2 2.2 collective-permute-done.73.refs_1_
  333.5 3.4 collective-permute-done.74.refs_2_
  (283 shorter events, 100.7 us)
Async XLA Ops:
  6.6 107.9 %all-gather.6.cloned.1.call-start = ((), (), s32[]{:S(2)}) async-start(), calls=%async_computation | async-start | bytes 4587520 | tf_op jit(solution)/shard_map/all_gather | solution.py:66
  7.9 29.4 %collective-permute-start.3 = (bf16[7,256,256]{2,1,0:T(8,128)(2,1)S(1)}, bf16[7,256,256]{2,1,0:T(8,128)(2,1)}, u32[]{:S(2)}, u32[]{:S(2)}) collective-permute-start(bf16[7,256,256]{2,1,0:T(8,128)(2,1)S(1)} %shard_map.92.refs_10_.refs_9_.refs_11_.refs_12_), channel_id=1, source_target_pairs={{0,64},{8,72},{16,80},{24,88},{32,96},{40,104},{48,112},{56,120},{... | collective-permute-start | bytes 2752520 | tf_op jit(solution)/shard_map/ppermute | solution.py:28
  9.4 27.8 %collective-permute-start.4 = (bf16[7,256,256]{2,1,0:T(8,128)(2,1)S(1)}, bf16[7,256,256]{2,1,0:T(8,128)(2,1)}, u32[]{:S(2)}, u32[]{:S(2)}) collective-permute-start(bf16[7,256,256]{2,1,0:T(8,128)(2,1)S(1)} %shard_map.92.refs_10_.refs_9_.refs_11_.refs_12_), channel_id=1, source_target_pairs={{0,192},{8,200},{16,208},{24,216},{32,224},{40,232},{48,240},{56,2... | collective-permute-start | bytes 2752520 | tf_op jit(solution)/shard_map/ppermute | solution.py:28
  13.1 23.4 %collective-permute-start.2 = (bf16[272,256]{1,0:T(8,128)(2,1)S(1)}, bf16[272,256]{1,0:T(8,128)(2,1)S(1)}, u32[]{:S(2)}, u32[]{:S(2)}) collective-permute-start(bf16[272,256]{1,0:T(8,128)(2,1)S(1)} %get-tuple-element.73), channel_id=1, source_target_pairs={{0,192},{8,200},{16,208},{24,216},{32,224},{40,232},{48,240},{56,2... | collective-permute-start | bytes 417800 | tf_op jit(solution)/shard_map/ppermute | solution.py:28
  14.8 21.8 %collective-permute-start.1 = (bf16[272,256]{1,0:T(8,128)(2,1)S(1)}, bf16[272,256]{1,0:T(8,128)(2,1)S(1)}, u32[]{:S(2)}, u32[]{:S(2)}) collective-permute-start(bf16[272,256]{1,0:T(8,128)(2,1)S(1)} %get-tuple-element.72), channel_id=1, source_target_pairs={{0,128},{8,136},{16,144},{24,152},{32,160},{40,168},{48,176},{56,1... | collective-permute-start | bytes 417800 | tf_op jit(solution)/shard_map/ppermute | solution.py:28
  15.6 21.6 %collective-permute-start = (bf16[272,256]{1,0:T(8,128)(2,1)S(1)}, bf16[272,256]{1,0:T(8,128)(2,1)S(1)}, u32[]{:S(2)}, u32[]{:S(2)}) collective-permute-start(bf16[272,256]{1,0:T(8,128)(2,1)S(1)} %get-tuple-element.71), channel_id=1, source_target_pairs={{0,64},{8,72},{16,80},{24,88},{32,96},{40,104},{48,112},{56,120},{... | collective-permute-start | bytes 417800 | tf_op jit(solution)/shard_map/ppermute | solution.py:28
  37.3 130.1 %all-gather.8.cloned.1.call-start = ((), (), s32[]{:S(2)}) async-start(), calls=%async_computation.1 | async-start | bytes 5242880 | tf_op jit(solution)/shard_map/all_gather | solution.py:66
  37.4 8.9 %collective-permute-start.5 = (bf16[4,64,256]{2,1,0:T(8,128)(2,1)S(1)}, bf16[4,64,256]{2,1,0:T(8,128)(2,1)S(1)}, u32[]{:S(2)}, u32[]{:S(2)}) collective-permute-start(bf16[4,64,256]{2,1,0:T(8,128)(2,1)S(1)} %pad_maximum_fusion.4.refs_2_), channel_id=1, source_target_pairs={{0,8},{8,16},{16,24},{24,32},{32,40},{40,48},{48,56},{56,0},{64,72... | collective-permute-start | bytes 393224 | tf_op jit(solution)/shard_map/ppermute | solution.py:32
  39.5 12.6 %collective-permute-start.9 = (bf16[4,64,256]{2,1,0:T(8,128)(2,1)S(1)}, bf16[4,64,256]{2,1,0:T(8,128)(2,1)}, u32[]{:S(2)}, u32[]{:S(2)}) collective-permute-start(bf16[4,64,256]{2,1,0:T(8,128)(2,1)S(1)} %pad_maximum_fusion.4.refs_2_), channel_id=1, source_target_pairs={{0,56},{8,0},{16,8},{24,16},{32,24},{40,32},{48,40},{56,48},{64,12... | collective-permute-start | bytes 393224 | tf_op jit(solution)/shard_map/ppermute | solution.py:32
  46.2 9.0 %collective-permute-start.6 = (bf16[4,64,256]{2,1,0:T(8,128)(2,1)S(1)}, bf16[4,64,256]{2,1,0:T(8,128)(2,1)}, u32[]{:S(2)}, u32[]{:S(2)}) collective-permute-start(bf16[4,64,256]{2,1,0:T(8,128)(2,1)S(1)} %collective-permute-done.5.refs_3_), channel_id=1, source_target_pairs={{0,8},{8,16},{16,24},{24,32},{32,40},{40,48},{48,56},{56,0},{64,72... | collective-permute-start | bytes 393224 | tf_op jit(solution)/shard_map/ppermute | solution.py:32
  47.5 20.9 %collective-permute-start.12 = (bf16[4,256,256]{2,1,0:T(8,128)(2,1)S(1)}, bf16[4,256,256]{2,1,0:T(8,128)(2,1)S(1)}, u32[]{:S(2)}, u32[]{:S(2)}) collective-permute-start(bf16[4,256,256]{2,1,0:T(8,128)(2,1)S(1)} %slice.132), channel_id=1, source_target_pairs={{0,64},{8,72},{16,80},{24,88},{32,96},{40,104},{48,112},{56,120},{... | collective-permute-start | bytes 1572872 | tf_op jit(solution)/shard_map/ppermute | solution.py:28
  50.9 15.0 %collective-permute-start.13 = (bf16[3,256,256]{2,1,0:T(8,128)(2,1)S(1)}, bf16[3,256,256]{2,1,0:T(8,128)(2,1)S(1)}, u32[]{:S(2)}, u32[]{:S(2)}) collective-permute-start(bf16[3,256,256]{2,1,0:T(8,128)(2,1)S(1)} %slice.133), channel_id=1, source_target_pairs={{0,192},{8,200},{16,208},{24,216},{32,224},{40,232},{48,240},{56,2... | collective-permute-start | bytes 1179656 | tf_op jit(solution)/shard_map/ppermute | solution.py:28
  52.0 6.1 %collective-permute-start.10 = (bf16[4,64,256]{2,1,0:T(8,128)(2,1)}, bf16[4,64,256]{2,1,0:T(8,128)(2,1)}, u32[]{:S(2)}, u32[]{:S(2)}) collective-permute-start(bf16[4,64,256]{2,1,0:T(8,128)(2,1)} %collective-permute-done.9.refs_9_), channel_id=1, source_target_pairs={{0,56},{8,0},{16,8},{24,16},{32,24},{40,32},{48,40},{56,48},{64,12... | collective-permute-start | bytes 393224 | tf_op jit(solution)/shard_map/ppermute | solution.py:32
  55.3 6.5 %collective-permute-start.7 = (bf16[4,64,256]{2,1,0:T(8,128)(2,1)}, bf16[4,64,256]{2,1,0:T(8,128)(2,1)}, u32[]{:S(2)}, u32[]{:S(2)}) collective-permute-start(bf16[4,64,256]{2,1,0:T(8,128)(2,1)} %collective-permute-done.6.refs_4_), channel_id=1, source_target_pairs={{0,8},{8,16},{16,24},{24,32},{32,40},{40,48},{48,56},{56,0},{64,72... | collective-permute-start | bytes 393224 | tf_op jit(solution)/shard_map/ppermute | solution.py:32
  58.1 6.5 %collective-permute-start.11 = (bf16[4,64,256]{2,1,0:T(8,128)(2,1)}, bf16[4,64,256]{2,1,0:T(8,128)(2,1)S(1)}, u32[]{:S(2)}, u32[]{:S(2)}) collective-permute-start(bf16[4,64,256]{2,1,0:T(8,128)(2,1)} %collective-permute-done.10.refs_8_), channel_id=1, source_target_pairs={{0,56},{8,0},{16,8},{24,16},{32,24},{40,32},{48,40},{56,48},{64,12... | collective-permute-start | bytes 393224 | tf_op jit(solution)/shard_map/ppermute | solution.py:32
  61.8 6.6 %collective-permute-start.8 = (bf16[4,64,256]{2,1,0:T(8,128)(2,1)}, bf16[4,64,256]{2,1,0:T(8,128)(2,1)S(1)}, u32[]{:S(2)}, u32[]{:S(2)}) collective-permute-start(bf16[4,64,256]{2,1,0:T(8,128)(2,1)} %collective-permute-done.7.refs_5_), channel_id=1, source_target_pairs={{0,8},{8,16},{16,24},{24,32},{32,40},{40,48},{48,56},{56,0},{64,72... | collective-permute-start | bytes 393224 | tf_op jit(solution)/shard_map/ppermute | solution.py:32
  77.5 7.9 %collective-permute-start.16 = (bf16[4,64,256]{2,1,0:T(8,128)(2,1)S(1)}, bf16[4,64,256]{2,1,0:T(8,128)(2,1)S(1)}, u32[]{:S(2)}, u32[]{:S(2)}) collective-permute-start(bf16[4,64,256]{2,1,0:T(8,128)(2,1)S(1)} %get-tuple-element.79), channel_id=1, source_target_pairs={{0,4},{1,5},{2,6},{3,7},{4,0},{5,1},{6,2},{7,3},{8,12},{9,13},{10,... | collective-permute-start | bytes 393224 | tf_op jit(solution)/shard_map/ppermute | solution.py:36
  78.7 8.1 %collective-permute-start.17 = (bf16[4,64,256]{2,1,0:T(8,128)(2,1)S(1)}, bf16[4,64,256]{2,1,0:T(8,128)(2,1)S(1)}, u32[]{:S(2)}, u32[]{:S(2)}) collective-permute-start(bf16[4,64,256]{2,1,0:T(8,128)(2,1)S(1)} %get-tuple-element.80), channel_id=1, source_target_pairs={{0,6},{1,7},{2,0},{3,1},{4,2},{5,3},{6,4},{7,5},{8,14},{9,15},{10,... | collective-permute-start | bytes 393224 | tf_op jit(solution)/shard_map/ppermute | solution.py:36
  89.1 6.5 %collective-permute-start.18 = (bf16[4,64,256]{2,1,0:T(8,128)(2,1)S(1)}, bf16[4,64,256]{2,1,0:T(8,128)(2,1)S(1)}, u32[]{:S(2)}, u32[]{:S(2)}) collective-permute-start(bf16[4,64,256]{2,1,0:T(8,128)(2,1)S(1)} %get-tuple-element.81.refs_2_), channel_id=1, source_target_pairs={{0,8},{8,16},{16,24},{24,32},{32,40},{40,48},{48,56},{56,0},{64,72... | collective-permute-start | bytes 393224 | tf_op jit(solution)/shard_map/ppermute | solution.py:32
  95.7 120.0 %all-gather.10.cloned.1.call-start = ((), (), s32[]{:S(2)}) async-start(), calls=%async_computation.2 | async-start | bytes 4587520 | tf_op jit(solution)/shard_map/all_gather | solution.py:66
  95.8 6.3 %collective-permute-start.19 = (bf16[4,64,256]{2,1,0:T(8,128)(2,1)S(1)}, bf16[4,64,256]{2,1,0:T(8,128)(2,1)S(1)}, u32[]{:S(2)}, u32[]{:S(2)}) collective-permute-start(bf16[4,64,256]{2,1,0:T(8,128)(2,1)S(1)} %collective-permute-done.18.refs_3_), channel_id=1, source_target_pairs={{0,8},{8,16},{16,24},{24,32},{32,40},{40,48},{48,56},{56,0},{64,72... | collective-permute-start | bytes 393224 | tf_op jit(solution)/shard_map/ppermute | solution.py:32
  102.1 6.2 %collective-permute-start.20 = (bf16[4,64,256]{2,1,0:T(8,128)(2,1)S(1)}, bf16[4,64,256]{2,1,0:T(8,128)(2,1)S(1)}, u32[]{:S(2)}, u32[]{:S(2)}) collective-permute-start(bf16[4,64,256]{2,1,0:T(8,128)(2,1)S(1)} %collective-permute-done.19.refs_4_), channel_id=1, source_target_pairs={{0,8},{8,16},{16,24},{24,32},{32,40},{40,48},{48,56},{56,0},{64,72... | collective-permute-start | bytes 393224 | tf_op jit(solution)/shard_map/ppermute | solution.py:32
  108.3 6.2 %collective-permute-start.21 = (bf16[4,64,256]{2,1,0:T(8,128)(2,1)S(1)}, bf16[4,64,256]{2,1,0:T(8,128)(2,1)S(1)}, u32[]{:S(2)}, u32[]{:S(2)}) collective-permute-start(bf16[4,64,256]{2,1,0:T(8,128)(2,1)S(1)} %collective-permute-done.20.refs_5_), channel_id=1, source_target_pairs={{0,8},{8,16},{16,24},{24,32},{32,40},{40,48},{48,56},{56,0},{64,72... | collective-permute-start | bytes 393224 | tf_op jit(solution)/shard_map/ppermute | solution.py:32
  122.7 12.7 %collective-permute-start.26 = (bf16[4,64,256]{2,1,0:T(8,128)(2,1)S(1)}, bf16[4,64,256]{2,1,0:T(8,128)(2,1)S(1)}, u32[]{:S(2)}, u32[]{:S(2)}) collective-permute-start(bf16[4,64,256]{2,1,0:T(8,128)(2,1)S(1)} %get-tuple-element.87), channel_id=1, source_target_pairs={{0,2},{1,3},{2,4},{3,5},{4,6},{5,7},{6,0},{7,1},{8,10},{9,11},{10,... | collective-permute-start | bytes 393224 | tf_op jit(solution)/shard_map/ppermute | solution.py:36
  124.0 11.3 %collective-permute-start.27 = (bf16[4,64,256]{2,1,0:T(8,128)(2,1)S(1)}, bf16[4,64,256]{2,1,0:T(8,128)(2,1)S(1)}, u32[]{:S(2)}, u32[]{:S(2)}) collective-permute-start(bf16[4,64,256]{2,1,0:T(8,128)(2,1)S(1)} %get-tuple-element.88), channel_id=1, source_target_pairs={{0,4},{1,5},{2,6},{3,7},{4,0},{5,1},{6,2},{7,3},{8,12},{9,13},{10,... | collective-permute-start | bytes 393224 | tf_op jit(solution)/shard_map/ppermute | solution.py:36
  125.6 13.6 %collective-permute-start.28 = (bf16[4,64,256]{2,1,0:T(8,128)(2,1)S(1)}, bf16[4,64,256]{2,1,0:T(8,128)(2,1)S(1)}, u32[]{:S(2)}, u32[]{:S(2)}) collective-permute-start(bf16[4,64,256]{2,1,0:T(8,128)(2,1)S(1)} %get-tuple-element.89), channel_id=1, source_target_pairs={{0,6},{1,7},{2,0},{3,1},{4,2},{5,3},{6,4},{7,5},{8,14},{9,15},{10,... | collective-permute-start | bytes 393224 | tf_op jit(solution)/shard_map/ppermute | solution.py:36
  141.5 6.3 %collective-permute-start.29 = (bf16[4,64,256]{2,1,0:T(8,128)(2,1)S(1)}, bf16[4,64,256]{2,1,0:T(8,128)(2,1)S(1)}, u32[]{:S(2)}, u32[]{:S(2)}) collective-permute-start(bf16[4,64,256]{2,1,0:T(8,128)(2,1)S(1)} %get-tuple-element.90.refs_2_), channel_id=1, source_target_pairs={{0,8},{8,16},{16,24},{24,32},{32,40},{40,48},{48,56},{56,0},{64,72... | collective-permute-start | bytes 393224 | tf_op jit(solution)/shard_map/ppermute | solution.py:32
  147.8 112.8 %all-gather.12.cloned.1.call-start = ((), (), s32[]{:S(2)}) async-start(), calls=%async_computation.3 | async-start | bytes 4587520 | tf_op jit(solution)/shard_map/all_gather | solution.py:66
  147.9 6.0 %collective-permute-start.33 = (bf16[4,64,256]{2,1,0:T(8,128)(2,1)S(1)}, bf16[4,64,256]{2,1,0:T(8,128)(2,1)S(1)}, u32[]{:S(2)}, u32[]{:S(2)}) collective-permute-start(bf16[4,64,256]{2,1,0:T(8,128)(2,1)S(1)} %get-tuple-element.90.refs_2_), channel_id=1, source_target_pairs={{0,56},{8,0},{16,8},{24,16},{32,24},{40,32},{48,40},{56,48},{64,12... | collective-permute-start | bytes 393224 | tf_op jit(solution)/shard_map/ppermute | solution.py:32
  148.0 6.3 %collective-permute-start.30 = (bf16[4,64,256]{2,1,0:T(8,128)(2,1)S(1)}, bf16[4,64,256]{2,1,0:T(8,128)(2,1)S(1)}, u32[]{:S(2)}, u32[]{:S(2)}) collective-permute-start(bf16[4,64,256]{2,1,0:T(8,128)(2,1)S(1)} %collective-permute-done.29.refs_3_), channel_id=1, source_target_pairs={{0,8},{8,16},{16,24},{24,32},{32,40},{40,48},{48,56},{56,0},{64,72... | collective-permute-start | bytes 393224 | tf_op jit(solution)/shard_map/ppermute | solution.py:32
  153.8 5.9 %collective-permute-start.34 = (bf16[4,64,256]{2,1,0:T(8,128)(2,1)S(1)}, bf16[4,64,256]{2,1,0:T(8,128)(2,1)S(1)}, u32[]{:S(2)}, u32[]{:S(2)}) collective-permute-start(bf16[4,64,256]{2,1,0:T(8,128)(2,1)S(1)} %collective-permute-done.33.refs_9_), channel_id=1, source_target_pairs={{0,56},{8,0},{16,8},{24,16},{32,24},{40,32},{48,40},{56,48},{64,12... | collective-permute-start | bytes 393224 | tf_op jit(solution)/shard_map/ppermute | solution.py:32
  154.2 7.0 %collective-permute-start.31 = (bf16[4,64,256]{2,1,0:T(8,128)(2,1)S(1)}, bf16[4,64,256]{2,1,0:T(8,128)(2,1)S(1)}, u32[]{:S(2)}, u32[]{:S(2)}) collective-permute-start(bf16[4,64,256]{2,1,0:T(8,128)(2,1)S(1)} %collective-permute-done.30.refs_4_), channel_id=1, source_target_pairs={{0,8},{8,16},{16,24},{24,32},{32,40},{40,48},{48,56},{56,0},{64,72... | collective-permute-start | bytes 393224 | tf_op jit(solution)/shard_map/ppermute | solution.py:32
  161.3 6.2 %collective-permute-start.32 = (bf16[4,64,256]{2,1,0:T(8,128)(2,1)S(1)}, bf16[4,64,256]{2,1,0:T(8,128)(2,1)S(1)}, u32[]{:S(2)}, u32[]{:S(2)}) collective-permute-start(bf16[4,64,256]{2,1,0:T(8,128)(2,1)S(1)} %collective-permute-done.31.refs_5_), channel_id=1, source_target_pairs={{0,8},{8,16},{16,24},{24,32},{32,40},{40,48},{48,56},{56,0},{64,72... | collective-permute-start | bytes 393224 | tf_op jit(solution)/shard_map/ppermute | solution.py:32
  175.4 6.9 %collective-permute-start.37 = (bf16[4,64,256]{2,1,0:T(8,128)(2,1)S(1)}, bf16[4,64,256]{2,1,0:T(8,128)(2,1)S(1)}, u32[]{:S(2)}, u32[]{:S(2)}) collective-permute-start(bf16[4,64,256]{2,1,0:T(8,128)(2,1)S(1)} %get-tuple-element.96), channel_id=1, source_target_pairs={{0,2},{1,3},{2,4},{3,5},{4,6},{5,7},{6,0},{7,1},{8,10},{9,11},{10,... | collective-permute-start | bytes 393224 | tf_op jit(solution)/shard_map/ppermute | solution.py:36
  176.5 7.9 %collective-permute-start.38 = (bf16[4,64,256]{2,1,0:T(8,128)(2,1)S(1)}, bf16[4,64,256]{2,1,0:T(8,128)(2,1)S(1)}, u32[]{:S(2)}, u32[]{:S(2)}) collective-permute-start(bf16[4,64,256]{2,1,0:T(8,128)(2,1)S(1)} %get-tuple-element.97), channel_id=1, source_target_pairs={{0,4},{1,5},{2,6},{3,7},{4,0},{5,1},{6,2},{7,3},{8,12},{9,13},{10,... | collective-permute-start | bytes 393224 | tf_op jit(solution)/shard_map/ppermute | solution.py:36
  179.7 6.6 %collective-permute-start.39 = (bf16[4,64,256]{2,1,0:T(8,128)(2,1)S(1)}, bf16[4,64,256]{2,1,0:T(8,128)(2,1)S(1)}, u32[]{:S(2)}, u32[]{:S(2)}) collective-permute-start(bf16[4,64,256]{2,1,0:T(8,128)(2,1)S(1)} %get-tuple-element.98), channel_id=1, source_target_pairs={{0,6},{1,7},{2,0},{3,1},{4,2},{5,3},{6,4},{7,5},{8,14},{9,15},{10,... | collective-permute-start | bytes 393224 | tf_op jit(solution)/shard_map/ppermute | solution.py:36
  189.5 6.6 %collective-permute-start.40 = (bf16[4,64,256]{2,1,0:T(8,128)(2,1)S(1)}, bf16[4,64,256]{2,1,0:T(8,128)(2,1)S(1)}, u32[]{:S(2)}, u32[]{:S(2)}) collective-permute-start(bf16[4,64,256]{2,1,0:T(8,128)(2,1)S(1)} %get-tuple-element.99.refs_2_), channel_id=1, source_target_pairs={{0,8},{8,16},{16,24},{24,32},{32,40},{40,48},{48,56},{56,0},{64,72... | collective-permute-start | bytes 393224 | tf_op jit(solution)/shard_map/ppermute | solution.py:32
  196.2 109.8 %all-gather.14.cloned.1.call-start = ((), (), s32[]{:S(2)}) async-start(), calls=%async_computation.4 | async-start | bytes 3932160 | tf_op jit(solution)/shard_map/all_gather | solution.py:66
  196.7 6.6 %collective-permute-start.41 = (bf16[4,64,256]{2,1,0:T(8,128)(2,1)S(1)}, bf16[4,64,256]{2,1,0:T(8,128)(2,1)S(1)}, u32[]{:S(2)}, u32[]{:S(2)}) collective-permute-start(bf16[4,64,256]{2,1,0:T(8,128)(2,1)S(1)} %collective-permute-done.40.refs_3_), channel_id=1, source_target_pairs={{0,8},{8,16},{16,24},{24,32},{32,40},{40,48},{48,56},{56,0},{64,72... | collective-permute-start | bytes 393224 | tf_op jit(solution)/shard_map/ppermute | solution.py:32
  203.3 6.2 %collective-permute-start.42 = (bf16[4,64,256]{2,1,0:T(8,128)(2,1)S(1)}, bf16[4,64,256]{2,1,0:T(8,128)(2,1)S(1)}, u32[]{:S(2)}, u32[]{:S(2)}) collective-permute-start(bf16[4,64,256]{2,1,0:T(8,128)(2,1)S(1)} %collective-permute-done.41.refs_4_), channel_id=1, source_target_pairs={{0,8},{8,16},{16,24},{24,32},{32,40},{40,48},{48,56},{56,0},{64,72... | collective-permute-start | bytes 393224 | tf_op jit(solution)/shard_map/ppermute | solution.py:32
  209.5 6.2 %collective-permute-start.43 = (bf16[4,64,256]{2,1,0:T(8,128)(2,1)S(1)}, bf16[4,64,256]{2,1,0:T(8,128)(2,1)S(1)}, u32[]{:S(2)}, u32[]{:S(2)}) collective-permute-start(bf16[4,64,256]{2,1,0:T(8,128)(2,1)S(1)} %collective-permute-done.42.refs_5_), channel_id=1, source_target_pairs={{0,8},{8,16},{16,24},{24,32},{32,40},{40,48},{48,56},{56,0},{64,72... | collective-permute-start | bytes 393224 | tf_op jit(solution)/shard_map/ppermute | solution.py:32
  222.7 5.9 %collective-permute-start.48 = (bf16[4,64,256]{2,1,0:T(8,128)(2,1)S(1)}, bf16[4,64,256]{2,1,0:T(8,128)(2,1)S(1)}, u32[]{:S(2)}, u32[]{:S(2)}) collective-permute-start(bf16[4,64,256]{2,1,0:T(8,128)(2,1)S(1)} %get-tuple-element.104), channel_id=1, source_target_pairs={{0,2},{1,3},{2,4},{3,5},{4,6},{5,7},{6,0},{7,1},{8,10},{9,11},{10,... | collective-permute-start | bytes 393224 | tf_op jit(solution)/shard_map/ppermute | solution.py:36
  222.8 7.9 %collective-permute-start.49 = (bf16[4,64,256]{2,1,0:T(8,128)(2,1)S(1)}, bf16[4,64,256]{2,1,0:T(8,128)(2,1)S(1)}, u32[]{:S(2)}, u32[]{:S(2)}) collective-permute-start(bf16[4,64,256]{2,1,0:T(8,128)(2,1)S(1)} %get-tuple-element.105), channel_id=1, source_target_pairs={{0,4},{1,5},{2,6},{3,7},{4,0},{5,1},{6,2},{7,3},{8,12},{9,13},{10,... | collective-permute-start | bytes 393224 | tf_op jit(solution)/shard_map/ppermute | solution.py:36
  226.1 6.6 %collective-permute-start.50 = (bf16[4,64,256]{2,1,0:T(8,128)(2,1)S(1)}, bf16[4,64,256]{2,1,0:T(8,128)(2,1)S(1)}, u32[]{:S(2)}, u32[]{:S(2)}) collective-permute-start(bf16[4,64,256]{2,1,0:T(8,128)(2,1)S(1)} %get-tuple-element.106), channel_id=1, source_target_pairs={{0,6},{1,7},{2,0},{3,1},{4,2},{5,3},{6,4},{7,5},{8,14},{9,15},{10,... | collective-permute-start | bytes 393224 | tf_op jit(solution)/shard_map/ppermute | solution.py:36
  235.1 6.6 %collective-permute-start.51 = (bf16[4,64,256]{2,1,0:T(8,128)(2,1)S(1)}, bf16[4,64,256]{2,1,0:T(8,128)(2,1)S(1)}, u32[]{:S(2)}, u32[]{:S(2)}) collective-permute-start(bf16[4,64,256]{2,1,0:T(8,128)(2,1)S(1)} %get-tuple-element.108.refs_2_), channel_id=1, source_target_pairs={{0,8},{8,16},{16,24},{24,32},{32,40},{40,48},{48,56},{56,0},{64,72... | collective-permute-start | bytes 393224 | tf_op jit(solution)/shard_map/ppermute | solution.py:32
  241.9 6.3 %collective-permute-start.52 = (bf16[4,64,256]{2,1,0:T(8,128)(2,1)S(1)}, bf16[4,64,256]{2,1,0:T(8,128)(2,1)S(1)}, u32[]{:S(2)}, u32[]{:S(2)}) collective-permute-start(bf16[4,64,256]{2,1,0:T(8,128)(2,1)S(1)} %collective-permute-done.51.refs_3_), channel_id=1, source_target_pairs={{0,8},{8,16},{16,24},{24,32},{32,40},{40,48},{48,56},{56,0},{64,72... | collective-permute-start | bytes 393224 | tf_op jit(solution)/shard_map/ppermute | solution.py:32
  248.1 6.2 %collective-permute-start.53 = (bf16[4,64,256]{2,1,0:T(8,128)(2,1)S(1)}, bf16[4,64,256]{2,1,0:T(8,128)(2,1)S(1)}, u32[]{:S(2)}, u32[]{:S(2)}) collective-permute-start(bf16[4,64,256]{2,1,0:T(8,128)(2,1)S(1)} %collective-permute-done.52.refs_4_), channel_id=1, source_target_pairs={{0,8},{8,16},{16,24},{24,32},{32,40},{40,48},{48,56},{56,0},{64,72... | collective-permute-start | bytes 393224 | tf_op jit(solution)/shard_map/ppermute | solution.py:32
  254.3 6.3 %collective-permute-start.54 = (bf16[4,64,256]{2,1,0:T(8,128)(2,1)S(1)}, bf16[4,64,256]{2,1,0:T(8,128)(2,1)S(1)}, u32[]{:S(2)}, u32[]{:S(2)}) collective-permute-start(bf16[4,64,256]{2,1,0:T(8,128)(2,1)S(1)} %collective-permute-done.53.refs_5_), channel_id=1, source_target_pairs={{0,8},{8,16},{16,24},{24,32},{32,40},{40,48},{48,56},{56,0},{64,72... | collective-permute-start | bytes 393224 | tf_op jit(solution)/shard_map/ppermute | solution.py:32
  268.4 6.1 %collective-permute-start.59 = (bf16[4,64,256]{2,1,0:T(8,128)(2,1)S(1)}, bf16[4,64,256]{2,1,0:T(8,128)(2,1)S(1)}, u32[]{:S(2)}, u32[]{:S(2)}) collective-permute-start(bf16[4,64,256]{2,1,0:T(8,128)(2,1)S(1)} %get-tuple-element.114), channel_id=1, source_target_pairs={{0,2},{1,3},{2,4},{3,5},{4,6},{5,7},{6,0},{7,1},{8,10},{9,11},{10,... | collective-permute-start | bytes 393224 | tf_op jit(solution)/shard_map/ppermute | solution.py:36
  269.1 7.9 %collective-permute-start.60 = (bf16[4,64,256]{2,1,0:T(8,128)(2,1)S(1)}, bf16[4,64,256]{2,1,0:T(8,128)(2,1)S(1)}, u32[]{:S(2)}, u32[]{:S(2)}) collective-permute-start(bf16[4,64,256]{2,1,0:T(8,128)(2,1)S(1)} %get-tuple-element.115), channel_id=1, source_target_pairs={{0,4},{1,5},{2,6},{3,7},{4,0},{5,1},{6,2},{7,3},{8,12},{9,13},{10,... | collective-permute-start | bytes 393224 | tf_op jit(solution)/shard_map/ppermute | solution.py:36
  272.4 6.3 %collective-permute-start.61 = (bf16[4,64,256]{2,1,0:T(8,128)(2,1)S(1)}, bf16[4,64,256]{2,1,0:T(8,128)(2,1)S(1)}, u32[]{:S(2)}, u32[]{:S(2)}) collective-permute-start(bf16[4,64,256]{2,1,0:T(8,128)(2,1)S(1)} %get-tuple-element.116), channel_id=1, source_target_pairs={{0,6},{1,7},{2,0},{3,1},{4,2},{5,3},{6,4},{7,5},{8,14},{9,15},{10,... | collective-permute-start | bytes 393224 | tf_op jit(solution)/shard_map/ppermute | solution.py:36
  281.1 6.3 %collective-permute-start.62 = (bf16[4,64,256]{2,1,0:T(8,128)(2,1)S(1)}, bf16[4,64,256]{2,1,0:T(8,128)(2,1)S(1)}, u32[]{:S(2)}, u32[]{:S(2)}) collective-permute-start(bf16[4,64,256]{2,1,0:T(8,128)(2,1)S(1)} %get-tuple-element.118.refs_2_), channel_id=1, source_target_pairs={{0,8},{8,16},{16,24},{24,32},{32,40},{40,48},{48,56},{56,0},{64,72... | collective-permute-start | bytes 393224 | tf_op jit(solution)/shard_map/ppermute | solution.py:32
  281.2 6.2 %collective-permute-start.66 = (bf16[4,64,256]{2,1,0:T(8,128)(2,1)S(1)}, bf16[4,64,256]{2,1,0:T(8,128)(2,1)S(1)}, u32[]{:S(2)}, u32[]{:S(2)}) collective-permute-start(bf16[4,64,256]{2,1,0:T(8,128)(2,1)S(1)} %get-tuple-element.118.refs_2_), channel_id=1, source_target_pairs={{0,56},{8,0},{16,8},{24,16},{32,24},{40,32},{48,40},{56,48},{64,12... | collective-permute-start | bytes 393224 | tf_op jit(solution)/shard_map/ppermute | solution.py:32
  287.4 6.2 %collective-permute-start.63 = (bf16[4,64,256]{2,1,0:T(8,128)(2,1)S(1)}, bf16[4,64,256]{2,1,0:T(8,128)(2,1)S(1)}, u32[]{:S(2)}, u32[]{:S(2)}) collective-permute-start(bf16[4,64,256]{2,1,0:T(8,128)(2,1)S(1)} %collective-permute-done.62.refs_3_), channel_id=1, source_target_pairs={{0,8},{8,16},{16,24},{24,32},{32,40},{40,48},{48,56},{56,0},{64,72... | collective-permute-start | bytes 393224 | tf_op jit(solution)/shard_map/ppermute | solution.py:32
  287.4 6.2 %collective-permute-start.67 = (bf16[4,64,256]{2,1,0:T(8,128)(2,1)S(1)}, bf16[4,64,256]{2,1,0:T(8,128)(2,1)S(1)}, u32[]{:S(2)}, u32[]{:S(2)}) collective-permute-start(bf16[4,64,256]{2,1,0:T(8,128)(2,1)S(1)} %collective-permute-done.66.refs_9_), channel_id=1, source_target_pairs={{0,56},{8,0},{16,8},{24,16},{32,24},{40,32},{48,40},{56,48},{64,12... | collective-permute-start | bytes 393224 | tf_op jit(solution)/shard_map/ppermute | solution.py:32
  293.5 6.2 %collective-permute-start.64 = (bf16[4,64,256]{2,1,0:T(8,128)(2,1)S(1)}, bf16[4,64,256]{2,1,0:T(8,128)(2,1)S(1)}, u32[]{:S(2)}, u32[]{:S(2)}) collective-permute-start(bf16[4,64,256]{2,1,0:T(8,128)(2,1)S(1)} %collective-permute-done.63.refs_4_), channel_id=1, source_target_pairs={{0,8},{8,16},{16,24},{24,32},{32,40},{40,48},{48,56},{56,0},{64,72... | collective-permute-start | bytes 393224 | tf_op jit(solution)/shard_map/ppermute | solution.py:32
  293.6 6.2 %collective-permute-start.68 = (bf16[4,64,256]{2,1,0:T(8,128)(2,1)S(1)}, bf16[4,64,256]{2,1,0:T(8,128)(2,1)S(1)}, u32[]{:S(2)}, u32[]{:S(2)}) collective-permute-start(bf16[4,64,256]{2,1,0:T(8,128)(2,1)S(1)} %collective-permute-done.67.refs_8_), channel_id=1, source_target_pairs={{0,56},{8,0},{16,8},{24,16},{32,24},{40,32},{48,40},{56,48},{64,12... | collective-permute-start | bytes 393224 | tf_op jit(solution)/shard_map/ppermute | solution.py:32
  299.7 6.2 %collective-permute-start.65 = (bf16[4,64,256]{2,1,0:T(8,128)(2,1)S(1)}, bf16[4,64,256]{2,1,0:T(8,128)(2,1)S(1)}, u32[]{:S(2)}, u32[]{:S(2)}) collective-permute-start(bf16[4,64,256]{2,1,0:T(8,128)(2,1)S(1)} %collective-permute-done.64.refs_5_), channel_id=1, source_target_pairs={{0,8},{8,16},{16,24},{24,32},{32,40},{40,48},{48,56},{56,0},{64,72... | collective-permute-start | bytes 393224 | tf_op jit(solution)/shard_map/ppermute | solution.py:32
  314.9 6.0 %collective-permute-start.70 = (bf16[4,64,256]{2,1,0:T(8,128)(2,1)S(1)}, bf16[4,64,256]{2,1,0:T(8,128)(2,1)S(1)}, u32[]{:S(2)}, u32[]{:S(2)}) collective-permute-start(bf16[4,64,256]{2,1,0:T(8,128)(2,1)S(1)} %get-tuple-element.124), channel_id=1, source_target_pairs={{0,2},{1,3},{2,4},{3,5},{4,6},{5,7},{6,0},{7,1},{8,10},{9,11},{10,... | collective-permute-start | bytes 393224 | tf_op jit(solution)/shard_map/ppermute | solution.py:36
  315.4 8.1 %collective-permute-start.71 = (bf16[4,64,256]{2,1,0:T(8,128)(2,1)S(1)}, bf16[4,64,256]{2,1,0:T(8,128)(2,1)S(1)}, u32[]{:S(2)}, u32[]{:S(2)}) collective-permute-start(bf16[4,64,256]{2,1,0:T(8,128)(2,1)S(1)} %get-tuple-element.125), channel_id=1, source_target_pairs={{0,4},{1,5},{2,6},{3,7},{4,0},{5,1},{6,2},{7,3},{8,12},{9,13},{10,... | collective-permute-start | bytes 393224 | tf_op jit(solution)/shard_map/ppermute | solution.py:36
  318.4 6.8 %collective-permute-start.72 = (bf16[4,64,256]{2,1,0:T(8,128)(2,1)S(1)}, bf16[4,64,256]{2,1,0:T(8,128)(2,1)S(1)}, u32[]{:S(2)}, u32[]{:S(2)}) collective-permute-start(bf16[4,64,256]{2,1,0:T(8,128)(2,1)S(1)} %get-tuple-element.126), channel_id=1, source_target_pairs={{0,6},{1,7},{2,0},{3,1},{4,2},{5,3},{6,4},{7,5},{8,14},{9,15},{10,... | collective-permute-start | bytes 393224 | tf_op jit(solution)/shard_map/ppermute | solution.py:36
  325.2 8.2 %collective-permute-start.73 = (bf16[4,64,256]{2,1,0:T(8,128)(2,1)S(1)}, bf16[4,64,256]{2,1,0:T(8,128)(2,1)S(1)}, u32[]{:S(2)}, u32[]{:S(2)}) collective-permute-start(bf16[4,64,256]{2,1,0:T(8,128)(2,1)S(1)} %get-tuple-element.131), channel_id=1, source_target_pairs={{0,192},{8,200},{16,208},{24,216},{32,224},{40,232},{48,240},{56,2... | collective-permute-start | bytes 393224 | tf_op jit(solution)/shard_map/ppermute | solution.py:28
  328.9 7.9 %collective-permute-start.74 = (bf16[4,64,256]{2,1,0:T(8,128)(2,1)S(1)}, bf16[4,64,256]{2,1,0:T(8,128)(2,1)S(1)}, u32[]{:S(2)}, u32[]{:S(2)}) collective-permute-start(bf16[4,64,256]{2,1,0:T(8,128)(2,1)S(1)} %get-tuple-element.132), channel_id=1, source_target_pairs={{0,128},{8,136},{16,144},{24,152},{32,160},{40,168},{48,176},{56,1... | collective-permute-start | bytes 393224 | tf_op jit(solution)/shard_map/ppermute | solution.py:28
  331.2 7.2 %collective-permute-start.75 = (bf16[4,64,256]{2,1,0:T(8,128)(2,1)S(1)}, bf16[4,64,256]{2,1,0:T(8,128)(2,1)S(1)}, u32[]{:S(2)}, u32[]{:S(2)}) collective-permute-start(bf16[4,64,256]{2,1,0:T(8,128)(2,1)S(1)} %get-tuple-element.133), channel_id=1, source_target_pairs={{0,64},{8,72},{16,80},{24,88},{32,96},{40,104},{48,112},{56,120},{... | collective-permute-start | bytes 393224 | tf_op jit(solution)/shard_map/ppermute | solution.py:28
  (77 other events, 658.1 us)
Sparse Core Ops, SparseCore 0:
  37.4 52.8 all-gather.5
  95.8 49.7 all-gather.7
  148.0 48.2 all-gather.9
  197.9 47.1 all-gather.11
  246.8 42.3 all-gather.13

commit v2 on v1

--- a/solution.py
+++ b/solution.py
@@ -80,67 +80,76 @@
     return up + down[:0:-1]
 
 
-def update_body(level, columns, slots, sizes, keep, *refs):
+def update_body(level, columns, slots, sizes, late, *refs):
     count = len(columns)
     place, table = refs[:2]
-    pieces = refs[2 : 2 + Z]
-    kept = refs[2 + Z : 1 + Z + count]
-    rest = refs[1 + Z + count :]
-    blocks = []
+    rest = refs[2:]
+    if late:
+        last, rest = rest[0], rest[2:]
+    else:
+        pieces, rest = rest[: Z - 1], rest[Z - 1 :]
+    kept, blocks = [], []
+    for _ in range(count - 1):
+        kept.append(rest[:Z])
+        rest = rest[Z:]
     for size in sizes:
         blocks.append(rest[:size])
         rest = rest[size:]
-    mine, other, rest = rest[0], rest[1], rest[2:]
-    if keep:
-        held, rest = rest[0], rest[1:]
-    block_buf, piece_buf, acc, slot_at, slot_from, block_sem, piece_sem, panel_sem, keep_sem = rest
+    if late:
+        mine, other, rest = rest[0], rest[1], rest[2:]
+    acc, block_buf, piece_buf, slot_at, slot_from, block_sem, piece_sem, panel_sem = rest
     x, y, core = place[0], place[2], place[3]
     spare = piece_buf.shape[0] - 1
+    far = Z // 2
+
+    def piece_copy(n, dz, piece, at):
+        return pltpu.make_async_copy(
+            kept[n][dz].at[piece & (X - 1)], piece_buf.at[X * Z + at], piece_sem.at[at]
+        )
 
     def scan(n, found):
         for d in range(X):
-
-            def visit(k, at, d=d):
+            for k in range(slots):
                 entry = table[d, columns[n] + k]
+                piece, hop = entry & (X * Z - 1), (entry >> 2) & (Z - 1)
                 live = (entry >> 8) == level
+                if n == count - 1:
+                    live = live & ((hop == far) if late else (hop != far))
+                at = found
 
                 @pl.when(live)
-                def _():
+                def _(n=n, d=d, k=k, entry=entry, piece=piece, hop=hop, at=at):
                     block = block_at(blocks[n], x, d, k)
                     pltpu.make_async_copy(block, block_buf.at[at], block_sem.at[at]).start()
                     slot_at[at] = ((entry >> 5) & (LOCAL - 1)) * X + d
-                    piece = entry & (X * Z - 1)
                     if n < count - 1:
-                        copy = pltpu.make_async_copy(
-                            kept[n].at[piece], piece_buf.at[X * Z + at], piece_sem.at[at]
-                        )
-                        copy.start()
                         slot_from[at] = X * Z + at
+                        for dz in range(Z):
+                            pl.when(hop == dz)(lambda dz=dz: piece_copy(n, dz, piece, at).start())
                     else:
                         slot_from[at] = piece
 
-                return at + live.astype(jnp.int32)
-
-            for k in range(slots):
-                found = visit(k, found)
+                found = found + live.astype(jnp.int32)
         return found
 
-    def panel_copy(d):
-        return pltpu.make_async_copy(pieces[d], piece_buf.at[pl.ds(d * X, X)], panel_sem.at[d])
-
-    for d in range(Z):
-        panel_copy(d).start()
+    def panel_copy(n, d):
+        return pltpu.make_async_copy(pieces[n], piece_buf.at[pl.ds(d * X, X)], panel_sem.at[n])
+
+    places = [d for d in range(Z) if d != far]
+    if not late:
+        for n, d in enumerate(places):
+            panel_copy(n, d).start()
     earlier = jnp.int32(0)
     for n in range(count - 1):
         earlier = scan(n, earlier)
     live = scan(count - 1, earlier)
-    acc[...] = jnp.zeros_like(acc)
     piece_buf[spare] = jnp.zeros_like(piece_buf[spare])
-    for d in range(Z):
-        panel_copy(d).wait()
-    if keep:
-        keep_copy = pltpu.make_async_copy(piece_buf.at[pl.ds(0, X * Z)], held, keep_sem)
-        keep_copy.start()
+    if late:
+        piece_buf[far * X : (far + 1) * X] = last[...]
+    else:
+        acc[...] = jnp.zeros_like(acc)
+        for n, d in enumerate(places):
+            panel_copy(n, d).wait()
     for i in range(GROUP - 1):
         slot_from[live + i] = spare
         slot_at[live + i] = 0
@@ -155,10 +164,7 @@
                 pltpu.make_async_copy(blocks[0][0].at[0], block_buf.at[at], block_sem.at[at]).wait()
 
             if count > 1:
-
-                @pl.when(at < earlier)
-                def _():
-                    pltpu.make_async_copy(kept[0].at[0], piece_buf.at[X * Z + at], piece_sem.at[at]).wait()
+                pl.when(at < earlier)(lambda: piece_copy(0, 0, 0, at).wait())
 
         for i in range(GROUP):
             at = group * GROUP + i
@@ -169,39 +175,51 @@
         return carry
 
     lax.fori_loop(0, (live + (GROUP - 1)) // GROUP, add_products, 0)
-    for d in range(Y):
-        column = ((y + d) & (Y - 1)) * C
-        mine[d] = acc[pl.ds((column + core) * X, X)].astype(mine.dtype)
-        other[d] = acc[pl.ds((column + 1 - core) * X, X)].astype(other.dtype)
-    if keep:
-        keep_copy.wait()
-
-
-def block_updates(place, table, level, columns, slots, pieces, kept, blocks, keep):
-    panel = pieces[0].shape
+    if late:
+        for d in range(Y):
+            column = ((y + d) & (Y - 1)) * C
+            mine[d] = acc[pl.ds((column + core) * X, X)].astype(mine.dtype)
+            other[d] = acc[pl.ds((column + 1 - core) * X, X)].astype(other.dtype)
+
+
+def update_call(place, table, level, columns, slots, inputs, kept, blocks, late):
+    panel = inputs[0].shape
     count = len(columns)
     half = jax.ShapeDtypeStruct((Y,) + panel, jnp.bfloat16)
-    held = jax.ShapeDtypeStruct((X * Z,) + panel[1:], jnp.bfloat16)
+    totals = jax.ShapeDtypeStruct((LOCAL * X,) + panel[1:], jnp.float32)
     total = count * X * slots
+    kept, blocks_in = sum(kept, []), sum(blocks, [])
     return pl.pallas_call(
-        functools.partial(update_body, level, columns, slots, [len(b) for b in blocks], keep),
-        out_shape=(half, half) + (held,) * keep,
-        in_specs=[SMEM] * 2 + [ANY] * (Z + count - 1 + sum(len(b) for b in blocks)),
-        out_specs=(VMEM, VMEM) + (ANY,) * keep,
+        functools.partial(update_body, level, columns, slots, [len(b) for b in blocks], late),
+        out_shape=(half, half, totals) if late else totals,
+        in_specs=[SMEM] * 2
+        + [VMEM if late else ANY] * len(inputs)
+        + [ANY] * (len(kept) + len(blocks_in)),
+        out_specs=(VMEM,) * 3 if late else VMEM,
+        input_output_aliases={3: 2} if late else {},
         scratch_shapes=[
             pltpu.VMEM((total,) + blocks[0][0].shape[1:], jnp.bfloat16),
             pltpu.VMEM((X * Z + total + 1,) + panel[1:], jnp.bfloat16),
-            pltpu.VMEM((LOCAL * X,) + panel[1:], jnp.float32),
             pltpu.SMEM((total + GROUP,), jnp.int32),
             pltpu.SMEM((total + GROUP,), jnp.int32),
             pltpu.SemaphoreType.DMA((total,)),
             pltpu.SemaphoreType.DMA((total,)),
             pltpu.SemaphoreType.DMA((Z,)),
-            pltpu.SemaphoreType.DMA,
         ],
-        compiler_params=params(6 + 5 * count),
-        cost_estimate=pl.CostEstimate(flops=400_000_000, bytes_accessed=9_000_000, transcendentals=0),
-    )(place, table, *map(hbm, pieces), *map(hbm, kept), *sum(blocks, []))
+        compiler_params=params(4 + 5 * count),
+        cost_estimate=pl.CostEstimate(
+            flops=200_000_000, bytes_accessed=3_000_000 if late else 9_000_000, transcendentals=0
+        ),
+    )(place, table, *inputs, *kept, *blocks_in)
+
+
+def block_updates(place, table, level, columns, slots, pieces, kept, blocks):
+    far = Z // 2
+    early = [hbm(piece) for d, piece in enumerate(pieces) if d != far]
+    kept = [[hbm(piece) for piece in held] for held in kept]
+    acc = update_call(place, table, level, columns, slots, early, kept, blocks, False)
+    last = [pieces[far], acc]
+    return update_call(place, table, level, columns[-1:], slots, last, [], blocks[-1:], True)[:2]
 
 
 def pack_body(plan, *refs):
@@ -442,10 +460,10 @@
         if level > 0:
             next_group(pieces[1])
         columns = [n * slots for n in range(level + 1)]
-        mine, other, *held = block_updates(
-            place, table, level + 1, columns, slots, pieces, kept, groups[: level + 1], level + 1 < top
+        mine, other = block_updates(
+            place, table, level + 1, columns, slots, pieces, kept, groups[: level + 1]
         )
-        kept += held
+        kept.append(pieces)
         terms = col_total(mine, other)
         is_top = level + 1 == top
         forward[level + 1], panel = diag_solve(
@@ -460,10 +478,8 @@
         next_group(pieces[1])
         columns = [(top + n) * slots for n in range(top - 1, level - 1, -1)]
         held_blocks = groups[top : 2 * top - level]
-        mine, other, *held = block_updates(
-            place, table, level, columns, slots, pieces, kept, held_blocks, level > 0
-        )
-        kept += held
+        mine, other = block_updates(place, table, level, columns, slots, pieces, kept, held_blocks)
+        kept.append(pieces)
         terms = col_total(mine, other)
         if level > 0:
             rights = [forward[level][d] for d in range(X)]

time: 353 us -> 352 us (level)
  waiting for transfers between devices: 161 us -> 145 us
  Pallas kernels: 44.1 us -> 56.7 us
  starting transfers between devices: 107 us -> 113 us
  local copies, waits for them, and re-layouts: 15.4 us -> 11.2 us
    ppermute x42, waiting for transfers between devices: 102 us -> 73.3 us  [along_z(): lax.ppermute(value, 'row', [(x * Z + z, x * Z + (z + d) % Z) for x in ran...]
    ppermute x42, starting transfers between devices: 48.3 us -> 61.6 us  [along_z(): lax.ppermute(value, 'row', [(x * Z + z, x * Z + (z + d) % Z) for x in ran...]
    pallas_call x6 -> x12, Pallas kernels: 26.8 us -> 39.5 us  [update_call(): pl.pallas_call(functools.partial(update_body, level, columns, slots, [len...]
    ppermute x18, waiting for transfers between devices: 26.1 us -> 35.6 us  [along_y(): lax.ppermute(value, 'col', [(y * C + k, (y + d) % Y * C + k) for y in ran...]
    ppermute x18, starting transfers between devices: 42.5 us -> 36.1 us  [along_y(): lax.ppermute(value, 'col', [(y * C + k, (y + d) % Y * C + k) for y in ran...]
    unnamed x122 -> x118, local copies, waits for them, and re-layouts: 8.47 us -> 4.02 us
  transfers between devices with their start and end apart: 81 -> 81, of which waited for: 60 -> 56; matrix products, arithmetic and copies ran while one was open for 3% -> 3% of each run, Pallas kernels for 10% -> 15%
where the time goes in v2:
time: 352 us; the launch traced here: 345 us
  waiting for transfers between devices  145 us (41%)
  starting transfers between devices  113 us (32%)
  Pallas kernels  56.7 us (16%)
  between operations  14.3 us (4%)
  local copies, waits for them, and re-layouts  11.2 us (3%)
  other arithmetic  4.6 us (1%)
    ppermute x42, waiting for transfers between devices, along_z(): lax.ppermute(value, 'row', [(x * Z + z, x * Z + (z + d) % Z) for x in ran...  73.3 us
    ppermute x42, starting transfers between devices, along_z(): lax.ppermute(value, 'row', [(x * Z + z, x * Z + (z + d) % Z) for x in ran...  61.6 us
    pallas_call x12, Pallas kernels, update_call(): pl.pallas_call(functools.partial(update_body, level, columns, slots, [len...  39.5 us
    ppermute x18, starting transfers between devices, along_y(): lax.ppermute(value, 'col', [(y * C + k, (y + d) % Y * C + k) for y in ran...  36.1 us
    ppermute x18, waiting for transfers between devices, along_y(): lax.ppermute(value, 'col', [(y * C + k, (y + d) % Y * C + k) for y in ran...  35.6 us
    ppermute x10, waiting for transfers between devices, along_x(): lax.ppermute(value, 'row', [(x * Z + z, (x + d) % X * Z + z) for x in ran...  24.6 us
    ppermute x10, starting transfers between devices, along_x(): lax.ppermute(value, 'row', [(x * Z + z, (x + d) % X * Z + z) for x in ran...  14.9 us
    pallas_call x5, Pallas kernels, diag_solve(): pl.pallas_call(functools.partial(solve_body, at, inverses, start, keep_re...  12.4 us
  transfers between devices with their start and end apart: 81, of which 56 were waited for; matrix products, arithmetic and copies ran while one was open for 3% of the time, Pallas kernels for 15%

profile of v2, /device:TPU:8, one launch (start us, length us, event | category | flops | bytes accessed | tf_op | source)
XLA Modules:
  0.0 345.2 jit_solution(11584541854616484211)
XLA Ops:
  16.5 2.6 slice_bitcast_fusion
  23.7 12.8 %collective-permute-done.2.refs_8_ = bf16[272,256]{1,0:T(8,128)(2,1)S(1)} collective-permute-done((bf16[272,256]{1,0:T(8,128)(2,1)S(1)}, bf16[272,256]{1,0:T(8,128)(2,1)S(1)}, u32[]{:S(2)}, u32[]{:S(2)}) %collective-permute-start.2) | collective-permute-done | bytes 139296 | tf_op jit(solution)/shard_map/ppermute | solution.py:28
  39.5 4.0 %collective-permute-start.9 = (bf16[4,64,256]{2,1,0:T(8,128)(2,1)S(1)}, bf16[4,64,256]{2,1,0:T(8,128)(2,1)S(1)}, u32[]{:S(2)}, u32[]{:S(2)}) collective-permute-start(bf16[4,64,256]{2,1,0:T(8,128)(2,1)S(1)} %pad_maximum_fusion.4.refs_2_.refs_9_), channel_id=1, source_target_pairs={{0,56},{8,0},{16,8},{24,16},{32,24},{40,32},{48,40},{56,48},{64,12... | collective-permute-start | bytes 393224 | tf_op jit(solution)/shard_map/ppermute | solution.py:32
  43.5 2.7 collective-permute-done.5.refs_3_.refs_10_
  52.7 3.2 collective-permute-start.10
  56.2 2.3 collective-permute-done.10.refs_7_.refs_15_
  58.5 3.7 %collective-permute-start.11 = (bf16[4,64,256]{2,1,0:T(8,128)(2,1)S(1)}, bf16[4,64,256]{2,1,0:T(8,128)(2,1)S(1)}, u32[]{:S(2)}, u32[]{:S(2)}) collective-permute-start(bf16[4,64,256]{2,1,0:T(8,128)(2,1)S(1)} %collective-permute-done.10.refs_7_.refs_15_), channel_id=1, source_target_pairs={{0,56},{8,0},{16,8},{24,16},{32,24},{40,32},{48,40},{56,48},{64,12... | collective-permute-start | bytes 393224 | tf_op jit(solution)/shard_map/ppermute | solution.py:32
  64.7 3.0 collective-permute-done.13.refs_12_.refs_7_.refs_20_.refs_28_
  69.9 3.2 shard_map.93.refs_3_
  76.6 2.9 collective-permute-start.15
  80.4 2.5 collective-permute-start.17
  82.9 4.5 %collective-permute-done.16.refs_3_ = bf16[4,64,256]{2,1,0:T(8,128)(2,1)S(1)} collective-permute-done((bf16[4,64,256]{2,1,0:T(8,128)(2,1)S(1)}, bf16[4,64,256]{2,1,0:T(8,128)(2,1)S(1)}, u32[]{:S(2)}, u32[]{:S(2)}) %collective-permute-start.16) | collective-permute-done | bytes 131104 | tf_op jit(solution)/shard_map/ppermute | solution.py:36
  88.5 2.3 shard_map.96
  90.9 6.2 %collective-permute-done.18.refs_3_.refs_18_ = bf16[4,64,256]{2,1,0:T(8,128)(2,1)S(1)} collective-permute-done((bf16[4,64,256]{2,1,0:T(8,128)(2,1)S(1)}, bf16[4,64,256]{2,1,0:T(8,128)(2,1)S(1)}, u32[]{:S(2)}, u32[]{:S(2)}) %collective-permute-start.18) | collective-permute-done | bytes 131104 | tf_op jit(solution)/shard_map/ppermute | solution.py:32
  99.2 3.1 collective-permute-done.22.refs_8_.refs_24_
  104.7 3.7 %collective-permute-done.23.refs_7_.refs_23_ = bf16[4,64,256]{2,1,0:T(8,128)(2,1)S(1)} collective-permute-done((bf16[4,64,256]{2,1,0:T(8,128)(2,1)S(1)}, bf16[4,64,256]{2,1,0:T(8,128)(2,1)S(1)}, u32[]{:S(2)}, u32[]{:S(2)}) %collective-permute-start.23) | collective-permute-done | bytes 131104 | tf_op jit(solution)/shard_map/ppermute | solution.py:32
  108.4 2.5 collective-permute-start.24
  111.1 2.3 collective-permute-done.24.refs_6_.refs_22_
  114.1 3.9 %shard_map.97.refs_3_ = f32[32,64,256]{2,1,0:T(8,128)S(1)} custom-call(s32[4]{0:T(128)S(1)} %pad_add_fusion.place.refs_0_, s32[4,36]{1,0:T(4,128)S(1)} %fusion.4.refs_1_, bf16[4,64,256]{2,1,0:T(8,128)(2,1)} %copy-done.6, bf16[4,64,256]{2,1,0:T(8,128)(2,1)} %copy-done.29, bf16[4,64,256]{2,1,0:T(8,128)(2,1)} %copy-done.33, bf16[4,64,256]{2,1,0:T(8,128)(2,1)} %copy-done.37, ...), custom_call_target="tpu_custom_call" | custom-call | flops 200000000 | bytes 9000000 | tf_op jit(solution)/shard_map/pallas_call | solution.py:192
  118.0 2.5 shard_map.98
  122.6 10.7 %collective-permute-start.26 = (bf16[4,64,256]{2,1,0:T(8,128)(2,1)S(1)}, bf16[4,64,256]{2,1,0:T(8,128)(2,1)S(1)}, u32[]{:S(2)}, u32[]{:S(2)}) collective-permute-start(bf16[4,64,256]{2,1,0:T(8,128)(2,1)S(1)} %get-tuple-element.82), channel_id=1, source_target_pairs={{0,2},{1,3},{2,4},{3,5},{4,6},{5,7},{6,0},{7,1},{8,10},{9,11},{10,... | collective-permute-start | bytes 393224 | tf_op jit(solution)/shard_map/ppermute | solution.py:36
  138.0 3.3 collective-permute-done.27.refs_3_
  142.2 2.3 shard_map.100
  145.7 5.1 %collective-permute-done.29.refs_3_ = bf16[4,64,256]{2,1,0:T(8,128)(2,1)S(1)} collective-permute-done((bf16[4,64,256]{2,1,0:T(8,128)(2,1)S(1)}, bf16[4,64,256]{2,1,0:T(8,128)(2,1)S(1)}, u32[]{:S(2)}, u32[]{:S(2)}) %collective-permute-start.29) | collective-permute-done | bytes 131104 | tf_op jit(solution)/shard_map/ppermute | solution.py:32
  153.0 2.9 collective-permute-done.33.refs_8_
  156.0 2.9 collective-permute-start.34
  158.9 2.7 collective-permute-done.34.refs_7_
  161.6 3.5 %collective-permute-start.35 = (bf16[4,64,256]{2,1,0:T(8,128)(2,1)S(1)}, bf16[4,64,256]{2,1,0:T(8,128)(2,1)S(1)}, u32[]{:S(2)}, u32[]{:S(2)}) collective-permute-start(bf16[4,64,256]{2,1,0:T(8,128)(2,1)S(1)} %collective-permute-done.34.refs_7_), channel_id=1, source_target_pairs={{0,56},{8,0},{16,8},{24,16},{32,24},{40,32},{48,40},{56,48},{64,12... | collective-permute-start | bytes 393224 | tf_op jit(solution)/shard_map/ppermute | solution.py:32
  165.1 2.5 collective-permute-done.35.refs_6_
  168.3 5.9 %shard_map.101.refs_3_ = f32[32,64,256]{2,1,0:T(8,128)S(1)} custom-call(s32[4]{0:T(128)S(1)} %pad_add_fusion.place.refs_0_, s32[4,36]{1,0:T(4,128)S(1)} %fusion.4.refs_1_, bf16[4,64,256]{2,1,0:T(8,128)(2,1)} %copy-done.10, bf16[4,64,256]{2,1,0:T(8,128)(2,1)} %copy-done.42, bf16[4,64,256]{2,1,0:T(8,128)(2,1)} %copy-done.46, bf16[4,64,256]{2,1,0:T(8,128)(2,1)} %copy-done.50, ...), custom_call_target="tpu_custom_call" | custom-call | flops 200000000 | bytes 9000000 | tf_op jit(solution)/shard_map/pallas_call | solution.py:192
  174.2 2.5 shard_map.102
  181.1 2.3 collective-permute-start.39
  188.8 3.2 shard_map.104
  192.1 2.5 collective-permute-start.40
  194.6 5.0 %collective-permute-done.40.refs_3_.refs_10_ = bf16[4,64,256]{2,1,0:T(8,128)(2,1)S(1)} collective-permute-done((bf16[4,64,256]{2,1,0:T(8,128)(2,1)S(1)}, bf16[4,64,256]{2,1,0:T(8,128)(2,1)S(1)}, u32[]{:S(2)}, u32[]{:S(2)}) %collective-permute-start.40) | collective-permute-done | bytes 131104 | tf_op jit(solution)/shard_map/ppermute | solution.py:32
  201.8 2.9 collective-permute-done.44.refs_8_.refs_16_
  204.7 2.9 collective-permute-start.45
  207.8 2.8 collective-permute-done.45.refs_7_.refs_15_
  210.7 3.2 collective-permute-start.46
  213.9 2.5 collective-permute-done.46.refs_6_.refs_14_
  217.1 2.8 shard_map.105.refs_3_
  220.1 2.5 shard_map.106
  234.8 2.3 shard_map.108
  237.1 2.7 collective-permute-start.51
  239.8 4.6 %collective-permute-done.51.refs_3_.refs_18_ = bf16[4,64,256]{2,1,0:T(8,128)(2,1)S(1)} collective-permute-done((bf16[4,64,256]{2,1,0:T(8,128)(2,1)S(1)}, bf16[4,64,256]{2,1,0:T(8,128)(2,1)S(1)}, u32[]{:S(2)}, u32[]{:S(2)}) %collective-permute-start.51) | collective-permute-done | bytes 131104 | tf_op jit(solution)/shard_map/ppermute | solution.py:32
  246.6 3.1 collective-permute-done.55.refs_8_.refs_24_
  249.7 3.0 collective-permute-start.56
  252.9 2.8 collective-permute-done.56.refs_7_.refs_23_
  255.7 3.1 collective-permute-start.57
  258.9 2.5 collective-permute-done.57.refs_6_.refs_22_
  262.0 4.1 %shard_map.109.refs_3_ = f32[32,64,256]{2,1,0:T(8,128)S(1)} custom-call(s32[4]{0:T(128)S(1)} %pad_add_fusion.place.refs_0_, s32[4,36]{1,0:T(4,128)S(1)} %fusion.4.refs_1_, bf16[4,64,256]{2,1,0:T(8,128)(2,1)} %copy-done.5, bf16[4,64,256]{2,1,0:T(8,128)(2,1)} %copy-done.30, bf16[4,64,256]{2,1,0:T(8,128)(2,1)} %copy-done.34, bf16[4,64,256]{2,1,0:T(8,128)(2,1)} %copy-done.38, ...), custom_call_target="tpu_custom_call" | custom-call | flops 200000000 | bytes 9000000 | tf_op jit(solution)/shard_map/pallas_call | solution.py:192
  266.1 2.4 shard_map.110
  280.7 2.3 shard_map.112
  283.0 3.1 collective-permute-start.62
  286.5 3.3 collective-permute-done.62.refs_3_
  293.1 2.9 collective-permute-done.63.refs_4_
  299.3 2.9 collective-permute-done.64.refs_5_
  304.0 5.9 %shard_map.113.refs_3_ = f32[32,64,256]{2,1,0:T(8,128)S(1)} custom-call(s32[4]{0:T(128)S(1)} %pad_add_fusion.place.refs_0_, s32[4,36]{1,0:T(4,128)S(1)} %fusion.4.refs_1_, bf16[4,64,256]{2,1,0:T(8,128)(2,1)} %copy-done.11, bf16[4,64,256]{2,1,0:T(8,128)(2,1)} %copy-done.43, bf16[4,64,256]{2,1,0:T(8,128)(2,1)} %copy-done.47, bf16[4,64,256]{2,1,0:T(8,128)(2,1)} %copy-done.51, ...), custom_call_target="tpu_custom_call" | custom-call | flops 200000000 | bytes 9000000 | tf_op jit(solution)/shard_map/pallas_call | solution.py:192
  310.0 2.5 shard_map.114
  318.1 3.0 collective-permute-done.70.refs_1_
  321.0 2.5 collective-permute-done.71.refs_2_
  327.0 2.9 collective-permute-start.74
  329.8 2.3 collective-permute-done.73.refs_1_
  332.1 2.7 collective-permute-done.74.refs_2_
  (285 shorter events, 112.7 us)
Async XLA Ops:
  6.6 106.8 %all-gather.6.cloned.1.call-start = ((), (), s32[]{:S(2)}) async-start(), calls=%async_computation | async-start | bytes 4587520 | tf_op jit(solution)/shard_map/all_gather | solution.py:66
  7.9 29.4 %collective-permute-start.3 = (bf16[7,256,256]{2,1,0:T(8,128)(2,1)S(1)}, bf16[7,256,256]{2,1,0:T(8,128)(2,1)}, u32[]{:S(2)}, u32[]{:S(2)}) collective-permute-start(bf16[7,256,256]{2,1,0:T(8,128)(2,1)S(1)} %shard_map.92.refs_9_.refs_4_.refs_17_.refs_25_), channel_id=1, source_target_pairs={{0,64},{8,72},{16,80},{24,88},{32,96},{40,104},{48,112},{56,120},{... | collective-permute-start | bytes 2752520 | tf_op jit(solution)/shard_map/ppermute | solution.py:28
  9.4 27.8 %collective-permute-start.4 = (bf16[7,256,256]{2,1,0:T(8,128)(2,1)S(1)}, bf16[7,256,256]{2,1,0:T(8,128)(2,1)}, u32[]{:S(2)}, u32[]{:S(2)}) collective-permute-start(bf16[7,256,256]{2,1,0:T(8,128)(2,1)S(1)} %shard_map.92.refs_9_.refs_4_.refs_17_.refs_25_), channel_id=1, source_target_pairs={{0,192},{8,200},{16,208},{24,216},{32,224},{40,232},{48,240},{56,2... | collective-permute-start | bytes 2752520 | tf_op jit(solution)/shard_map/ppermute | solution.py:28
  13.2 23.3 %collective-permute-start.2 = (bf16[272,256]{1,0:T(8,128)(2,1)S(1)}, bf16[272,256]{1,0:T(8,128)(2,1)S(1)}, u32[]{:S(2)}, u32[]{:S(2)}) collective-permute-start(bf16[272,256]{1,0:T(8,128)(2,1)S(1)} %get-tuple-element.69), channel_id=1, source_target_pairs={{0,192},{8,200},{16,208},{24,216},{32,224},{40,232},{48,240},{56,2... | collective-permute-start | bytes 417800 | tf_op jit(solution)/shard_map/ppermute | solution.py:28
  14.8 21.7 %collective-permute-start.1 = (bf16[272,256]{1,0:T(8,128)(2,1)S(1)}, bf16[272,256]{1,0:T(8,128)(2,1)S(1)}, u32[]{:S(2)}, u32[]{:S(2)}) collective-permute-start(bf16[272,256]{1,0:T(8,128)(2,1)S(1)} %get-tuple-element.68), channel_id=1, source_target_pairs={{0,128},{8,136},{16,144},{24,152},{32,160},{40,168},{48,176},{56,1... | collective-permute-start | bytes 417800 | tf_op jit(solution)/shard_map/ppermute | solution.py:28
  15.6 21.6 %collective-permute-start = (bf16[272,256]{1,0:T(8,128)(2,1)S(1)}, bf16[272,256]{1,0:T(8,128)(2,1)S(1)}, u32[]{:S(2)}, u32[]{:S(2)}) collective-permute-start(bf16[272,256]{1,0:T(8,128)(2,1)S(1)} %get-tuple-element.67), channel_id=1, source_target_pairs={{0,64},{8,72},{16,80},{24,88},{32,96},{40,104},{48,112},{56,120},{... | collective-permute-start | bytes 417800 | tf_op jit(solution)/shard_map/ppermute | solution.py:28
  37.3 130.3 %all-gather.8.cloned.1.call-start = ((), (), s32[]{:S(2)}) async-start(), calls=%async_computation.1 | async-start | bytes 5242880 | tf_op jit(solution)/shard_map/all_gather | solution.py:66
  37.3 8.9 %collective-permute-start.5 = (bf16[4,64,256]{2,1,0:T(8,128)(2,1)S(1)}, bf16[4,64,256]{2,1,0:T(8,128)(2,1)S(1)}, u32[]{:S(2)}, u32[]{:S(2)}) collective-permute-start(bf16[4,64,256]{2,1,0:T(8,128)(2,1)S(1)} %pad_maximum_fusion.4.refs_2_.refs_9_), channel_id=1, source_target_pairs={{0,8},{8,16},{16,24},{24,32},{32,40},{40,48},{48,56},{56,0},{64,72... | collective-permute-start | bytes 393224 | tf_op jit(solution)/shard_map/ppermute | solution.py:32
  39.5 13.3 %collective-permute-start.9 = (bf16[4,64,256]{2,1,0:T(8,128)(2,1)S(1)}, bf16[4,64,256]{2,1,0:T(8,128)(2,1)S(1)}, u32[]{:S(2)}, u32[]{:S(2)}) collective-permute-start(bf16[4,64,256]{2,1,0:T(8,128)(2,1)S(1)} %pad_maximum_fusion.4.refs_2_.refs_9_), channel_id=1, source_target_pairs={{0,56},{8,0},{16,8},{24,16},{32,24},{40,32},{48,40},{56,48},{64,12... | collective-permute-start | bytes 393224 | tf_op jit(solution)/shard_map/ppermute | solution.py:32
  46.2 9.8 %collective-permute-start.6 = (bf16[4,64,256]{2,1,0:T(8,128)(2,1)S(1)}, bf16[4,64,256]{2,1,0:T(8,128)(2,1)S(1)}, u32[]{:S(2)}, u32[]{:S(2)}) collective-permute-start(bf16[4,64,256]{2,1,0:T(8,128)(2,1)S(1)} %collective-permute-done.5.refs_3_.refs_10_), channel_id=1, source_target_pairs={{0,8},{8,16},{16,24},{24,32},{32,40},{40,48},{48,56},{56,0},{64,72... | collective-permute-start | bytes 393224 | tf_op jit(solution)/shard_map/ppermute | solution.py:32
  48.3 20.8 %collective-permute-start.12 = (bf16[4,256,256]{2,1,0:T(8,128)(2,1)}, bf16[4,256,256]{2,1,0:T(8,128)(2,1)S(1)}, u32[]{:S(2)}, u32[]{:S(2)}) collective-permute-start(bf16[4,256,256]{2,1,0:T(8,128)(2,1)} %slice.132), channel_id=1, source_target_pairs={{0,64},{8,72},{16,80},{24,88},{32,96},{40,104},{48,112},{56,120},{... | collective-permute-start | bytes 1572872 | tf_op jit(solution)/shard_map/ppermute | solution.py:28
  51.6 16.1 %collective-permute-start.13 = (bf16[3,256,256]{2,1,0:T(8,128)(2,1)S(1)}, bf16[3,256,256]{2,1,0:T(8,128)(2,1)S(1)}, u32[]{:S(2)}, u32[]{:S(2)}) collective-permute-start(bf16[3,256,256]{2,1,0:T(8,128)(2,1)S(1)} %slice.133), channel_id=1, source_target_pairs={{0,192},{8,200},{16,208},{24,216},{32,224},{40,232},{48,240},{56,2... | collective-permute-start | bytes 1179656 | tf_op jit(solution)/shard_map/ppermute | solution.py:28
  56.0 6.2 %collective-permute-start.7 = (bf16[4,64,256]{2,1,0:T(8,128)(2,1)S(1)}, bf16[4,64,256]{2,1,0:T(8,128)(2,1)S(1)}, u32[]{:S(2)}, u32[]{:S(2)}) collective-permute-start(bf16[4,64,256]{2,1,0:T(8,128)(2,1)S(1)} %collective-permute-done.6.refs_4_.refs_11_), channel_id=1, source_target_pairs={{0,8},{8,16},{16,24},{24,32},{32,40},{40,48},{48,56},{56,0},{64,72... | collective-permute-start | bytes 393224 | tf_op jit(solution)/shard_map/ppermute | solution.py:32
  58.5 6.2 %collective-permute-start.11 = (bf16[4,64,256]{2,1,0:T(8,128)(2,1)S(1)}, bf16[4,64,256]{2,1,0:T(8,128)(2,1)S(1)}, u32[]{:S(2)}, u32[]{:S(2)}) collective-permute-start(bf16[4,64,256]{2,1,0:T(8,128)(2,1)S(1)} %collective-permute-done.10.refs_7_.refs_15_), channel_id=1, source_target_pairs={{0,56},{8,0},{16,8},{24,16},{32,24},{40,32},{48,40},{56,48},{64,12... | collective-permute-start | bytes 393224 | tf_op jit(solution)/shard_map/ppermute | solution.py:32
  62.2 10.9 %collective-permute-start.8 = (bf16[4,64,256]{2,1,0:T(8,128)(2,1)S(1)}, bf16[4,64,256]{2,1,0:T(8,128)(2,1)S(1)}, u32[]{:S(2)}, u32[]{:S(2)}) collective-permute-start(bf16[4,64,256]{2,1,0:T(8,128)(2,1)S(1)} %collective-permute-done.7.refs_5_.refs_12_), channel_id=1, source_target_pairs={{0,8},{8,16},{16,24},{24,32},{32,40},{40,48},{48,56},{56,0},{64,72... | collective-permute-start | bytes 393224 | tf_op jit(solution)/shard_map/ppermute | solution.py:32
  76.6 6.3 %collective-permute-start.15 = (bf16[4,64,256]{2,1,0:T(8,128)(2,1)S(1)}, bf16[4,64,256]{2,1,0:T(8,128)(2,1)S(1)}, u32[]{:S(2)}, u32[]{:S(2)}) collective-permute-start(bf16[4,64,256]{2,1,0:T(8,128)(2,1)S(1)} %get-tuple-element.74), channel_id=1, source_target_pairs={{0,2},{1,3},{2,4},{3,5},{4,6},{5,7},{6,0},{7,1},{8,10},{9,11},{10,... | collective-permute-start | bytes 393224 | tf_op jit(solution)/shard_map/ppermute | solution.py:36
  79.5 7.9 %collective-permute-start.16 = (bf16[4,64,256]{2,1,0:T(8,128)(2,1)S(1)}, bf16[4,64,256]{2,1,0:T(8,128)(2,1)S(1)}, u32[]{:S(2)}, u32[]{:S(2)}) collective-permute-start(bf16[4,64,256]{2,1,0:T(8,128)(2,1)S(1)} %get-tuple-element.75), channel_id=1, source_target_pairs={{0,4},{1,5},{2,6},{3,7},{4,0},{5,1},{6,2},{7,3},{8,12},{9,13},{10,... | collective-permute-start | bytes 393224 | tf_op jit(solution)/shard_map/ppermute | solution.py:36
  80.4 8.1 %collective-permute-start.17 = (bf16[4,64,256]{2,1,0:T(8,128)(2,1)S(1)}, bf16[4,64,256]{2,1,0:T(8,128)(2,1)S(1)}, u32[]{:S(2)}, u32[]{:S(2)}) collective-permute-start(bf16[4,64,256]{2,1,0:T(8,128)(2,1)S(1)} %get-tuple-element.76), channel_id=1, source_target_pairs={{0,6},{1,7},{2,0},{3,1},{4,2},{5,3},{6,4},{7,5},{8,14},{9,15},{10,... | collective-permute-start | bytes 393224 | tf_op jit(solution)/shard_map/ppermute | solution.py:36
  90.8 6.3 %collective-permute-start.18 = (bf16[4,64,256]{2,1,0:T(8,128)(2,1)S(1)}, bf16[4,64,256]{2,1,0:T(8,128)(2,1)S(1)}, u32[]{:S(2)}, u32[]{:S(2)}) collective-permute-start(bf16[4,64,256]{2,1,0:T(8,128)(2,1)S(1)} %get-tuple-element.77.refs_2_.refs_17_), channel_id=1, source_target_pairs={{0,8},{8,16},{16,24},{24,32},{32,40},{40,48},{48,56},{56,0},{64,72... | collective-permute-start | bytes 393224 | tf_op jit(solution)/shard_map/ppermute | solution.py:32
  97.1 119.3 %all-gather.10.cloned.1.call-start = ((), (), s32[]{:S(2)}) async-start(), calls=%async_computation.2 | async-start | bytes 4587520 | tf_op jit(solution)/shard_map/all_gather | solution.py:66
  97.9 6.2 %collective-permute-start.19 = (bf16[4,64,256]{2,1,0:T(8,128)(2,1)S(1)}, bf16[4,64,256]{2,1,0:T(8,128)(2,1)S(1)}, u32[]{:S(2)}, u32[]{:S(2)}) collective-permute-start(bf16[4,64,256]{2,1,0:T(8,128)(2,1)S(1)} %collective-permute-done.18.refs_3_.refs_18_), channel_id=1, source_target_pairs={{0,8},{8,16},{16,24},{24,32},{32,40},{40,48},{48,56},{56,0},{64,72... | collective-permute-start | bytes 393224 | tf_op jit(solution)/shard_map/ppermute | solution.py:32
  102.3 6.1 %collective-permute-start.23 = (bf16[4,64,256]{2,1,0:T(8,128)(2,1)S(1)}, bf16[4,64,256]{2,1,0:T(8,128)(2,1)S(1)}, u32[]{:S(2)}, u32[]{:S(2)}) collective-permute-start(bf16[4,64,256]{2,1,0:T(8,128)(2,1)S(1)} %collective-permute-done.22.refs_8_.refs_24_), channel_id=1, source_target_pairs={{0,56},{8,0},{16,8},{24,16},{32,24},{40,32},{48,40},{56,48},{64,12... | collective-permute-start | bytes 393224 | tf_op jit(solution)/shard_map/ppermute | solution.py:32
  104.1 7.0 %collective-permute-start.20 = (bf16[4,64,256]{2,1,0:T(8,128)(2,1)S(1)}, bf16[4,64,256]{2,1,0:T(8,128)(2,1)S(1)}, u32[]{:S(2)}, u32[]{:S(2)}) collective-permute-start(bf16[4,64,256]{2,1,0:T(8,128)(2,1)S(1)} %collective-permute-done.19.refs_4_.refs_19_), channel_id=1, source_target_pairs={{0,8},{8,16},{16,24},{24,32},{32,40},{40,48},{48,56},{56,0},{64,72... | collective-permute-start | bytes 393224 | tf_op jit(solution)/shard_map/ppermute | solution.py:32
  111.1 6.9 %collective-permute-start.21 = (bf16[4,64,256]{2,1,0:T(8,128)(2,1)S(1)}, bf16[4,64,256]{2,1,0:T(8,128)(2,1)S(1)}, u32[]{:S(2)}, u32[]{:S(2)}) collective-permute-start(bf16[4,64,256]{2,1,0:T(8,128)(2,1)S(1)} %collective-permute-done.20.refs_5_.refs_20_), channel_id=1, source_target_pairs={{0,8},{8,16},{16,24},{24,32},{32,40},{40,48},{48,56},{56,0},{64,72... | collective-permute-start | bytes 393224 | tf_op jit(solution)/shard_map/ppermute | solution.py:32
  122.6 15.4 %collective-permute-start.26 = (bf16[4,64,256]{2,1,0:T(8,128)(2,1)S(1)}, bf16[4,64,256]{2,1,0:T(8,128)(2,1)S(1)}, u32[]{:S(2)}, u32[]{:S(2)}) collective-permute-start(bf16[4,64,256]{2,1,0:T(8,128)(2,1)S(1)} %get-tuple-element.82), channel_id=1, source_target_pairs={{0,2},{1,3},{2,4},{3,5},{4,6},{5,7},{6,0},{7,1},{8,10},{9,11},{10,... | collective-permute-start | bytes 393224 | tf_op jit(solution)/shard_map/ppermute | solution.py:36
  133.3 7.9 %collective-permute-start.27 = (bf16[4,64,256]{2,1,0:T(8,128)(2,1)S(1)}, bf16[4,64,256]{2,1,0:T(8,128)(2,1)S(1)}, u32[]{:S(2)}, u32[]{:S(2)}) collective-permute-start(bf16[4,64,256]{2,1,0:T(8,128)(2,1)S(1)} %get-tuple-element.83), channel_id=1, source_target_pairs={{0,4},{1,5},{2,6},{3,7},{4,0},{5,1},{6,2},{7,3},{8,12},{9,13},{10,... | collective-permute-start | bytes 393224 | tf_op jit(solution)/shard_map/ppermute | solution.py:36
  134.4 7.8 %collective-permute-start.28 = (bf16[4,64,256]{2,1,0:T(8,128)(2,1)S(1)}, bf16[4,64,256]{2,1,0:T(8,128)(2,1)S(1)}, u32[]{:S(2)}, u32[]{:S(2)}) collective-permute-start(bf16[4,64,256]{2,1,0:T(8,128)(2,1)S(1)} %get-tuple-element.84), channel_id=1, source_target_pairs={{0,6},{1,7},{2,0},{3,1},{4,2},{5,3},{6,4},{7,5},{8,14},{9,15},{10,... | collective-permute-start | bytes 393224 | tf_op jit(solution)/shard_map/ppermute | solution.py:36
  144.5 6.3 %collective-permute-start.29 = (bf16[4,64,256]{2,1,0:T(8,128)(2,1)S(1)}, bf16[4,64,256]{2,1,0:T(8,128)(2,1)S(1)}, u32[]{:S(2)}, u32[]{:S(2)}) collective-permute-start(bf16[4,64,256]{2,1,0:T(8,128)(2,1)S(1)} %get-tuple-element.85.refs_2_), channel_id=1, source_target_pairs={{0,8},{8,16},{16,24},{24,32},{32,40},{40,48},{48,56},{56,0},{64,72... | collective-permute-start | bytes 393224 | tf_op jit(solution)/shard_map/ppermute | solution.py:32
  150.9 110.5 %all-gather.12.cloned.1.call-start = ((), (), s32[]{:S(2)}) async-start(), calls=%async_computation.3 | async-start | bytes 4587520 | tf_op jit(solution)/shard_map/all_gather | solution.py:66
  152.7 6.2 %collective-permute-start.30 = (bf16[4,64,256]{2,1,0:T(8,128)(2,1)S(1)}, bf16[4,64,256]{2,1,0:T(8,128)(2,1)S(1)}, u32[]{:S(2)}, u32[]{:S(2)}) collective-permute-start(bf16[4,64,256]{2,1,0:T(8,128)(2,1)S(1)} %collective-permute-done.29.refs_3_), channel_id=1, source_target_pairs={{0,8},{8,16},{16,24},{24,32},{32,40},{40,48},{48,56},{56,0},{64,72... | collective-permute-start | bytes 393224 | tf_op jit(solution)/shard_map/ppermute | solution.py:32
  158.9 6.2 %collective-permute-start.31 = (bf16[4,64,256]{2,1,0:T(8,128)(2,1)S(1)}, bf16[4,64,256]{2,1,0:T(8,128)(2,1)S(1)}, u32[]{:S(2)}, u32[]{:S(2)}) collective-permute-start(bf16[4,64,256]{2,1,0:T(8,128)(2,1)S(1)} %collective-permute-done.30.refs_4_), channel_id=1, source_target_pairs={{0,8},{8,16},{16,24},{24,32},{32,40},{40,48},{48,56},{56,0},{64,72... | collective-permute-start | bytes 393224 | tf_op jit(solution)/shard_map/ppermute | solution.py:32
  161.6 6.0 %collective-permute-start.35 = (bf16[4,64,256]{2,1,0:T(8,128)(2,1)S(1)}, bf16[4,64,256]{2,1,0:T(8,128)(2,1)S(1)}, u32[]{:S(2)}, u32[]{:S(2)}) collective-permute-start(bf16[4,64,256]{2,1,0:T(8,128)(2,1)S(1)} %collective-permute-done.34.refs_7_), channel_id=1, source_target_pairs={{0,56},{8,0},{16,8},{24,16},{32,24},{40,32},{48,40},{56,48},{64,12... | collective-permute-start | bytes 393224 | tf_op jit(solution)/shard_map/ppermute | solution.py:32
  165.1 9.1 %collective-permute-start.32 = (bf16[4,64,256]{2,1,0:T(8,128)(2,1)S(1)}, bf16[4,64,256]{2,1,0:T(8,128)(2,1)S(1)}, u32[]{:S(2)}, u32[]{:S(2)}) collective-permute-start(bf16[4,64,256]{2,1,0:T(8,128)(2,1)S(1)} %collective-permute-done.31.refs_5_), channel_id=1, source_target_pairs={{0,8},{8,16},{16,24},{24,32},{32,40},{40,48},{48,56},{56,0},{64,72... | collective-permute-start | bytes 393224 | tf_op jit(solution)/shard_map/ppermute | solution.py:32
  178.8 6.4 %collective-permute-start.37 = (bf16[4,64,256]{2,1,0:T(8,128)(2,1)S(1)}, bf16[4,64,256]{2,1,0:T(8,128)(2,1)S(1)}, u32[]{:S(2)}, u32[]{:S(2)}) collective-permute-start(bf16[4,64,256]{2,1,0:T(8,128)(2,1)S(1)} %get-tuple-element.90), channel_id=1, source_target_pairs={{0,2},{1,3},{2,4},{3,5},{4,6},{5,7},{6,0},{7,1},{8,10},{9,11},{10,... | collective-permute-start | bytes 393224 | tf_op jit(solution)/shard_map/ppermute | solution.py:36
  178.9 7.9 %collective-permute-start.38 = (bf16[4,64,256]{2,1,0:T(8,128)(2,1)S(1)}, bf16[4,64,256]{2,1,0:T(8,128)(2,1)S(1)}, u32[]{:S(2)}, u32[]{:S(2)}) collective-permute-start(bf16[4,64,256]{2,1,0:T(8,128)(2,1)S(1)} %get-tuple-element.91), channel_id=1, source_target_pairs={{0,4},{1,5},{2,6},{3,7},{4,0},{5,1},{6,2},{7,3},{8,12},{9,13},{10,... | collective-permute-start | bytes 393224 | tf_op jit(solution)/shard_map/ppermute | solution.py:36
  181.1 7.7 %collective-permute-start.39 = (bf16[4,64,256]{2,1,0:T(8,128)(2,1)S(1)}, bf16[4,64,256]{2,1,0:T(8,128)(2,1)S(1)}, u32[]{:S(2)}, u32[]{:S(2)}) collective-permute-start(bf16[4,64,256]{2,1,0:T(8,128)(2,1)S(1)} %get-tuple-element.92), channel_id=1, source_target_pairs={{0,6},{1,7},{2,0},{3,1},{4,2},{5,3},{6,4},{7,5},{8,14},{9,15},{10,... | collective-permute-start | bytes 393224 | tf_op jit(solution)/shard_map/ppermute | solution.py:36
  192.1 7.6 %collective-permute-start.40 = (bf16[4,64,256]{2,1,0:T(8,128)(2,1)S(1)}, bf16[4,64,256]{2,1,0:T(8,128)(2,1)S(1)}, u32[]{:S(2)}, u32[]{:S(2)}) collective-permute-start(bf16[4,64,256]{2,1,0:T(8,128)(2,1)S(1)} %get-tuple-element.93.refs_2_.refs_9_), channel_id=1, source_target_pairs={{0,8},{8,16},{16,24},{24,32},{32,40},{40,48},{48,56},{56,0},{64,72... | collective-permute-start | bytes 393224 | tf_op jit(solution)/shard_map/ppermute | solution.py:32
  199.6 103.7 %all-gather.14.cloned.1.call-start = ((), (), s32[]{:S(2)}) async-start(), calls=%async_computation.4 | async-start | bytes 3932160 | tf_op jit(solution)/shard_map/all_gather | solution.py:66
  201.5 6.2 %collective-permute-start.41 = (bf16[4,64,256]{2,1,0:T(8,128)(2,1)S(1)}, bf16[4,64,256]{2,1,0:T(8,128)(2,1)S(1)}, u32[]{:S(2)}, u32[]{:S(2)}) collective-permute-start(bf16[4,64,256]{2,1,0:T(8,128)(2,1)S(1)} %collective-permute-done.40.refs_3_.refs_10_), channel_id=1, source_target_pairs={{0,8},{8,16},{16,24},{24,32},{32,40},{40,48},{48,56},{56,0},{64,72... | collective-permute-start | bytes 393224 | tf_op jit(solution)/shard_map/ppermute | solution.py:32
  204.7 5.9 %collective-permute-start.45 = (bf16[4,64,256]{2,1,0:T(8,128)(2,1)S(1)}, bf16[4,64,256]{2,1,0:T(8,128)(2,1)S(1)}, u32[]{:S(2)}, u32[]{:S(2)}) collective-permute-start(bf16[4,64,256]{2,1,0:T(8,128)(2,1)S(1)} %collective-permute-done.44.refs_8_.refs_16_), channel_id=1, source_target_pairs={{0,56},{8,0},{16,8},{24,16},{32,24},{40,32},{48,40},{56,48},{64,12... | collective-permute-start | bytes 393224 | tf_op jit(solution)/shard_map/ppermute | solution.py:32
  207.7 6.2 %collective-permute-start.42 = (bf16[4,64,256]{2,1,0:T(8,128)(2,1)S(1)}, bf16[4,64,256]{2,1,0:T(8,128)(2,1)S(1)}, u32[]{:S(2)}, u32[]{:S(2)}) collective-permute-start(bf16[4,64,256]{2,1,0:T(8,128)(2,1)S(1)} %collective-permute-done.41.refs_4_.refs_11_), channel_id=1, source_target_pairs={{0,8},{8,16},{16,24},{24,32},{32,40},{40,48},{48,56},{56,0},{64,72... | collective-permute-start | bytes 393224 | tf_op jit(solution)/shard_map/ppermute | solution.py:32
  213.9 6.2 %collective-permute-start.43 = (bf16[4,64,256]{2,1,0:T(8,128)(2,1)S(1)}, bf16[4,64,256]{2,1,0:T(8,128)(2,1)S(1)}, u32[]{:S(2)}, u32[]{:S(2)}) collective-permute-start(bf16[4,64,256]{2,1,0:T(8,128)(2,1)S(1)} %collective-permute-done.42.refs_5_.refs_12_), channel_id=1, source_target_pairs={{0,8},{8,16},{16,24},{24,32},{32,40},{40,48},{48,56},{56,0},{64,72... | collective-permute-start | bytes 393224 | tf_op jit(solution)/shard_map/ppermute | solution.py:32
  224.7 6.4 %collective-permute-start.48 = (bf16[4,64,256]{2,1,0:T(8,128)(2,1)S(1)}, bf16[4,64,256]{2,1,0:T(8,128)(2,1)S(1)}, u32[]{:S(2)}, u32[]{:S(2)}) collective-permute-start(bf16[4,64,256]{2,1,0:T(8,128)(2,1)S(1)} %get-tuple-element.98), channel_id=1, source_target_pairs={{0,2},{1,3},{2,4},{3,5},{4,6},{5,7},{6,0},{7,1},{8,10},{9,11},{10,... | collective-permute-start | bytes 393224 | tf_op jit(solution)/shard_map/ppermute | solution.py:36
  225.3 7.9 %collective-permute-start.49 = (bf16[4,64,256]{2,1,0:T(8,128)(2,1)S(1)}, bf16[4,64,256]{2,1,0:T(8,128)(2,1)S(1)}, u32[]{:S(2)}, u32[]{:S(2)}) collective-permute-start(bf16[4,64,256]{2,1,0:T(8,128)(2,1)S(1)} %get-tuple-element.99), channel_id=1, source_target_pairs={{0,4},{1,5},{2,6},{3,7},{4,0},{5,1},{6,2},{7,3},{8,12},{9,13},{10,... | collective-permute-start | bytes 393224 | tf_op jit(solution)/shard_map/ppermute | solution.py:36
  227.0 7.8 %collective-permute-start.50 = (bf16[4,64,256]{2,1,0:T(8,128)(2,1)S(1)}, bf16[4,64,256]{2,1,0:T(8,128)(2,1)S(1)}, u32[]{:S(2)}, u32[]{:S(2)}) collective-permute-start(bf16[4,64,256]{2,1,0:T(8,128)(2,1)S(1)} %get-tuple-element.100), channel_id=1, source_target_pairs={{0,6},{1,7},{2,0},{3,1},{4,2},{5,3},{6,4},{7,5},{8,14},{9,15},{10,... | collective-permute-start | bytes 393224 | tf_op jit(solution)/shard_map/ppermute | solution.py:36
  237.1 7.3 %collective-permute-start.51 = (bf16[4,64,256]{2,1,0:T(8,128)(2,1)S(1)}, bf16[4,64,256]{2,1,0:T(8,128)(2,1)S(1)}, u32[]{:S(2)}, u32[]{:S(2)}) collective-permute-start(bf16[4,64,256]{2,1,0:T(8,128)(2,1)S(1)} %get-tuple-element.102.refs_2_.refs_17_), channel_id=1, source_target_pairs={{0,8},{8,16},{16,24},{24,32},{32,40},{40,48},{48,56},{56,0},{64,72... | collective-permute-start | bytes 393224 | tf_op jit(solution)/shard_map/ppermute | solution.py:32
  246.3 6.4 %collective-permute-start.52 = (bf16[4,64,256]{2,1,0:T(8,128)(2,1)S(1)}, bf16[4,64,256]{2,1,0:T(8,128)(2,1)S(1)}, u32[]{:S(2)}, u32[]{:S(2)}) collective-permute-start(bf16[4,64,256]{2,1,0:T(8,128)(2,1)S(1)} %collective-permute-done.51.refs_3_.refs_18_), channel_id=1, source_target_pairs={{0,8},{8,16},{16,24},{24,32},{32,40},{40,48},{48,56},{56,0},{64,72... | collective-permute-start | bytes 393224 | tf_op jit(solution)/shard_map/ppermute | solution.py:32
  249.7 6.1 %collective-permute-start.56 = (bf16[4,64,256]{2,1,0:T(8,128)(2,1)S(1)}, bf16[4,64,256]{2,1,0:T(8,128)(2,1)S(1)}, u32[]{:S(2)}, u32[]{:S(2)}) collective-permute-start(bf16[4,64,256]{2,1,0:T(8,128)(2,1)S(1)} %collective-permute-done.55.refs_8_.refs_24_), channel_id=1, source_target_pairs={{0,56},{8,0},{16,8},{24,16},{32,24},{40,32},{48,40},{56,48},{64,12... | collective-permute-start | bytes 393224 | tf_op jit(solution)/shard_map/ppermute | solution.py:32
  252.7 6.2 %collective-permute-start.53 = (bf16[4,64,256]{2,1,0:T(8,128)(2,1)S(1)}, bf16[4,64,256]{2,1,0:T(8,128)(2,1)S(1)}, u32[]{:S(2)}, u32[]{:S(2)}) collective-permute-start(bf16[4,64,256]{2,1,0:T(8,128)(2,1)S(1)} %collective-permute-done.52.refs_4_.refs_19_), channel_id=1, source_target_pairs={{0,8},{8,16},{16,24},{24,32},{32,40},{40,48},{48,56},{56,0},{64,72... | collective-permute-start | bytes 393224 | tf_op jit(solution)/shard_map/ppermute | solution.py:32
  258.9 7.3 %collective-permute-start.54 = (bf16[4,64,256]{2,1,0:T(8,128)(2,1)S(1)}, bf16[4,64,256]{2,1,0:T(8,128)(2,1)S(1)}, u32[]{:S(2)}, u32[]{:S(2)}) collective-permute-start(bf16[4,64,256]{2,1,0:T(8,128)(2,1)S(1)} %collective-permute-done.53.refs_5_.refs_20_), channel_id=1, source_target_pairs={{0,8},{8,16},{16,24},{24,32},{32,40},{40,48},{48,56},{56,0},{64,72... | collective-permute-start | bytes 393224 | tf_op jit(solution)/shard_map/ppermute | solution.py:32
  270.7 6.4 %collective-permute-start.59 = (bf16[4,64,256]{2,1,0:T(8,128)(2,1)S(1)}, bf16[4,64,256]{2,1,0:T(8,128)(2,1)S(1)}, u32[]{:S(2)}, u32[]{:S(2)}) collective-permute-start(bf16[4,64,256]{2,1,0:T(8,128)(2,1)S(1)} %get-tuple-element.107), channel_id=1, source_target_pairs={{0,2},{1,3},{2,4},{3,5},{4,6},{5,7},{6,0},{7,1},{8,10},{9,11},{10,... | collective-permute-start | bytes 393224 | tf_op jit(solution)/shard_map/ppermute | solution.py:36
  271.1 7.9 %collective-permute-start.60 = (bf16[4,64,256]{2,1,0:T(8,128)(2,1)S(1)}, bf16[4,64,256]{2,1,0:T(8,128)(2,1)S(1)}, u32[]{:S(2)}, u32[]{:S(2)}) collective-permute-start(bf16[4,64,256]{2,1,0:T(8,128)(2,1)S(1)} %get-tuple-element.108), channel_id=1, source_target_pairs={{0,4},{1,5},{2,6},{3,7},{4,0},{5,1},{6,2},{7,3},{8,12},{9,13},{10,... | collective-permute-start | bytes 393224 | tf_op jit(solution)/shard_map/ppermute | solution.py:36
  273.2 7.5 %collective-permute-start.61 = (bf16[4,64,256]{2,1,0:T(8,128)(2,1)S(1)}, bf16[4,64,256]{2,1,0:T(8,128)(2,1)S(1)}, u32[]{:S(2)}, u32[]{:S(2)}) collective-permute-start(bf16[4,64,256]{2,1,0:T(8,128)(2,1)S(1)} %get-tuple-element.109), channel_id=1, source_target_pairs={{0,6},{1,7},{2,0},{3,1},{4,2},{5,3},{6,4},{7,5},{8,14},{9,15},{10,... | collective-permute-start | bytes 393224 | tf_op jit(solution)/shard_map/ppermute | solution.py:36
  283.0 6.8 %collective-permute-start.62 = (bf16[4,64,256]{2,1,0:T(8,128)(2,1)S(1)}, bf16[4,64,256]{2,1,0:T(8,128)(2,1)S(1)}, u32[]{:S(2)}, u32[]{:S(2)}) collective-permute-start(bf16[4,64,256]{2,1,0:T(8,128)(2,1)S(1)} %get-tuple-element.111.refs_2_), channel_id=1, source_target_pairs={{0,8},{8,16},{16,24},{24,32},{32,40},{40,48},{48,56},{56,0},{64,72... | collective-permute-start | bytes 393224 | tf_op jit(solution)/shard_map/ppermute | solution.py:32
  289.8 6.2 %collective-permute-start.63 = (bf16[4,64,256]{2,1,0:T(8,128)(2,1)S(1)}, bf16[4,64,256]{2,1,0:T(8,128)(2,1)S(1)}, u32[]{:S(2)}, u32[]{:S(2)}) collective-permute-start(bf16[4,64,256]{2,1,0:T(8,128)(2,1)S(1)} %collective-permute-done.62.refs_3_), channel_id=1, source_target_pairs={{0,8},{8,16},{16,24},{24,32},{32,40},{40,48},{48,56},{56,0},{64,72... | collective-permute-start | bytes 393224 | tf_op jit(solution)/shard_map/ppermute | solution.py:32
  291.6 6.8 %collective-permute-start.67 = (bf16[4,64,256]{2,1,0:T(8,128)(2,1)S(1)}, bf16[4,64,256]{2,1,0:T(8,128)(2,1)S(1)}, u32[]{:S(2)}, u32[]{:S(2)}) collective-permute-start(bf16[4,64,256]{2,1,0:T(8,128)(2,1)S(1)} %collective-permute-done.66.refs_8_), channel_id=1, source_target_pairs={{0,56},{8,0},{16,8},{24,16},{32,24},{40,32},{48,40},{56,48},{64,12... | collective-permute-start | bytes 393224 | tf_op jit(solution)/shard_map/ppermute | solution.py:32
  296.0 6.2 %collective-permute-start.64 = (bf16[4,64,256]{2,1,0:T(8,128)(2,1)S(1)}, bf16[4,64,256]{2,1,0:T(8,128)(2,1)S(1)}, u32[]{:S(2)}, u32[]{:S(2)}) collective-permute-start(bf16[4,64,256]{2,1,0:T(8,128)(2,1)S(1)} %collective-permute-done.63.refs_4_), channel_id=1, source_target_pairs={{0,8},{8,16},{16,24},{24,32},{32,40},{40,48},{48,56},{56,0},{64,72... | collective-permute-start | bytes 393224 | tf_op jit(solution)/shard_map/ppermute | solution.py:32
  302.2 7.8 %collective-permute-start.65 = (bf16[4,64,256]{2,1,0:T(8,128)(2,1)S(1)}, bf16[4,64,256]{2,1,0:T(8,128)(2,1)S(1)}, u32[]{:S(2)}, u32[]{:S(2)}) collective-permute-start(bf16[4,64,256]{2,1,0:T(8,128)(2,1)S(1)} %collective-permute-done.64.refs_5_), channel_id=1, source_target_pairs={{0,8},{8,16},{16,24},{24,32},{32,40},{40,48},{48,56},{56,0},{64,72... | collective-permute-start | bytes 393224 | tf_op jit(solution)/shard_map/ppermute | solution.py:32
  314.6 6.4 %collective-permute-start.70 = (bf16[4,64,256]{2,1,0:T(8,128)(2,1)S(1)}, bf16[4,64,256]{2,1,0:T(8,128)(2,1)S(1)}, u32[]{:S(2)}, u32[]{:S(2)}) collective-permute-start(bf16[4,64,256]{2,1,0:T(8,128)(2,1)S(1)} %get-tuple-element.116), channel_id=1, source_target_pairs={{0,2},{1,3},{2,4},{3,5},{4,6},{5,7},{6,0},{7,1},{8,10},{9,11},{10,... | collective-permute-start | bytes 393224 | tf_op jit(solution)/shard_map/ppermute | solution.py:36
  315.6 7.9 %collective-permute-start.71 = (bf16[4,64,256]{2,1,0:T(8,128)(2,1)S(1)}, bf16[4,64,256]{2,1,0:T(8,128)(2,1)S(1)}, u32[]{:S(2)}, u32[]{:S(2)}) collective-permute-start(bf16[4,64,256]{2,1,0:T(8,128)(2,1)S(1)} %get-tuple-element.117), channel_id=1, source_target_pairs={{0,4},{1,5},{2,6},{3,7},{4,0},{5,1},{6,2},{7,3},{8,12},{9,13},{10,... | collective-permute-start | bytes 393224 | tf_op jit(solution)/shard_map/ppermute | solution.py:36
  317.0 7.8 %collective-permute-start.72 = (bf16[4,64,256]{2,1,0:T(8,128)(2,1)S(1)}, bf16[4,64,256]{2,1,0:T(8,128)(2,1)S(1)}, u32[]{:S(2)}, u32[]{:S(2)}) collective-permute-start(bf16[4,64,256]{2,1,0:T(8,128)(2,1)S(1)} %get-tuple-element.118), channel_id=1, source_target_pairs={{0,6},{1,7},{2,0},{3,1},{4,2},{5,3},{6,4},{7,5},{8,14},{9,15},{10,... | collective-permute-start | bytes 393224 | tf_op jit(solution)/shard_map/ppermute | solution.py:36
  324.9 7.2 %collective-permute-start.73 = (bf16[4,64,256]{2,1,0:T(8,128)(2,1)S(1)}, bf16[4,64,256]{2,1,0:T(8,128)(2,1)S(1)}, u32[]{:S(2)}, u32[]{:S(2)}) collective-permute-start(bf16[4,64,256]{2,1,0:T(8,128)(2,1)S(1)} %get-tuple-element.123), channel_id=1, source_target_pairs={{0,192},{8,200},{16,208},{24,216},{32,224},{40,232},{48,240},{56,2... | collective-permute-start | bytes 393224 | tf_op jit(solution)/shard_map/ppermute | solution.py:28
  327.0 7.9 %collective-permute-start.74 = (bf16[4,64,256]{2,1,0:T(8,128)(2,1)S(1)}, bf16[4,64,256]{2,1,0:T(8,128)(2,1)S(1)}, u32[]{:S(2)}, u32[]{:S(2)}) collective-permute-start(bf16[4,64,256]{2,1,0:T(8,128)(2,1)S(1)} %get-tuple-element.124), channel_id=1, source_target_pairs={{0,128},{8,136},{16,144},{24,152},{32,160},{40,168},{48,176},{56,1... | collective-permute-start | bytes 393224 | tf_op jit(solution)/shard_map/ppermute | solution.py:28
  329.8 6.8 %collective-permute-start.75 = (bf16[4,64,256]{2,1,0:T(8,128)(2,1)S(1)}, bf16[4,64,256]{2,1,0:T(8,128)(2,1)S(1)}, u32[]{:S(2)}, u32[]{:S(2)}) collective-permute-start(bf16[4,64,256]{2,1,0:T(8,128)(2,1)S(1)} %get-tuple-element.125), channel_id=1, source_target_pairs={{0,64},{8,72},{16,80},{24,88},{32,96},{40,104},{48,112},{56,120},{... | collective-permute-start | bytes 393224 | tf_op jit(solution)/shard_map/ppermute | solution.py:28
  (75 other events, 577.3 us)
Sparse Core Ops, SparseCore 0:
  37.4 53.7 all-gather.5
  97.2 51.1 all-gather.7
  151.0 47.5 all-gather.9
  200.2 46.9 all-gather.11
  248.9 42.3 all-gather.13
